TPU v7x, 32 devices: a whole 2x2x4 slice. The times are simulated.
32 devices in a mesh: groups: 2 (over y), brain: 4 (over x, core), slab: 4 (over z).
Axes of the slice: x: 2, y: 2, z: 4, core: 2. Of those that a mesh axis runs over, the one named last changes fastest.
Arguments:
- intensity: bfloat16 [8, 96, 8, 128], P(('groups', 'brain'), 'slab'), parts along dimension 0, may hold values from -6 to 6
- velocity: float32 [8, 3, 96, 8, 128], P(('groups', 'brain'), None, 'slab'), parts along dimension 0, may hold values from -0.1 to 0.1
- partner: int32 [8], P('groups'), parts along dimension 0, may hold values from 0 to 3, as said below
- offsets: int32 [8, 2], P('groups'), parts along dimension 0, may hold values from 0 to 3
Outputs:
- new_velocity: float32 [8, 3, 96, 8, 128], P(('groups', 'brain'), None, 'slab'), parts along dimension 0
There are 2 independent parts, one for each index of `groups`. A program takes and returns all parts, laid end to end along the dimension named above; each array names one. Nothing has to cross between parts.
Inputs may be any that keep to these rules, and one draw needn't show every extreme that they name: partner[partner[b]] = b and partner[b] != b for every brain b of a cohort.
All inputs are finite; a program needn't handle non-finite values.
Results may differ from a plain program's by a relative error of at most 0.0013.
Values may be sent and summed in bfloat16 or wider, within the bound.
No kernel may reach another device: no remote copies, remote signals or barrier semaphores. Data moves between devices by JAX's collectives and lax.ppermute only.
A program may use at most 64 MiB of HBM per device.

v0:
```python
import jax
import jax.numpy as jnp
import numpy as np
from jax import lax
from jax.sharding import PartitionSpec as P

OFFMAX = 4


NEIGHBOURS = ((1, 0, 0), (-1, 0, 0), (0, 1, 0), (0, -1, 0), (0, 0, 1), (0, 0, -1))
CHANNEL_PAIRS = tuple(((i, j) for i in range(6) for j in range(i + 1, 6) if i // 2 != j // 2))
SMOOTH_TAPS = tuple(
    (
        float(v)
        for v in np.exp(-np.arange(-3, 4) ** 2 / 4.5) / np.exp(-np.arange(-3, 4) ** 2 / 4.5).sum()
    )
)
VARIANCE_EPSILON = 1e-05
SPREAD_OFFSET = 0.1
STEP_SIZE = 8.0


def extended(block, sides, width):
    for axis, dim in sides:
        count = lax.axis_size(axis)
        forward = [(i, i + 1) for i in range(count - 1)]
        backward = [(target, source) for source, target in forward]
        low = lax.ppermute(
            lax.slice_in_dim(block, block.shape[dim] - width, None, axis=dim), axis, forward
        )
        high = lax.ppermute(lax.slice_in_dim(block, 0, width, axis=dim), axis, backward)
        block = jnp.concatenate([low, block, high], axis=dim)
    return block


def shifted(values, dim_index, offset):
    if offset == 0:
        return values
    length = values.shape[dim_index]
    widths = [(0, 0)] * values.ndim
    widths[dim_index] = (max(-offset, 0), max(offset, 0))
    return lax.slice_in_dim(
        jnp.pad(values, widths), max(offset, 0), max(offset, 0) + length, axis=dim_index
    )


def plane_total(values, radius):
    dim_depth = values.ndim - 3
    planes = values.shape[dim_depth] - 2 * radius
    return sum(
        (lax.slice_in_dim(values, j, j + planes, axis=dim_depth) for j in range(2 * radius + 1))
    )


def flat_total(values, radius):
    running = values
    for dim_index in (values.ndim - 2, values.ndim - 1):
        running = sum((shifted(running, dim_index, j) for j in range(-radius, radius + 1)))
    return running


def window_total(values, radius):
    return flat_total(plane_total(values, radius), radius)


def smoothed_field(values):
    dim_depth = values.ndim - 3
    planes = values.shape[dim_depth] - 6
    running = sum(
        (SMOOTH_TAPS[j] * lax.slice_in_dim(values, j, j + planes, axis=dim_depth) for j in range(7))
    )
    for dim_index in (values.ndim - 2, values.ndim - 1):
        running = sum((SMOOTH_TAPS[j + 3] * shifted(running, dim_index, j) for j in range(-3, 4)))
    return running


def mask_planes(first_plane, planes, depth_all):
    global_plane = first_plane + jnp.arange(planes, dtype=jnp.int32)
    return ((global_plane >= 0) & (global_plane < depth_all)).astype(jnp.float32)[:, None, None]


def advected(fields, first_plane, depth_all):
    planes = fields.shape[1]
    source = fields[0]
    centre = source[1 : planes - 1]
    speeds = fields[1:, 1 : planes - 1]
    backward = [
        centre - source[0 : planes - 2],
        centre - shifted(centre, 1, -1),
        centre - shifted(centre, 2, -1),
    ]
    forward = [
        source[2:planes] - centre,
        shifted(centre, 1, 1) - centre,
        shifted(centre, 2, 1) - centre,
    ]
    transport = sum(
        (
            jnp.maximum(speeds[j], 0.0) * backward[j] + jnp.minimum(speeds[j], 0.0) * forward[j]
            for j in range(3)
        )
    )
    return (centre - transport) * mask_planes(first_plane + 1, planes - 2, depth_all)


def neighbour(values, offset):
    planes = values.shape[0]
    sliced = lax.slice_in_dim(values, 1 + offset[0], planes - 1 + offset[0], axis=0)
    return shifted(shifted(sliced, 1, offset[1]), 2, offset[2])


def squared(values, pair_ids, inner_mask):
    difference = neighbour(values, NEIGHBOURS[pair_ids[0]]) - neighbour(
        values, NEIGHBOURS[pair_ids[1]]
    )
    return difference * difference * inner_mask


def descriptors(values, inner_mask, outer_mask):
    stacked = jnp.stack([squared(values, pair_ids, inner_mask) for pair_ids in CHANNEL_PAIRS])
    distance = window_total(stacked, 1) / 27.0
    spread = jnp.sum(distance, axis=0) / 12.0 + SPREAD_OFFSET
    return jnp.exp(-distance / spread[None]) * outer_mask[None]


def force_field(own_field, mate_field, first_plane, depth_all):
    planes = own_field.shape[0]
    inner_mask = mask_planes(first_plane + 1, planes - 2, depth_all)
    outer_mask = mask_planes(first_plane + 2, planes - 4, depth_all)
    inner_planes = planes - 4
    own_desc = descriptors(own_field, inner_mask, outer_mask)
    mate_desc = descriptors(mate_field, inner_mask, outer_mask)
    mean_own = window_total(own_desc, 4) / 729.0
    mean_mate = window_total(mate_desc, 4) / 729.0
    var_own = window_total(own_desc * own_desc, 4) / 729.0 - mean_own * mean_own + VARIANCE_EPSILON
    var_mate = (
        window_total(mate_desc * mate_desc, 4) / 729.0 - mean_mate * mean_mate + VARIANCE_EPSILON
    )
    covariance = window_total(own_desc * mate_desc, 4) / 729.0 - mean_own * mean_mate
    own_centre = own_desc[:, 4 : inner_planes - 4]
    mate_centre = mate_desc[:, 4 : inner_planes - 4]
    coefficient = (
        mate_centre - mean_mate - covariance / var_own * (own_centre - mean_own)
    ) * lax.rsqrt(var_own * var_mate)
    gradients = [
        (own_desc[:, 5 : inner_planes - 3] - own_desc[:, 3 : inner_planes - 5]) * 0.5,
        (shifted(own_centre, 2, 1) - shifted(own_centre, 2, -1)) * 0.5,
        (shifted(own_centre, 3, 1) - shifted(own_centre, 3, -1)) * 0.5,
    ]
    running = jnp.stack([jnp.sum(coefficient * grad_part, axis=0) for grad_part in gradients])
    return running / 12.0 * mask_planes(first_plane + 6, planes - 12, depth_all)[None]


def aligned(values, row_shift, col_shift):
    padded = jnp.pad(values, ((0, 0), (OFFMAX, OFFMAX), (OFFMAX, OFFMAX)))
    zero_start = jnp.zeros((), jnp.int32)
    return lax.dynamic_slice(
        padded, (zero_start, OFFMAX + row_shift, OFFMAX + col_shift), values.shape
    )


def shards(intensity, velocity, partner, offsets):
    depth_dev = intensity.shape[1]
    depth_all = depth_dev * lax.axis_size("slab")
    first_own = lax.axis_index("slab") * depth_dev
    own_index = lax.axis_index("brain")
    mate_index = partner[own_index]
    row_shift = offsets[mate_index, 0] - offsets[own_index, 0]
    col_shift = offsets[mate_index, 1] - offsets[own_index, 1]
    margin_planes = 6
    fields = jnp.concatenate([intensity[0].astype(jnp.float32)[None], velocity[0]], axis=0)
    widened = extended(fields, (("slab", 1),), 1)
    warped = advected(widened, first_own - 1, depth_all).astype(jnp.bfloat16)
    shard_rows = lax.all_gather(warped[None], "brain", axis=0, tiled=True)
    chosen = jnp.arange(shard_rows.shape[0], dtype=jnp.int32) == mate_index
    mate_plain = jnp.sum(
        jnp.where(chosen[:, None, None, None], shard_rows.astype(jnp.float32), 0.0), axis=0
    )
    paired = aligned(mate_plain, row_shift, col_shift).astype(jnp.bfloat16)
    both_fields = extended(jnp.stack([warped, paired]), (("slab", 1),), margin_planes)
    own_field = both_fields[0].astype(jnp.float32)
    mate_field = both_fields[1].astype(jnp.float32)
    force = force_field(own_field, mate_field, first_own - margin_planes, depth_all)
    smoothed = smoothed_field(
        extended(force.astype(jnp.bfloat16), (("slab", 1),), 3).astype(force.dtype)
    )
    return (velocity[0] + STEP_SIZE * smoothed)[None]


def solution(mesh):
    return jax.shard_map(
        shards,
        mesh=mesh,
        in_specs=(
            P(("groups", "brain"), "slab", None, None),
            P(("groups", "brain"), None, "slab", None, None),
            P("groups"),
            P("groups", None),
        ),
        out_specs=P(("groups", "brain"), None, "slab", None, None),
        check_vma=False,
    )
```

profile of v0, /device:TPU:0, one launch (start us, length us, event | category | flops | bytes accessed | tf_op | source)
XLA Modules:
  0.0 72.5 jit_solution(10711263805647790823)
XLA Ops:
  0.0 0.8 %fusion.184 = (f32[1,24,8,128]{3,2,1,0:T(8,128)S(1)}, f32[24,8,128]{2,1,0:T(8,128)S(1)}) fusion(bf16[1,24,8,128]{3,2,1,0:T(8,128)(2,1)} %param.4), kind=kLoop, calls=%fused_computation.407 | loop fusion | flops 24576 | bytes 245760 | tf_op jit(solution)/shard_map/convert_element_type | solution.py:171
  0.8 0.7 %pad_maximum_fusion.8 = (f32[4,1,8,128]{3,2,1,0:T(8,128)S(1)}, f32[4,1,8,128]{3,2,1,0:T(8,128)S(1)}) fusion(f32[3,24,8,128]{3,2,1,0:T(8,128)} %bitcast.141, f32[1,24,8,128]{3,2,1,0:T(8,128)S(1)} %get-tuple-element.22), kind=kLoop, calls=%fused_computation.390 | loop fusion | flops 8192 | bytes 425984 | tf_op jit(solution)/shard_map/slice | solution.py:29
  1.5 4.9 %collective-permute-start = (f32[4,1,8,128]{3,2,1,0:T(8,128)S(1)}, f32[4,1,8,128]{3,2,1,0:T(8,128)S(1)}, u32[]{:S(2)}, u32[]{:S(2)}) collective-permute-start(f32[4,1,8,128]{3,2,1,0:T(8,128)S(1)} %get-tuple-element.14), channel_id=1, source_target_pairs={{0,1},{1,2},{2,3},{4,5},{5,6},{6,7},{8,9},{9,10},{10,11},{12,13},{... | collective-permute-start | bytes 49160 | tf_op jit(solution)/shard_map/ppermute | solution.py:28
  6.5 1.3 %collective-permute-start.1 = (f32[4,1,8,128]{3,2,1,0:T(8,128)S(1)}, f32[4,1,8,128]{3,2,1,0:T(8,128)S(1)}, u32[]{:S(2)}, u32[]{:S(2)}) collective-permute-start(f32[4,1,8,128]{3,2,1,0:T(8,128)S(1)} %get-tuple-element.15), channel_id=1, source_target_pairs={{1,0},{2,1},{3,2},{5,4},{6,5},{7,6},{9,8},{10,9},{11,10},{13,12},{... | collective-permute-start | bytes 49160 | tf_op jit(solution)/shard_map/ppermute | solution.py:31
  7.8 1.2 %dynamic_slice.18 = s32[1]{0:T(128)} dynamic-slice(s32[4]{0:T(128)} %param.6, s32[]{:T(128)S(6)} %select_n.19), dynamic_slice_sizes={1} | dynamic-slice | bytes 12 | tf_op jit(solution)/shard_map/dynamic_slice | solution.py:167
  9.1 0.6 iota_compare_fusion
  11.7 1.5 %constant_dynamic-slice_fusion = (s32[1,1]{0,1:T(1,128)}, s32[1,1]{0,1:T(1,128)}, s32[1,1]{0,1:T(1,128)}, s32[1,1]{0,1:T(1,128)}) fusion(s32[4,2]{0,1:T(2,128)} %param.7, s32[]{:T(128)S(6)} %select_n.19, s32[]{:T(128)S(6)} %select_n.21), kind=kLoop, calls=%fused_computation.394 | loop fusion | bytes 40 | tf_op jit(solution)/shard_map/dynamic_slice | solution.py:169
  15.7 1.1 %fusion.160 = bf16[24,8,128]{2,1,0:T(8,128)(2,1)S(1)} fusion(f32[24,8,128]{2,1,0:T(8,128)S(1)} %get-tuple-element.23, f32[4,1,8,128]{3,2,1,0:T(8,128)S(1)} %collective-permute-done.1, f32[3,24,8,128]{3,2,1,0:T(8,128)} %bitcast.142, f32[1,24,8,128]{3,2,1,0:T(8,128)S(1)} %get-tuple-element.22, f32[4,1,8,128]{3,2,1,0:T(8,128)S(1)} %collective-permute-done, ...), kind=kLoop, calls=%fused_computation.363 | loop fusion | flops 737280 | bytes 868448 | tf_op jit(solution)/shard_map/convert_element_type | solution.py:173
  16.8 5.6 %all-gather = bf16[96,8,128]{2,1,0:T(8,128)(2,1)S(1)} all-gather(bf16[24,8,128]{2,1,0:T(8,128)(2,1)S(1)} %fusion.160), channel_id=2, replica_groups=mesh['groups'=2,'brain'=4,'slab'=4] {'brain'}, dimensions={0}, use_global_device_ids=true | all-gather | bytes 245760 | tf_op jit(solution)/shard_map/all_gather | solution.py:174
  22.7 4.5 %collective-permute-start.2 = (bf16[2,6,8,128]{3,2,1,0:T(8,128)(2,1)S(1)}, bf16[2,6,8,128]{3,2,1,0:T(8,128)(2,1)S(1)}, u32[]{:S(2)}, u32[]{:S(2)}) collective-permute-start(bf16[2,6,8,128]{3,2,1,0:T(8,128)(2,1)S(1)} %get-tuple-element.20), channel_id=1, source_target_pairs={{0,1},{1,2},{2,3},{4,5},{5,6},{6,7},{8,9},{9,10},{10,11},{12,13},{... | collective-permute-start | bytes 73736 | tf_op jit(solution)/shard_map/ppermute | solution.py:28
  27.2 1.3 %collective-permute-start.3 = (bf16[2,6,8,128]{3,2,1,0:T(8,128)(2,1)S(1)}, bf16[2,6,8,128]{3,2,1,0:T(8,128)(2,1)S(1)}, u32[]{:S(2)}, u32[]{:S(2)}) collective-permute-start(bf16[2,6,8,128]{3,2,1,0:T(8,128)(2,1)S(1)} %get-tuple-element.21), channel_id=1, source_target_pairs={{1,0},{2,1},{3,2},{5,4},{6,5},{7,6},{9,8},{10,9},{11,10},{13,12},{... | collective-permute-start | bytes 73736 | tf_op jit(solution)/shard_map/ppermute | solution.py:31
  28.7 4.2 %collective-permute-done.3 = bf16[2,6,8,128]{3,2,1,0:T(8,128)(2,1)S(1)} collective-permute-done((bf16[2,6,8,128]{3,2,1,0:T(8,128)(2,1)S(1)}, bf16[2,6,8,128]{3,2,1,0:T(8,128)(2,1)S(1)}, u32[]{:S(2)}, u32[]{:S(2)}) %collective-permute-start.3) | collective-permute-done | bytes 24608 | tf_op jit(solution)/shard_map/ppermute | solution.py:31
  34.8 0.3 fusion.1
  36.7 0.3 fusion.6
  37.0 1.7 %fusion.178 = (f32[32,8,128]{2,1,0:T(8,128)S(1)}, f32[32,8,128]{2,1,0:T(8,128)S(1)}) fusion(f32[12,32,8,128]{3,2,1,0:T(8,128)S(1)} %fusion.6, f32[12,32,8,128]{3,2,1,0:T(8,128)S(1)} %fusion.1), kind=kLoop, calls=%fused_computation.401 | loop fusion | flops 3080192 | bytes 3407872 | tf_op jit(solution)/shard_map/reduce_sum | solution.py:122
  38.8 2.0 %fusion.181 = (f32[12,32,8,128]{3,2,1,0:T(8,128)S(1)}, f32[12,32,8,128]{3,2,1,0:T(8,128)S(1)}, f32[12,32,8,128]{3,2,1,0:T(8,128)S(1)}, f32[12,32,8,128]{3,2,1,0:T(8,128)S(1)}) fusion(f32[32]{0:T(128)S(1)} %and_convert_fusion, f32[32,8,128]{2,1,0:T(8,128)S(1)} %multiply_add_fusion.1, f32[12,32,8,128]{3,2,1,0:T(8,128)S(1)} %fusion.1, ...), kind=kLoop, calls=%fused_computation.404 | loop fusion | flops 5505024 | bytes 9699456 | tf_op jit(solution)/shard_map/mul | solution.py:137
  40.8 0.4 slice_add_fusion.33
  41.4 0.4 fusion.182
  41.8 0.4 slice_add_fusion.4
  42.2 0.9 %fusion.92 = f32[12,24,8,128]{3,2,1,0:T(8,128)S(1)} fusion(f32[12,24,8,128]{3,2,1,0:T(8,128)S(1)} %slice_add_fusion.4), kind=kLoop, calls=%fused_computation.190 | loop fusion | flops 2359296 | bytes 2359296 | tf_op jit(solution)/shard_map/add | solution.py:58
  43.1 0.4 slice_add_fusion.12
  43.6 0.9 %fusion.73 = f32[12,24,8,128]{3,2,1,0:T(8,128)S(1)} fusion(f32[12,24,8,128]{3,2,1,0:T(8,128)S(1)} %slice_add_fusion.12), kind=kLoop, calls=%fused_computation.171 | loop fusion | flops 2359296 | bytes 2359296 | tf_op jit(solution)/shard_map/add | solution.py:58
  44.5 0.9 %fusion.17 = f32[12,24,8,128]{3,2,1,0:T(8,128)S(1)} fusion(f32[12,24,8,128]{3,2,1,0:T(8,128)S(1)} %slice_add_fusion.33), kind=kLoop, calls=%fused_computation.115 | loop fusion | flops 2359296 | bytes 2359296 | tf_op jit(solution)/shard_map/add | solution.py:58
  45.4 0.4 slice_add_fusion.25
  45.8 0.9 %fusion.34 = f32[12,24,8,128]{3,2,1,0:T(8,128)S(1)} fusion(f32[12,24,8,128]{3,2,1,0:T(8,128)S(1)} %slice_add_fusion.25), kind=kLoop, calls=%fused_computation.132 | loop fusion | flops 2359296 | bytes 2359296 | tf_op jit(solution)/shard_map/add | solution.py:58
  46.8 0.9 %fusion.56 = f32[12,24,8,128]{3,2,1,0:T(8,128)S(1)} fusion(f32[12,24,8,128]{3,2,1,0:T(8,128)S(1)} %get-tuple-element.13), kind=kLoop, calls=%fused_computation.154 | loop fusion | flops 2359296 | bytes 2359296 | tf_op jit(solution)/shard_map/add | solution.py:58
  47.7 13.2 %fusion.109 = (f32[24,8,128]{2,1,0:T(8,128)S(1)}, f32[24,8,128]{2,1,0:T(8,128)S(1)}, f32[24,8,128]{2,1,0:T(8,128)S(1)}) fusion(f32[12,24,8,128]{3,2,1,0:T(8,128)S(1)} %get-tuple-element.12, f32[12,32,8,128]{3,2,1,0:T(8,128)S(1)} %get-tuple-element.29, f32[12,24,8,128]{3,2,1,0:T(8,128)S(1)} %fusion.92, f32[12,24,8,128]{3,2,1,0:T(8,128)S(1)} %fusion.73, ...), kind=kLoop, calls=%fused_computation.207 | loop fusion | flops 21159936 | bytes 12091392 | tf_op jit(solution)/shard_map/reduce_sum | solution.py:150
  61.1 3.5 %collective-permute-start.4 = (bf16[3,3,8,128]{3,2,1,0:T(8,128)(2,1)S(1)}, bf16[3,3,8,128]{3,2,1,0:T(8,128)(2,1)S(1)}, u32[]{:S(2)}, u32[]{:S(2)}) collective-permute-start(bf16[3,3,8,128]{3,2,1,0:T(8,128)(2,1)S(1)} %get-tuple-element.16), channel_id=1, source_target_pairs={{0,1},{1,2},{2,3},{4,5},{5,6},{6,7},{8,9},{9,10},{10,11},{12,13},{... | collective-permute-start | bytes 55304 | tf_op jit(solution)/shard_map/ppermute | solution.py:28
  64.6 1.3 %collective-permute-start.5 = (bf16[3,3,8,128]{3,2,1,0:T(8,128)(2,1)S(1)}, bf16[3,3,8,128]{3,2,1,0:T(8,128)(2,1)S(1)}, u32[]{:S(2)}, u32[]{:S(2)}) collective-permute-start(bf16[3,3,8,128]{3,2,1,0:T(8,128)(2,1)S(1)} %get-tuple-element.17), channel_id=1, source_target_pairs={{1,0},{2,1},{3,2},{5,4},{6,5},{7,6},{9,8},{10,9},{11,10},{13,12},{... | collective-permute-start | bytes 55304 | tf_op jit(solution)/shard_map/ppermute | solution.py:31
  66.0 4.2 %collective-permute-done.5 = bf16[3,3,8,128]{3,2,1,0:T(8,128)(2,1)S(1)} collective-permute-done((bf16[3,3,8,128]{3,2,1,0:T(8,128)(2,1)S(1)}, bf16[3,3,8,128]{3,2,1,0:T(8,128)(2,1)S(1)}, u32[]{:S(2)}, u32[]{:S(2)}) %collective-permute-start.5) | collective-permute-done | bytes 18464 | tf_op jit(solution)/shard_map/ppermute | solution.py:31
  70.6 0.6 copy-done
  71.2 1.2 %fusion.140 = f32[1,3,24,8,128]{4,3,2,1,0:T(8,128)} fusion(f32[3,24,8,128]{3,2,1,0:T(8,128)S(1)} %fusion.125, f32[1,3,24,8,128]{4,3,2,1,0:T(8,128)S(1)} %copy-done), kind=kLoop, calls=%fused_computation.289 | loop fusion | flops 1105920 | bytes 884736 | tf_op jit(solution)/shard_map/broadcast_in_dim | solution.py:187
  (49 shorter events, 4.6 us)
Async XLA Ops:
  1.5 14.1 %collective-permute-start = (f32[4,1,8,128]{3,2,1,0:T(8,128)S(1)}, f32[4,1,8,128]{3,2,1,0:T(8,128)S(1)}, u32[]{:S(2)}, u32[]{:S(2)}) collective-permute-start(f32[4,1,8,128]{3,2,1,0:T(8,128)S(1)} %get-tuple-element.14), channel_id=1, source_target_pairs={{0,1},{1,2},{2,3},{4,5},{5,6},{6,7},{8,9},{9,10},{10,11},{12,13},{... | collective-permute-start | bytes 49160 | tf_op jit(solution)/shard_map/ppermute | solution.py:28
  6.5 9.2 %collective-permute-start.1 = (f32[4,1,8,128]{3,2,1,0:T(8,128)S(1)}, f32[4,1,8,128]{3,2,1,0:T(8,128)S(1)}, u32[]{:S(2)}, u32[]{:S(2)}) collective-permute-start(f32[4,1,8,128]{3,2,1,0:T(8,128)S(1)} %get-tuple-element.15), channel_id=1, source_target_pairs={{1,0},{2,1},{3,2},{5,4},{6,5},{7,6},{9,8},{10,9},{11,10},{13,12},{... | collective-permute-start | bytes 49160 | tf_op jit(solution)/shard_map/ppermute | solution.py:31
  22.7 6.1 %collective-permute-start.2 = (bf16[2,6,8,128]{3,2,1,0:T(8,128)(2,1)S(1)}, bf16[2,6,8,128]{3,2,1,0:T(8,128)(2,1)S(1)}, u32[]{:S(2)}, u32[]{:S(2)}) collective-permute-start(bf16[2,6,8,128]{3,2,1,0:T(8,128)(2,1)S(1)} %get-tuple-element.20), channel_id=1, source_target_pairs={{0,1},{1,2},{2,3},{4,5},{5,6},{6,7},{8,9},{9,10},{10,11},{12,13},{... | collective-permute-start | bytes 73736 | tf_op jit(solution)/shard_map/ppermute | solution.py:28
  27.2 5.7 %collective-permute-start.3 = (bf16[2,6,8,128]{3,2,1,0:T(8,128)(2,1)S(1)}, bf16[2,6,8,128]{3,2,1,0:T(8,128)(2,1)S(1)}, u32[]{:S(2)}, u32[]{:S(2)}) collective-permute-start(bf16[2,6,8,128]{3,2,1,0:T(8,128)(2,1)S(1)} %get-tuple-element.21), channel_id=1, source_target_pairs={{1,0},{2,1},{3,2},{5,4},{6,5},{7,6},{9,8},{10,9},{11,10},{13,12},{... | collective-permute-start | bytes 73736 | tf_op jit(solution)/shard_map/ppermute | solution.py:31
  61.1 4.9 %collective-permute-start.4 = (bf16[3,3,8,128]{3,2,1,0:T(8,128)(2,1)S(1)}, bf16[3,3,8,128]{3,2,1,0:T(8,128)(2,1)S(1)}, u32[]{:S(2)}, u32[]{:S(2)}) collective-permute-start(bf16[3,3,8,128]{3,2,1,0:T(8,128)(2,1)S(1)} %get-tuple-element.16), channel_id=1, source_target_pairs={{0,1},{1,2},{2,3},{4,5},{5,6},{6,7},{8,9},{9,10},{10,11},{12,13},{... | collective-permute-start | bytes 55304 | tf_op jit(solution)/shard_map/ppermute | solution.py:28
  64.6 5.7 %collective-permute-start.5 = (bf16[3,3,8,128]{3,2,1,0:T(8,128)(2,1)S(1)}, bf16[3,3,8,128]{3,2,1,0:T(8,128)(2,1)S(1)}, u32[]{:S(2)}, u32[]{:S(2)}) collective-permute-start(bf16[3,3,8,128]{3,2,1,0:T(8,128)(2,1)S(1)} %get-tuple-element.17), channel_id=1, source_target_pairs={{1,0},{2,1},{3,2},{5,4},{6,5},{7,6},{9,8},{10,9},{11,10},{13,12},{... | collective-permute-start | bytes 55304 | tf_op jit(solution)/shard_map/ppermute | solution.py:31
  70.2 1.0 %copy-start = (f32[1,3,24,8,128]{4,3,2,1,0:T(8,128)S(1)}, f32[1,3,24,8,128]{4,3,2,1,0:T(8,128)}, u32[]{:S(2)}) copy-start(f32[1,3,24,8,128]{4,3,2,1,0:T(8,128)} %param.5) | copy-start | bytes 884740
where the time goes:
time: 73 us; the launch traced here: 72.5 us
  other arithmetic  32.9 us (45%)
  starting transfers between devices  16.8 us (23%)
  waiting for transfers between devices  8.76 us (12%)
  blocking collectives  5.61 us (8%)
  between operations  4.92 us (7%)
  local copies, waits for them, and re-layouts  3.48 us (5%)
    reduce_sum x1, other arithmetic, force_field(): jnp.sum(coefficient * grad_part, axis=0)  13.2 us
    ppermute x3, starting transfers between devices, extended(): lax.ppermute(lax.slice_in_dim(block, block.shape[dim] - width, None, axis...  13 us
    ppermute x3, waiting for transfers between devices, extended(): lax.ppermute(lax.slice_in_dim(block, 0, width, axis=dim), axis, backward)  8.43 us
    all_gather x1, blocking collectives, shards(): shard_rows = lax.all_gather(warped[None], 'brain', axis=0, tiled=True)  5.61 us
    add x7, other arithmetic, flat_total(): sum((shifted(running, dim_index, j) for j in range(-radius, radius + 1)))  5.2 us
    ppermute x3, starting transfers between devices, extended(): lax.ppermute(lax.slice_in_dim(block, 0, width, axis=dim), axis, backward)  3.88 us
    unnamed x21, other arithmetic  2.62 us
    mul x1, other arithmetic, force_field(): mate_desc * mate_desc  2.04 us
  transfers between devices with their start and end apart: 6, of which 4 were waited for; matrix products, arithmetic and copies ran while one was open for 5% of the time, Pallas kernels for 0%

commit v1 on v0

v1 whole, which is shorter than its diff:
```python
import functools
import jax, jax.numpy as jnp, numpy as np
from jax import lax
from jax.experimental import pallas as pl
from jax.experimental.pallas import tpu as pltpu
from jax.sharding import PartitionSpec as P

PAIRS = tuple((i, j) for i in range(6) for j in range(i + 1, 6) if i // 2 != j // 2)
TAPS = tuple(float(v) for v in np.exp(-np.arange(-3, 4) ** 2 / 4.5) / np.exp(-np.arange(-3, 4) ** 2 / 4.5).sum())
f32, bf16 = jnp.float32, jnp.bfloat16
LOG2E = 1.4426950408889634


def split(v):
    hi = v.astype(bf16)
    return hi, (v - hi.astype(f32)).astype(bf16)


def main_kernel(planes, meta, own, m1, m2, m3, vel, out, mats, xs, raw, tb, desc, ys, lhs, res, frc):
    nx = planes + 18
    nd = planes + 16
    nf = planes + 8
    ng, nfg = nd // 8, nf // 8
    dr, dc = meta[1], meta[2]
    low, high = meta[3].astype(f32), meta[4].astype(f32)

    i = lax.broadcasted_iota(jnp.int32, (128, 128), 0)
    j = lax.broadcasted_iota(jnp.int32, (128, 128), 1)
    one = lambda cond: jnp.where(cond, 1.0, 0.0).astype(bf16)
    box9 = one(jnp.abs(i - j) <= 4)
    box3 = one(jnp.abs(i - j) <= 1)
    grad = jnp.where(i == j + 1, 1.0, jnp.where(i == j - 1, -1.0, 0.0)).astype(bf16)
    smooth = jnp.zeros((128, 128), f32)
    for d in range(4):
        smooth = jnp.where(jnp.abs(i - j) == d, TAPS[3 + d], smooth)
    shi, slo = split(smooth)
    for h in (0, 128):
        mats[0, h:h + 128] = box3
        mats[1, h:h + 128] = box9
        mats[2, h:h + 128] = grad
        mats[3, h:h + 128] = shi
    mats[4, 0:128] = slo
    row = lax.broadcasted_iota(jnp.int32, (8, 128), 0)

    x = own[...]
    for n, d in ((0, 0), (3, 1), (4, -1)):
        if d == 0:
            v = x.astype(f32)
        else:
            v = jnp.dot(x, one(i == j + d), preferred_element_type=f32)
        xs[0, n] = v
    which = meta[0]
    x = jnp.where(which == 1, m1[...], jnp.where(which == 2, m2[...], m3[...]))
    for n, d in ((0, 0), (1, 1), (2, -1)):
        sel = one((i == j + d + dc) & (j + d >= 0) & (j + d < 128))
        raw[n, pl.ds(8, nx * 8), :] = jnp.dot(x, sel, preferred_element_type=f32)

    def rowmask(d):
        return (row + d >= 0) & (row + d < 8)

    def prep(p, _):
        at = pl.multiple_of(p * 8, 8)
        for n, d in ((1, 1), (2, -1)):
            if True:
                v = raw_own(p, d)
                xs[0, n, pl.ds(at, 8), :] = jnp.where(rowmask(d), v, 0.0)
        for n, b, d in ((0, 0, 0), (1, 0, 1), (2, 0, -1), (3, 1, 0), (4, 2, 0)):
            v = raw[b, pl.ds(at + 8 + dr + d, 8), :]
            xs[1, n, pl.ds(at, 8), :] = jnp.where(rowmask(d) & rowmask(d + dr), v, 0.0)
        return 0

    def raw_own(p, d):
        return pltpu.roll(xs[0, 0, pl.ds(pl.multiple_of(p * 8, 8), 8), :], (-d) % 8, 0)
    lax.fori_loop(0, nx, prep, 0, unroll=6)

    for m in range(2):
        def squares(g, carry, m=m):
            c1, c2 = carry
            scale = jnp.where(g == 0, low, jnp.where(g == ng - 1, high, 1.0))
            for i in range(8):
                s = g * 8 + i
                ld = lambda n, p: xs[m, n, pl.ds(pl.multiple_of(p * 8, 8), 8), :]
                near = [ld(0, s + 2), ld(0, s)] + [ld(j, s + 1) for j in (1, 2, 3, 4)]
                n1, n2 = [], []
                for k, (a, b) in enumerate(PAIRS):
                    d = near[a] - near[b]
                    q = d * d * scale
                    tb[k, pl.ds(pl.multiple_of(s * 8, 8), 8), :] = c2[k] + q
                    n2.append(c1[k] + q)
                    n1.append(q)
                c1, c2 = n1, n2
            return c1, c2
        zero = [jnp.zeros((8, 128), f32)] * 12
        c1, c2 = lax.fori_loop(0, ng, squares, (zero, zero))
        for k in range(12):
            tb[k, pl.ds(nd * 8, 8), :] = c2[k]

        def descr(g, _, m=m):
            base = g * 64
            for k in range(12):
                t = [tb[k, pl.ds(base + 8 + r, 8, stride=8), :] for r in range(8)]
                p = [t[r] + t[r + 1] for r in range(7)]
                w = [p[0]] + [p[r - 1] + t[r + 1] for r in range(1, 7)] + [p[6]]
                hi, lo = split(jnp.concatenate(w, axis=0))
                lhs[pl.ds(k * 64, 64), 0:128] = hi
                lhs[pl.ds(k * 64, 64), 128:256] = lo
            ys[0, 0:768] = jnp.dot(lhs[0:768], mats[0], preferred_element_type=f32)
            mask = jnp.where(g == 0, low, jnp.where(g == ng - 1, high, 1.0))
            for r in range(8):
                v = [ys[0, pl.ds(k * 64 + r * 8, 8), :] for k in range(12)]
                total = functools.reduce(jnp.add, v)
                inv = (-LOG2E / 27.0) / (total * (1.0 / 324.0) + 0.1)
                for k in range(12):
                    desc[m, k, pl.ds(base + r, 8, stride=8), :] = jnp.exp2(v[k] * inv) * mask
            return 0
        lax.fori_loop(0, ng, descr, 0)

    def channel(k, _):
        for q in range(5):
            def val(t):
                ld = lambda m: desc[m, k, pl.ds(t * 8, 8), :]
                if q == 0:
                    return ld(0)
                if q == 1:
                    return ld(1)
                if q == 2:
                    v = ld(0)
                    return v * v
                if q == 3:
                    v = ld(1)
                    return v * v
                return ld(0) * ld(1)
            d = [val(t) for t in range(nd)]
            s2 = [d[t] + d[t + 1] for t in range(nd - 1)]
            s4 = [s2[t] + s2[t + 2] for t in range(nd - 3)]
            for f in range(nf):
                ys[q, pl.ds(f * 8, 8), :] = s4[f] + s4[f + 4] + d[f + 8]

        for g in range(nfg):
            base = g * 64
            for q in range(5):
                t = [ys[q, pl.ds(base + r, 8, stride=8), :] for r in range(8)]
                lo = (t[0] + t[1]) + (t[2] + t[3])
                hi = (t[4] + t[5]) + (t[6] + t[7])
                w = [None] * 8
                w[0] = lo + t[4]
                w[1] = w[0] + t[5]
                w[2] = w[1] + t[6]
                w[3] = lo + hi
                w[4] = w[3]
                w[7] = hi + t[3]
                w[6] = w[7] + t[2]
                w[5] = w[6] + t[1]
                hi, lo = split(jnp.concatenate(w, axis=0))
                at = pl.ds(q * nf * 8 + base, 64)
                lhs[at, 0:128] = hi
                lhs[at, 128:256] = lo
            a = [desc[0, k, pl.ds(base + 32 + r, 8, stride=8), :] for r in range(8)]
            hi, lo = split(jnp.concatenate(a, axis=0))
            at = pl.ds(5 * nf * 8 + base, 64)
            lhs[at, 0:128] = hi
            lhs[at, 128:256] = lo
        n5 = 5 * nf * 8
        res[0:n5] = jnp.dot(lhs[0:n5], mats[1], preferred_element_type=f32)
        res[n5:n5 + nf * 8] = jnp.dot(lhs[n5:n5 + nf * 8], mats[2], preferred_element_type=f32)

        for g in range(nfg):
            base = g * 64
            a = [desc[0, k, pl.ds(base + 32 + r, 8, stride=8), :] for r in range(8)]
            for r in range(8):
                mo, mm, so, sm, sc, gc = [res[pl.ds(q * nf * 8 + base + r * 8, 8), :] for q in range(6)]
                b = desc[1, k, pl.ds(base + 32 + r, 8, stride=8), :]
                vo = 729.0 * so - mo * mo + (1e-5 * 729.0 * 729.0)
                vm = 729.0 * sm - mm * mm + (1e-5 * 729.0 * 729.0)
                cv = 729.0 * sc - mo * mm
                io, im = lax.rsqrt(vo), lax.rsqrt(vm)
                coef = (729.0 * b - mm - (cv * io) * io * (729.0 * a[r] - mo)) * (io * im)
                gz = desc[0, k, pl.ds(base + 40 + r, 8, stride=8), :] - desc[0, k, pl.ds(base + 24 + r, 8, stride=8), :]
                if r == 0:
                    gr = a[1]
                elif r == 7:
                    gr = -a[6]
                else:
                    gr = a[r + 1] - a[r - 1]
                for c, gg in enumerate((gz, gr, gc)):
                    at = (c, pl.ds(base + r * 8, 8), slice(None))
                    frc[at] = frc[at] + coef * gg
        return 0
    frc[...] = jnp.zeros_like(frc)
    lax.fori_loop(0, 12, channel, 0)

    for c in range(3):
        scale = 729.0 / 24.0
        for g in range(nfg):
            for r in range(8):
                v = frc[c, pl.ds(g * 64 + r * 8, 8), :]
                if g == 0:
                    v = jnp.where(row >= 4, v, v * low)
                if g == nfg - 1:
                    v = jnp.where(row < 4, v, v * high)
                ys[0, pl.ds(g * 64 + r, 8, stride=8), :] = v
        for o in range(planes):
            p = [ys[0, pl.ds((o + 1 + j) * 8, 8), :] for j in range(7)]
            v = TAPS[3] * p[3]
            for j in range(3):
                v = v + TAPS[j] * (p[j] + p[6 - j])
            ys[1, pl.ds(o * 8, 8), :] = v
        for g in range(planes // 8):
            t = [ys[1, pl.ds(g * 64 + r, 8, stride=8), :] for r in range(8)]
            w = []
            for r in range(8):
                v = TAPS[3] * t[r]
                for j in range(1, 4):
                    n = [t[i] for i in (r - j, r + j) if 0 <= i < 8]
                    v = v + TAPS[3 + j] * (n[0] + n[1] if len(n) == 2 else n[0])
                w.append(v)
            hi, lo = split(jnp.concatenate(w, axis=0))
            lhs[pl.ds((c * planes + g * 8) * 8, 64), 0:128] = hi
            lhs[pl.ds((c * planes + g * 8) * 8, 64), 128:256] = lo
    n3 = 3 * planes * 8
    v = jnp.dot(lhs[0:n3], mats[3], preferred_element_type=f32)
    v = v + jnp.dot(lhs[0:n3, 0:128], mats[4, 0:128], preferred_element_type=f32)
    res[0:n3] = v
    for c in range(3):
        for g in range(planes // 8):
            for r in range(8):
                ys[0, pl.ds(g * 64 + r, 8, stride=8), :] = res[pl.ds((c * planes + g * 8 + r) * 8, 8), :]
        for o in range(planes):
            out[c, o] = vel[c, o] + (8.0 * scale) * ys[0, pl.ds(o * 8, 8), :]


EDGE = 13


def advect_kernel(planes, image, vel, warp, down, up):
    lane = lax.broadcasted_iota(jnp.int32, (8, 128), 1)
    row = lax.broadcasted_iota(jnp.int32, (8, 128), 0)

    def halves(x):
        hi = x.astype(bf16)
        return hi, (x - hi.astype(f32)).astype(bf16)

    for z in range(planes):
        x = image[0, z].astype(f32)
        before = image[0, z - 1].astype(f32) if z > 0 else x
        after = image[0, z + 1].astype(f32) if z < planes - 1 else x
        sides = (
            (before, after),
            (jnp.where(row >= 1, pltpu.roll(x, 1, 0), 0.0), jnp.where(row < 7, pltpu.roll(x, 7, 0), 0.0)),
            (jnp.where(lane >= 1, pltpu.roll(x, 1, 1), 0.0), jnp.where(lane < 127, pltpu.roll(x, 127, 1), 0.0)),
        )
        moved = 0.0
        for c, (lo, hi) in enumerate(sides):
            v = vel[0, c, z]
            moved = moved + (jnp.maximum(v, 0.0) * (x - lo) + jnp.minimum(v, 0.0) * (hi - x))
        y = x - moved
        warp[z] = y
        if z == 0 or z == planes - 1:
            ref, v = (down, jnp.maximum(vel[0, 0, z], 0.0)) if z == 0 else (up, jnp.minimum(vel[0, 0, z], 0.0))
            for n, part in enumerate(halves(y) + halves(v) + (image[0, z],)):
                ref[8 + n] = part
        if 1 <= z <= 8:
            down[z - 1] = y.astype(bf16)
        if planes - 9 <= z < planes - 1:
            up[z - (planes - 9)] = y.astype(bf16)


def widen_kernel(planes, warp, below, above, image, vel, out):
    has_low = lax.axis_index("slab") > 0
    has_high = lax.axis_index("slab") < lax.axis_size("slab") - 1
    ld = lambda ref, n: ref[n].astype(f32)
    first, last = image[0, 0].astype(f32), image[0, planes - 1].astype(f32)
    top = planes - 1
    for n in range(8):
        out[n] = below[n]
        out[planes + 10 + n] = above[n]
    out[8] = ((ld(below, 8) + ld(below, 9)) - (ld(below, 10) + ld(below, 11)) * (first - ld(below, 12))).astype(bf16)
    out[planes + 9] = ((ld(above, 8) + ld(above, 9)) - (ld(above, 10) + ld(above, 11)) * (ld(above, 12) - last)).astype(bf16)
    for z in range(1, top):
        out[9 + z] = warp[z].astype(bf16)
    out[9] = (warp[0] - jnp.maximum(vel[0, 0, 0], 0.0) * (first - ld(below, 12))).astype(bf16)
    out[9 + top] = (warp[top] - jnp.minimum(vel[0, 0, top], 0.0) * (ld(above, 12) - last)).astype(bf16)
    zero = jnp.zeros((9, 8, 128), bf16)

    @pl.when(jnp.logical_not(has_low))
    def _():
        out[0:9] = zero

    @pl.when(jnp.logical_not(has_high))
    def _():
        out[planes + 9:planes + 18] = zero


def shards(intensity, velocity, partner, offsets):
    planes = intensity.shape[1]
    slabs, brains = lax.axis_size("slab"), lax.axis_size("brain")
    vm = pl.BlockSpec(memory_space=pltpu.VMEM)
    edge = jax.ShapeDtypeStruct((EDGE, 8, 128), bf16)
    warp, down, up = pl.pallas_call(
        functools.partial(advect_kernel, planes),
        out_shape=(jax.ShapeDtypeStruct((planes, 8, 128), f32), edge, edge),
        in_specs=[vm, vm],
        out_specs=(vm, vm, vm),
        compiler_params=pltpu.CompilerParams(vmem_limit_bytes=8 * 2**20),
        name="advect",
    )(intensity, velocity)
    below = lax.ppermute(up, "slab", [(n, n + 1) for n in range(slabs - 1)])
    above = lax.ppermute(down, "slab", [(n + 1, n) for n in range(slabs - 1)])
    own = pl.pallas_call(
        functools.partial(widen_kernel, planes),
        out_shape=jax.ShapeDtypeStruct((planes + 18, 8, 128), bf16),
        in_specs=[vm] * 5,
        out_specs=vm,
        compiler_params=pltpu.CompilerParams(vmem_limit_bytes=8 * 2**20),
        name="widen",
    )(warp, below, above, intensity, velocity)
    me = lax.axis_index("brain")
    mate = partner[me]
    if brains == 4:
        mates = [lax.ppermute(own, "brain", [(n, n ^ k) for n in range(4)]) for k in (1, 2, 3)]
        which = me ^ mate
    else:
        gathered = lax.all_gather(own, "brain")
        mates = [lax.dynamic_index_in_dim(gathered, mate, 0, keepdims=False)] * 3
        which = jnp.int32(1)
    slab = lax.axis_index("slab")
    shift = offsets[mate] - offsets[me]
    meta = jnp.stack([which, shift[0], shift[1], (slab > 0).astype(jnp.int32), (slab < slabs - 1).astype(jnp.int32)])
    nx, nd, nf = planes + 18, planes + 16, planes + 8
    return pl.pallas_call(
        functools.partial(main_kernel, planes),
        out_shape=jax.ShapeDtypeStruct(velocity.shape[1:], f32),
        in_specs=[pl.BlockSpec(memory_space=pltpu.SMEM)] + [vm] * 5,
        out_specs=vm,
        scratch_shapes=[
            pltpu.VMEM((5, 256, 128), bf16),
            pltpu.VMEM((2, 5, nx * 8, 128), f32),
            pltpu.VMEM((3, nx * 8 + 16, 128), f32),
            pltpu.VMEM((12, (nd + 1) * 8, 128), f32),
            pltpu.VMEM((2, 12, nd * 8, 128), f32),
            pltpu.VMEM((5, max(nf * 8, 768), 128), f32),
            pltpu.VMEM((6 * nf * 8, 256), bf16),
            pltpu.VMEM((6 * nf * 8, 128), f32),
            pltpu.VMEM((3, nf * 8, 128), f32),
        ],
        compiler_params=pltpu.CompilerParams(vmem_limit_bytes=32 * 2**20),
        name="force",
    )(meta, own.reshape(-1, 128), *[m.reshape(-1, 128) for m in mates], velocity[0])[None]


def solution(mesh):
    return jax.shard_map(
        shards,
        mesh=mesh,
        in_specs=(
            P(("groups", "brain"), "slab", None, None),
            P(("groups", "brain"), None, "slab", None, None),
            P("groups"),
            P("groups", None),
        ),
        out_specs=P(("groups", "brain"), None, "slab", None, None),
        check_vma=False,
    )
```

time: 73 us -> 34.6 us (0.47)
  other arithmetic: 32.9 us -> 0.26 us
  Pallas kernels: 0 us -> 15.1 us
  starting transfers between devices: 16.8 us -> 8.15 us
  blocking collectives: 5.61 us -> 0 us
  waiting for transfers between devices: 8.76 us -> 5.13 us
  between operations: 4.92 us -> 2.62 us
    pallas_call x0 -> x3, Pallas kernels: none -> 15.1 us  [the longest x1 14.9 us: shards(): pl.pallas_call(functools.partial(main_kernel, planes), out_shape=jax.Shap...]
    reduce_sum x3 -> x0, other arithmetic: 15 us -> none  [the longest x1 13.2 us: force_field(): jnp.sum(coefficient * grad_part, axis=0)]
    ppermute x6 -> x5, starting transfers between devices: 16.8 us -> 8.15 us  [the longest x1 4.93 us: shards(): below = lax.ppermute(up, 'slab', [(n, n + 1) for n in range(slabs - 1)])]
    add x17 -> x0, other arithmetic: 7.53 us -> none  [the longest x7 5.2 us: flat_total(): sum((shifted(running, dim_index, j) for j in range(-radius, radius + 1)))]
    all_gather x1 -> x0, blocking collectives: 5.61 us -> none  [shards(): shard_rows = lax.all_gather(warped[None], 'brain', axis=0, tiled=True)]
    ppermute x6 -> x5, waiting for transfers between devices: 8.76 us -> 5.13 us  [the longest x3 4.74 us: shards(): lax.ppermute(own, 'brain', [(n, n ^ k) for n in range(4)])]
    unnamed x21 -> x0, other arithmetic: 2.62 us -> none
    mul x3 -> x0, other arithmetic: 2.2 us -> none  [the longest x1 2.04 us: force_field(): mate_desc * mate_desc]
  transfers between devices with their start and end apart: 6 -> 5, of which waited for: 4 -> 3; matrix products, arithmetic and copies ran while one was open for 5% -> 3% of each run, Pallas kernels for 0% -> 0%
where the time goes in v1:
time: 34.6 us; the launch traced here: 34.3 us
  Pallas kernels  15.1 us (44%)
  starting transfers between devices  8.15 us (24%)
  waiting for transfers between devices  5.13 us (15%)
  local copies, waits for them, and re-layouts  3.05 us (9%)
  between operations  2.62 us (8%)
    pallas_call x1, Pallas kernels, shards(): pl.pallas_call(functools.partial(main_kernel, planes), out_shape=jax.Shap...  14.9 us
    ppermute x1, starting transfers between devices, shards(): below = lax.ppermute(up, 'slab', [(n, n + 1) for n in range(slabs - 1)])  4.93 us
    ppermute x3, waiting for transfers between devices, shards(): lax.ppermute(own, 'brain', [(n, n ^ k) for n in range(4)])  4.74 us
    unnamed x12, local copies, waits for them, and re-layouts  2.44 us
    ppermute x3, starting transfers between devices, shards(): lax.ppermute(own, 'brain', [(n, n ^ k) for n in range(4)])  1.93 us
    ppermute x1, starting transfers between devices, shards(): above = lax.ppermute(down, 'slab', [(n + 1, n) for n in range(slabs - 1)])  1.29 us
  transfers between devices with their start and end apart: 5, of which 3 were waited for; matrix products, arithmetic and copies ran while one was open for 3% of the time, Pallas kernels for 0%

profile of v1, /device:TPU:0, one launch (start us, length us, event | category | flops | bytes accessed | tf_op | source)
XLA Modules:
  0.0 34.3 jit_solution(5924598324961858459)
XLA Ops:
  0.0 0.0 copy-start
  0.0 1.0 %copy-done = f32[1,3,24,8,128]{4,3,2,1,0:T(8,128)S(1)} copy-done((f32[1,3,24,8,128]{4,3,2,1,0:T(8,128)S(1)}, f32[1,3,24,8,128]{4,3,2,1,0:T(8,128)}, u32[]{:S(2)}) %copy-start) | copy-done | bytes 294936
  1.0 0.0 copy-start.2
  1.0 0.8 %copy-done.2 = bf16[1,24,8,128]{3,2,1,0:T(8,128)(2,1)S(1)} copy-done((bf16[1,24,8,128]{3,2,1,0:T(8,128)(2,1)S(1)}, bf16[1,24,8,128]{3,2,1,0:T(8,128)(2,1)}, u32[]{:S(2)}) %copy-start.2) | copy-done | bytes 49176
  1.8 0.0 copy-start.1
  1.8 0.0 copy-start.3
  1.8 0.1 advect.1
  1.9 4.9 %collective-permute-start = (bf16[13,8,128]{2,1,0:T(8,128)(2,1)S(1)}, bf16[13,8,128]{2,1,0:T(8,128)(2,1)S(1)}, u32[]{:S(2)}, u32[]{:S(2)}) collective-permute-start(bf16[13,8,128]{2,1,0:T(8,128)(2,1)S(1)} %get-tuple-element.9), channel_id=1, source_target_pairs={{0,1},{1,2},{2,3},{4,5},{5,6},{6,7},{8,9},{9,10},{10,11},{12,13},{... | collective-permute-start | bytes 79880 | tf_op jit(solution)/shard_map/ppermute | solution.py:307
  6.8 1.3 %collective-permute-start.1 = (bf16[13,8,128]{2,1,0:T(8,128)(2,1)S(1)}, bf16[13,8,128]{2,1,0:T(8,128)(2,1)S(1)}, u32[]{:S(2)}, u32[]{:S(2)}) collective-permute-start(bf16[13,8,128]{2,1,0:T(8,128)(2,1)S(1)} %get-tuple-element.10), channel_id=1, source_target_pairs={{1,0},{2,1},{3,2},{5,4},{6,5},{7,6},{9,8},{10,9},{11,10},{13,12},{... | collective-permute-start | bytes 79880 | tf_op jit(solution)/shard_map/ppermute | solution.py:308
  8.1 0.0 copy-start.5
  8.2 0.6 %copy-done.5 = s32[4]{0:T(128)S(1)} copy-done((s32[4]{0:T(128)S(1)}, s32[4]{0:T(128)}, u32[]{:S(2)}) %copy-start.5) | copy-done | bytes 40
  8.8 0.6 %dynamic_slice.9 = s32[1]{0:T(128)} dynamic-slice(s32[4]{0:T(128)S(1)} %copy-done.5, s32[]{:T(128)S(6)} %select_n.7), dynamic_slice_sizes={1} | dynamic-slice | bytes 12 | tf_op jit(solution)/shard_map/dynamic_slice | solution.py:318
  11.3 0.0 copy-start.4
  12.0 0.0 copy-done.4
  12.0 0.2 subtract_reduce_fusion
  12.2 0.0 collective-permute-done.below
  12.2 0.4 %collective-permute-done.1.above = bf16[13,8,128]{2,1,0:T(8,128)(2,1)S(1)} collective-permute-done((bf16[13,8,128]{2,1,0:T(8,128)(2,1)S(1)}, bf16[13,8,128]{2,1,0:T(8,128)(2,1)S(1)}, u32[]{:S(2)}, u32[]{:S(2)}) %collective-permute-start.1) | collective-permute-done | bytes 26656 | tf_op jit(solution)/shard_map/ppermute | solution.py:308
  12.6 0.0 copy-done.1
  12.6 0.0 copy-done.3
  12.6 0.4 %collective-permute-start.4 = (bf16[42,8,128]{2,1,0:T(8,128)(2,1)S(1)}, bf16[42,8,128]{2,1,0:T(8,128)(2,1)S(1)}, u32[]{:S(2)}, u32[]{:S(2)}) collective-permute-start(bf16[42,8,128]{2,1,0:T(8,128)(2,1)S(1)} %widen.1), channel_id=1, source_target_pairs={{0,12},{4,8},{8,4},{12,0},{1,13},{5,9},{9,5},{13,1},{2,14},{6,10},... | collective-permute-start | bytes 258056 | tf_op jit(solution)/shard_map/ppermute | solution.py:320
  13.0 1.3 %collective-permute-start.3 = (bf16[42,8,128]{2,1,0:T(8,128)(2,1)S(1)}, bf16[42,8,128]{2,1,0:T(8,128)(2,1)S(1)}, u32[]{:S(2)}, u32[]{:S(2)}) collective-permute-start(bf16[42,8,128]{2,1,0:T(8,128)(2,1)S(1)} %widen.1), channel_id=1, source_target_pairs={{0,8},{4,12},{8,0},{12,4},{1,9},{5,13},{9,1},{13,5},{2,10},{6,14},... | collective-permute-start | bytes 258056 | tf_op jit(solution)/shard_map/ppermute | solution.py:320
  14.2 0.3 collective-permute-start.2
  14.5 0.1 pad_add_fusion.meta
  14.6 2.8 %collective-permute-done.4 = bf16[42,8,128]{2,1,0:T(8,128)(2,1)S(1)} collective-permute-done((bf16[42,8,128]{2,1,0:T(8,128)(2,1)S(1)}, bf16[42,8,128]{2,1,0:T(8,128)(2,1)S(1)}, u32[]{:S(2)}, u32[]{:S(2)}) %collective-permute-start.4) | collective-permute-done | bytes 86048 | tf_op jit(solution)/shard_map/ppermute | solution.py:320
  17.5 1.9 %collective-permute-done.3 = bf16[42,8,128]{2,1,0:T(8,128)(2,1)S(1)} collective-permute-done((bf16[42,8,128]{2,1,0:T(8,128)(2,1)S(1)}, bf16[42,8,128]{2,1,0:T(8,128)(2,1)S(1)}, u32[]{:S(2)}, u32[]{:S(2)}) %collective-permute-start.3) | collective-permute-done | bytes 86048 | tf_op jit(solution)/shard_map/ppermute | solution.py:320
  19.3 0.0 collective-permute-done.2
  19.4 14.9 %force.1 = f32[3,24,8,128]{3,2,1,0:T(8,128)} custom-call(s32[5]{0:T(128)S(1)} %pad_add_fusion.meta, bf16[336,128]{1,0:T(8,128)(2,1)S(1)} %bitcast.11, bf16[336,128]{1,0:T(8,128)(2,1)S(1)} %bitcast.14, bf16[336,128]{1,0:T(8,128)(2,1)S(1)} %bitcast.13, bf16[336,128]{1,0:T(8,128)(2,1)S(1)} %bitcast.12, f32[3,24,8,128]{3,2,1,0:T(8,128)S(1)} %bitcast.10), custom_call_target="tpu_custom_call" | custom-call | tf_op jit(solution)/shard_map/force/pallas_call | solution.py:330
  (1 shorter events, 0.0 us)
Async XLA Ops:
  0.0 1.0 %copy-start = (f32[1,3,24,8,128]{4,3,2,1,0:T(8,128)S(1)}, f32[1,3,24,8,128]{4,3,2,1,0:T(8,128)}, u32[]{:S(2)}) copy-start(f32[1,3,24,8,128]{4,3,2,1,0:T(8,128)} %vel.3) | copy-start | bytes 884740
  1.0 0.8 %copy-start.2 = (bf16[1,24,8,128]{3,2,1,0:T(8,128)(2,1)S(1)}, bf16[1,24,8,128]{3,2,1,0:T(8,128)(2,1)}, u32[]{:S(2)}) copy-start(bf16[1,24,8,128]{3,2,1,0:T(8,128)(2,1)} %image.3) | copy-start | bytes 147460
  1.8 10.8 %copy-start.1 = (f32[1,3,24,8,128]{4,3,2,1,0:T(8,128)S(1)}, f32[1,3,24,8,128]{4,3,2,1,0:T(8,128)}, u32[]{:S(2)}) copy-start(f32[1,3,24,8,128]{4,3,2,1,0:T(8,128)} %vel.3) | copy-start | bytes 884740
  1.8 10.8 %copy-start.3 = (bf16[1,24,8,128]{3,2,1,0:T(8,128)(2,1)S(1)}, bf16[1,24,8,128]{3,2,1,0:T(8,128)(2,1)}, u32[]{:S(2)}) copy-start(bf16[1,24,8,128]{3,2,1,0:T(8,128)(2,1)} %image.3) | copy-start | bytes 147460
  1.9 10.3 %collective-permute-start = (bf16[13,8,128]{2,1,0:T(8,128)(2,1)S(1)}, bf16[13,8,128]{2,1,0:T(8,128)(2,1)S(1)}, u32[]{:S(2)}, u32[]{:S(2)}) collective-permute-start(bf16[13,8,128]{2,1,0:T(8,128)(2,1)S(1)} %get-tuple-element.9), channel_id=1, source_target_pairs={{0,1},{1,2},{2,3},{4,5},{5,6},{6,7},{8,9},{9,10},{10,11},{12,13},{... | collective-permute-start | bytes 79880 | tf_op jit(solution)/shard_map/ppermute | solution.py:307
  6.8 5.7 %collective-permute-start.1 = (bf16[13,8,128]{2,1,0:T(8,128)(2,1)S(1)}, bf16[13,8,128]{2,1,0:T(8,128)(2,1)S(1)}, u32[]{:S(2)}, u32[]{:S(2)}) collective-permute-start(bf16[13,8,128]{2,1,0:T(8,128)(2,1)S(1)} %get-tuple-element.10), channel_id=1, source_target_pairs={{1,0},{2,1},{3,2},{5,4},{6,5},{7,6},{9,8},{10,9},{11,10},{13,12},{... | collective-permute-start | bytes 79880 | tf_op jit(solution)/shard_map/ppermute | solution.py:308
  8.1 0.7 %copy-start.5 = (s32[4]{0:T(128)S(1)}, s32[4]{0:T(128)}, u32[]{:S(2)}) copy-start(s32[4]{0:T(128)} %param.6) | copy-start | bytes 52
  11.3 0.7 %copy-start.4 = (s32[4,2]{0,1:T(2,128)S(1)}, s32[4,2]{0,1:T(2,128)}, u32[]{:S(2)}) copy-start(s32[4,2]{0,1:T(2,128)} %param.7) | copy-start | bytes 100
  12.6 4.8 %collective-permute-start.4 = (bf16[42,8,128]{2,1,0:T(8,128)(2,1)S(1)}, bf16[42,8,128]{2,1,0:T(8,128)(2,1)S(1)}, u32[]{:S(2)}, u32[]{:S(2)}) collective-permute-start(bf16[42,8,128]{2,1,0:T(8,128)(2,1)S(1)} %widen.1), channel_id=1, source_target_pairs={{0,12},{4,8},{8,4},{12,0},{1,13},{5,9},{9,5},{13,1},{2,14},{6,10},... | collective-permute-start | bytes 258056 | tf_op jit(solution)/shard_map/ppermute | solution.py:320
  13.0 6.4 %collective-permute-start.3 = (bf16[42,8,128]{2,1,0:T(8,128)(2,1)S(1)}, bf16[42,8,128]{2,1,0:T(8,128)(2,1)S(1)}, u32[]{:S(2)}, u32[]{:S(2)}) collective-permute-start(bf16[42,8,128]{2,1,0:T(8,128)(2,1)S(1)} %widen.1), channel_id=1, source_target_pairs={{0,8},{4,12},{8,0},{12,4},{1,9},{5,13},{9,1},{13,5},{2,10},{6,14},... | collective-permute-start | bytes 258056 | tf_op jit(solution)/shard_map/ppermute | solution.py:320
  14.2 5.1 %collective-permute-start.2 = (bf16[42,8,128]{2,1,0:T(8,128)(2,1)S(1)}, bf16[42,8,128]{2,1,0:T(8,128)(2,1)S(1)}, u32[]{:S(2)}, u32[]{:S(2)}) collective-permute-start(bf16[42,8,128]{2,1,0:T(8,128)(2,1)S(1)} %widen.1), channel_id=1, source_target_pairs={{0,4},{4,0},{8,12},{12,8},{1,5},{5,1},{9,13},{13,9},{2,6},{6,2},{1... | collective-permute-start | bytes 258056 | tf_op jit(solution)/shard_map/ppermute | solution.py:320

commit v2 on v1

v2 whole, which is shorter than its diff:
```python
import functools
import jax, jax.numpy as jnp, numpy as np
from jax import lax
from jax.experimental import pallas as pl
from jax.experimental.pallas import tpu as pltpu
from jax.sharding import PartitionSpec as P

PAIRS = tuple((i, j) for i in range(6) for j in range(i + 1, 6) if i // 2 != j // 2)
TAPS = tuple(float(v) for v in np.exp(-np.arange(-3, 4) ** 2 / 4.5) / np.exp(-np.arange(-3, 4) ** 2 / 4.5).sum())
f32, bf16 = jnp.float32, jnp.bfloat16
LOG2E = 1.4426950408889634
EDGE = 13
VOLUME = 729.0
FLOOR = 1e-5 * VOLUME * VOLUME


def split(v):
    hi = v.astype(bf16)
    return hi, (v - hi.astype(f32)).astype(bf16)


def lanes():
    return (lax.broadcasted_iota(jnp.int32, (128, 128), 0), lax.broadcasted_iota(jnp.int32, (128, 128), 1))


def ones_where(cond):
    return jnp.where(cond, 1.0, 0.0).astype(bf16)


def put_split(lhs, start, parts):
    hi, lo = split(jnp.concatenate(parts, axis=0))
    at = pl.ds(start, 8 * len(parts))
    lhs[at, 0:128] = hi
    lhs[at, 128:256] = lo


def dot(a, b):
    return jnp.dot(a, b, preferred_element_type=f32)


def faces():
    slab = lax.axis_index("slab")
    one = jnp.float32(1.0)
    zero = jnp.float32(0.0)
    return jnp.where(slab > 0, one, zero), jnp.where(slab < lax.axis_size("slab") - 1, one, zero)


def row_inside(d):
    row = lax.broadcasted_iota(jnp.int32, (8, 128), 0)
    return (row + d >= 0) & (row + d < 8)


def describe(planes, xs, box3, tb, lhs, dst, desc, low, high):
    nd = planes + 16
    ng = nd // 8

    def squares(g, carry):
        c1, c2 = carry
        scale = jnp.where(g == 0, low, jnp.where(g == ng - 1, high, 1.0))
        for i in range(8):
            s = g * 8 + i
            ld = lambda n, p: xs[n, pl.ds(pl.multiple_of(p * 8, 8), 8), :]
            near = [ld(0, s + 2), ld(0, s)] + [ld(j, s + 1) for j in (1, 2, 3, 4)]
            n1, n2 = [], []
            for k, (a, b) in enumerate(PAIRS):
                d = near[a] - near[b]
                q = d * d * scale
                tb[k, pl.ds(pl.multiple_of(s * 8, 8), 8), :] = c2[k] + q
                n2.append(c1[k] + q)
                n1.append(q)
            c1, c2 = n1, n2
        return c1, c2
    zero = [jnp.zeros((8, 128), f32)] * 12
    c1, c2 = lax.fori_loop(0, ng, squares, (zero, zero))
    for k in range(12):
        tb[k, pl.ds(nd * 8, 8), :] = c2[k]

    def rows(g):
        for k in range(12):
            t = [tb[k, pl.ds(g * 64 + 8 + r, 8, stride=8), :] for r in range(8)]
            p = [t[r] + t[r + 1] for r in range(7)]
            w = [p[0]] + [p[r - 1] + t[r + 1] for r in range(1, 7)] + [p[6]]
            put_split(lhs, (g % 2) * 768 + k * 64, w)

    rows(0)
    for g in range(ng):
        h = g % 2
        if g + 1 < ng:
            rows(g + 1)
        dst[h * 768:h * 768 + 768] = dot(lhs[h * 768:h * 768 + 768], box3[...])
        for r in range(8):
            v = [dst[pl.ds(h * 768 + k * 64 + r * 8, 8), :] for k in range(12)]
            total = functools.reduce(jnp.add, v)
            inv = (-LOG2E / 27.0) / (total * (1.0 / 324.0) + 0.1)
            for k in range(12):
                e = jnp.exp2(v[k] * inv)
                if g == 0:
                    e = e * low
                if g == ng - 1:
                    e = e * high
                desc[k, pl.ds(g * 64 + r, 8, stride=8), :] = e


def depth_sums(planes, value, ys, q):
    nd, nf = planes + 16, planes + 8
    d = [value(t) for t in range(nd)]
    s2 = [d[t] + d[t + 1] for t in range(nd - 1)]
    s4 = [s2[t] + s2[t + 2] for t in range(nd - 3)]
    for f in range(nf):
        ys[q, pl.ds(f * 8, 8), :] = s4[f] + s4[f + 4] + d[f + 8]


def row_sums(planes, ys, lhs, count):
    nf = planes + 8
    for g in range(nf // 8):
        for q in range(count):
            t = [ys[q, pl.ds(g * 64 + r, 8, stride=8), :] for r in range(8)]
            lo = (t[0] + t[1]) + (t[2] + t[3])
            hi = (t[4] + t[5]) + (t[6] + t[7])
            w = [None] * 8
            w[0] = lo + t[4]
            w[1] = w[0] + t[5]
            w[2] = w[1] + t[6]
            w[3] = lo + hi
            w[4] = w[3]
            w[7] = hi + t[3]
            w[6] = w[7] + t[2]
            w[5] = w[6] + t[1]
            put_split(lhs, q * nf * 8 + g * 64, w)


def over_channels(sums, rows, product, use):
    sums(0)
    rows(0)

    def step(k, _):
        product(k)
        sums(k + 1)
        use(k)
        rows(k + 1)
        return 0
    lax.fori_loop(0, 11, step, 0)
    product(11)
    use(11)


def own_kernel(planes, own, desc, mean, slope, grads, box3, box9, grad, xs, tb, ys, lhs, dst, res):
    nx, nd, nf = planes + 18, planes + 16, planes + 8
    low, high = faces()
    i, j = lanes()
    for h in (0, 128):
        box3[h:h + 128] = ones_where(jnp.abs(i - j) <= 1)
        box9[h:h + 128] = ones_where(jnp.abs(i - j) <= 4)
        grad[h:h + 128] = jnp.where(i == j + 1, 1.0, jnp.where(i == j - 1, -1.0, 0.0)).astype(bf16)
    x = own[...]
    xs[0] = x.astype(f32)
    xs[3] = dot(x, ones_where(i == j + 1))
    xs[4] = dot(x, ones_where(i == j - 1))

    def prep(p, _):
        at = pl.ds(pl.multiple_of(p * 8, 8), 8)
        v = xs[0, at, :]
        xs[1, at, :] = jnp.where(row_inside(1), pltpu.roll(v, 7, 0), 0.0)
        xs[2, at, :] = jnp.where(row_inside(-1), pltpu.roll(v, 1, 0), 0.0)
        return 0
    lax.fori_loop(0, nx, prep, 0, unroll=6)
    describe(planes, xs, box3, tb, lhs, dst, desc, low, high)

    def sums(k):
        ld = lambda t: desc[k, pl.ds(t * 8, 8), :]
        depth_sums(planes, ld, ys, 0)
        depth_sums(planes, lambda t: ld(t) * ld(t), ys, 1)

    def rows(k):
        row_sums(planes, ys, lhs, 2)
        for g in range(nf // 8):
            put_split(lhs, 2 * nf * 8 + g * 64, [desc[k, pl.ds(g * 64 + 32 + r, 8, stride=8), :] for r in range(8)])

    def product(k):
        n = 2 * nf * 8
        res[0:n] = dot(lhs[0:n], box9[...])
        res[n:n + nf * 8] = dot(lhs[n:n + nf * 8], grad[...])

    def use(k):
        for g in range(nf // 8):
            a = [desc[k, pl.ds(g * 64 + 32 + r, 8, stride=8), :] for r in range(8)]
            for r in range(8):
                at = pl.ds(g * 64 + r * 8, 8)
                mo, so, gc = [res[pl.ds(q * nf * 8 + g * 64 + r * 8, 8), :] for q in range(3)]
                inv = lax.rsqrt(VOLUME * so - mo * mo + FLOOR)
                gz = desc[k, pl.ds(g * 64 + 40 + r, 8, stride=8), :] - desc[k, pl.ds(g * 64 + 24 + r, 8, stride=8), :]
                gr = a[1] if r == 0 else -a[6] if r == 7 else a[r + 1] - a[r - 1]
                mean[k, at, :] = mo
                slope[k, at, :] = (inv * inv) * (VOLUME * a[r] - mo)
                for c, gg in enumerate((gz, gr, gc)):
                    grads[c, k, at, :] = gg * inv
    over_channels(sums, rows, product, use)


def mate_kernel(planes, count, partner, offsets, *refs):
    mates = refs[:count]
    adesc, mean, slope, grads, vel, out, box3, box9, smooth, xs, raw, tb, desc, ys, lhs, dst, res, frc = refs[count:]
    nx, nd, nf = planes + 18, planes + 16, planes + 8
    low, high = faces()
    me = lax.axis_index("brain")
    mate = partner[me]
    dr = offsets[mate, 0] - offsets[me, 0]
    dc = offsets[mate, 1] - offsets[me, 1]
    i, j = lanes()
    weights = jnp.zeros((128, 128), f32)
    for d in range(4):
        weights = jnp.where(jnp.abs(i - j) == d, TAPS[3 + d], weights)
    whi, wlo = split(weights)
    for h in (0, 128):
        box3[h:h + 128] = ones_where(jnp.abs(i - j) <= 1)
        box9[h:h + 128] = ones_where(jnp.abs(i - j) <= 4)
        smooth[h:h + 128] = whi
    smooth[256:384] = wlo
    row = lax.broadcasted_iota(jnp.int32, (8, 128), 0)

    x = mates[0][...]
    for n in range(1, count):
        x = jnp.where((me ^ mate) == n + 1, mates[n][...], x)
    for n, d in ((0, 0), (1, 1), (2, -1)):
        take = ones_where((i == j + d + dc) & (j + d >= 0) & (j + d < 128))
        raw[n, pl.ds(8, nx * 8), :] = dot(x, take)

    def prep(p, _):
        at = pl.multiple_of(p * 8, 8)
        for n, b, d in ((0, 0, 0), (1, 0, 1), (2, 0, -1), (3, 1, 0), (4, 2, 0)):
            v = raw[b, pl.ds(at + 8 + dr + d, 8), :]
            xs[n, pl.ds(at, 8), :] = jnp.where(row_inside(d) & row_inside(d + dr), v, 0.0)
        return 0
    lax.fori_loop(0, nx, prep, 0, unroll=6)
    describe(planes, xs, box3, tb, lhs, dst, desc, low, high)

    def sums(k):
        lda = lambda t: adesc[k, pl.ds(t * 8, 8), :]
        ldb = lambda t: desc[k, pl.ds(t * 8, 8), :]
        depth_sums(planes, ldb, ys, 0)
        depth_sums(planes, lambda t: ldb(t) * ldb(t), ys, 1)
        depth_sums(planes, lambda t: lda(t) * ldb(t), ys, 2)

    def rows(k):
        row_sums(planes, ys, lhs, 3)

    def product(k):
        res[0:3 * nf * 8] = dot(lhs[0:3 * nf * 8], box9[...])

    def use(k):
        for g in range(nf // 8):
            for r in range(8):
                at = pl.ds(g * 64 + r * 8, 8)
                mm, sm, sc = [res[pl.ds(q * nf * 8 + g * 64 + r * 8, 8), :] for q in range(3)]
                b = desc[k, pl.ds(g * 64 + 32 + r, 8, stride=8), :]
                inv = lax.rsqrt(VOLUME * sm - mm * mm + FLOOR)
                cov = VOLUME * sc - mean[k, at, :] * mm
                coef = (VOLUME * b - mm - cov * slope[k, at, :]) * inv
                for c in range(3):
                    frc[c, at, :] = frc[c, at, :] + coef * grads[c, k, at, :]
    frc[...] = jnp.zeros_like(frc)
    over_channels(sums, rows, product, use)

    for c in range(3):
        for g in range(nf // 8):
            for r in range(8):
                v = frc[c, pl.ds(g * 64 + r * 8, 8), :]
                if g == 0:
                    v = jnp.where(row >= 4, v, v * low)
                if g == nf // 8 - 1:
                    v = jnp.where(row < 4, v, v * high)
                ys[0, pl.ds(g * 64 + r, 8, stride=8), :] = v
        for o in range(planes):
            p = [ys[0, pl.ds((o + 1 + n) * 8, 8), :] for n in range(7)]
            v = TAPS[3] * p[3]
            for n in range(3):
                v = v + TAPS[n] * (p[n] + p[6 - n])
            ys[1, pl.ds(o * 8, 8), :] = v
        for g in range(planes // 8):
            t = [ys[1, pl.ds(g * 64 + r, 8, stride=8), :] for r in range(8)]
            w = []
            for r in range(8):
                v = TAPS[3] * t[r]
                for n in range(1, 4):
                    s = [t[q] for q in (r - n, r + n) if 0 <= q < 8]
                    v = v + TAPS[3 + n] * (s[0] + s[1] if len(s) == 2 else s[0])
                w.append(v)
            put_split(lhs, (c * planes + g * 8) * 8, w)
    n3 = 3 * planes * 8
    res[0:n3] = dot(lhs[0:n3], smooth[0:256]) + dot(lhs[0:n3, 0:128], smooth[256:384])
    for c in range(3):
        for g in range(planes // 8):
            for r in range(8):
                ys[0, pl.ds(g * 64 + r, 8, stride=8), :] = res[pl.ds((c * planes + g * 8 + r) * 8, 8), :]
        for o in range(planes):
            out[c, o] = vel[c, o] + (8.0 * VOLUME / 24.0) * ys[0, pl.ds(o * 8, 8), :]


VM = pl.BlockSpec(memory_space=pltpu.VMEM)
SM = pl.BlockSpec(memory_space=pltpu.SMEM)


def own_part(planes, own):
    nx, nd, nf = planes + 18, planes + 16, planes + 8
    shape = jax.ShapeDtypeStruct
    return pl.pallas_call(
        functools.partial(own_kernel, planes),
        out_shape=(
            shape((12, nd * 8, 128), f32),
            shape((12, nf * 8, 128), f32),
            shape((12, nf * 8, 128), f32),
            shape((3, 12, nf * 8, 128), f32),
        ),
        in_specs=[VM],
        out_specs=(VM,) * 4,
        scratch_shapes=[
            pltpu.VMEM((256, 128), bf16),
            pltpu.VMEM((256, 128), bf16),
            pltpu.VMEM((256, 128), bf16),
            pltpu.VMEM((5, nx * 8, 128), f32),
            pltpu.VMEM((12, (nd + 1) * 8, 128), f32),
            pltpu.VMEM((2, nf * 8, 128), f32),
            pltpu.VMEM((max(1536, 3 * nf * 8), 256), bf16),
            pltpu.VMEM((1536, 128), f32),
            pltpu.VMEM((3 * nf * 8, 128), f32),
        ],
        compiler_params=pltpu.CompilerParams(vmem_limit_bytes=16 * 2**20),
        cost_estimate=pl.CostEstimate(flops=6 * 10**8, bytes_accessed=16 * 2**20, transcendentals=10**6),
        name="own",
    )(own.reshape(-1, 128))


def mate_part(planes, partner, offsets, mates, owned, vel):
    nx, nd, nf = planes + 18, planes + 16, planes + 8
    count = len(mates)
    return pl.pallas_call(
        functools.partial(mate_kernel, planes, count),
        out_shape=jax.ShapeDtypeStruct(vel.shape, f32),
        in_specs=[SM, SM] + [VM] * (count + 5),
        out_specs=VM,
        scratch_shapes=[
            pltpu.VMEM((256, 128), bf16),
            pltpu.VMEM((256, 128), bf16),
            pltpu.VMEM((384, 128), bf16),
            pltpu.VMEM((5, nx * 8, 128), f32),
            pltpu.VMEM((3, nx * 8 + 16, 128), f32),
            pltpu.VMEM((12, (nd + 1) * 8, 128), f32),
            pltpu.VMEM((12, nd * 8, 128), f32),
            pltpu.VMEM((3, nf * 8, 128), f32),
            pltpu.VMEM((max(1536, 3 * nf * 8), 256), bf16),
            pltpu.VMEM((1536, 128), f32),
            pltpu.VMEM((3 * nf * 8, 128), f32),
            pltpu.VMEM((3, nf * 8, 128), f32),
        ],
        compiler_params=pltpu.CompilerParams(vmem_limit_bytes=16 * 2**20),
        name="mate",
    )(partner, offsets, *[m.reshape(-1, 128) for m in mates], *owned, vel)


def advect_kernel(planes, image, vel, warp, down, up):
    lane = lax.broadcasted_iota(jnp.int32, (8, 128), 1)

    for z in range(planes):
        x = image[0, z].astype(f32)
        before = image[0, z - 1].astype(f32) if z > 0 else x
        after = image[0, z + 1].astype(f32) if z < planes - 1 else x
        sides = (
            (before, after),
            (jnp.where(row_inside(-1), pltpu.roll(x, 1, 0), 0.0), jnp.where(row_inside(1), pltpu.roll(x, 7, 0), 0.0)),
            (jnp.where(lane >= 1, pltpu.roll(x, 1, 1), 0.0), jnp.where(lane < 127, pltpu.roll(x, 127, 1), 0.0)),
        )
        moved = 0.0
        for c, (lo, hi) in enumerate(sides):
            v = vel[0, c, z]
            moved = moved + (jnp.maximum(v, 0.0) * (x - lo) + jnp.minimum(v, 0.0) * (hi - x))
        y = x - moved
        warp[z] = y
        if z == 0 or z == planes - 1:
            ref, v = (down, jnp.maximum(vel[0, 0, z], 0.0)) if z == 0 else (up, jnp.minimum(vel[0, 0, z], 0.0))
            for n, part in enumerate(split(y) + split(v) + (image[0, z],)):
                ref[8 + n] = part
        if 1 <= z <= 8:
            down[z - 1] = y.astype(bf16)
        if planes - 9 <= z < planes - 1:
            up[z - (planes - 9)] = y.astype(bf16)


def widen_kernel(planes, warp, below, above, image, vel, out):
    low, high = faces()
    ld = lambda ref, n: ref[n].astype(f32)
    first, last = image[0, 0].astype(f32), image[0, planes - 1].astype(f32)
    top = planes - 1
    for n in range(8):
        out[n] = (ld(below, n) * low).astype(bf16)
        out[planes + 10 + n] = (ld(above, n) * high).astype(bf16)
    out[8] = (low * ((ld(below, 8) + ld(below, 9)) - (ld(below, 10) + ld(below, 11)) * (first - ld(below, 12)))).astype(bf16)
    out[planes + 9] = (high * ((ld(above, 8) + ld(above, 9)) - (ld(above, 10) + ld(above, 11)) * (ld(above, 12) - last))).astype(bf16)
    for z in range(1, top):
        out[9 + z] = warp[z].astype(bf16)
    out[9] = (warp[0] - jnp.maximum(vel[0, 0, 0], 0.0) * (first - ld(below, 12))).astype(bf16)
    out[9 + top] = (warp[top] - jnp.minimum(vel[0, 0, top], 0.0) * (ld(above, 12) - last)).astype(bf16)


def shards(intensity, velocity, partner, offsets):
    planes = intensity.shape[1]
    slabs, brains = lax.axis_size("slab"), lax.axis_size("brain")
    edge = jax.ShapeDtypeStruct((EDGE, 8, 128), bf16)
    warp, down, up = pl.pallas_call(
        functools.partial(advect_kernel, planes),
        out_shape=(jax.ShapeDtypeStruct((planes, 8, 128), f32), edge, edge),
        in_specs=[VM, VM],
        out_specs=(VM,) * 3,
        compiler_params=pltpu.CompilerParams(vmem_limit_bytes=8 * 2**20),
        name="advect",
    )(intensity, velocity)
    below = lax.ppermute(up, "slab", [(n, n + 1) for n in range(slabs - 1)])
    above = lax.ppermute(down, "slab", [(n + 1, n) for n in range(slabs - 1)])
    own = pl.pallas_call(
        functools.partial(widen_kernel, planes),
        out_shape=jax.ShapeDtypeStruct((planes + 18, 8, 128), bf16),
        in_specs=[VM] * 5,
        out_specs=VM,
        compiler_params=pltpu.CompilerParams(vmem_limit_bytes=8 * 2**20),
        name="widen",
    )(warp, below, above, intensity, velocity)
    if brains == 4:
        mates = [lax.ppermute(own, "brain", [(n, n ^ k) for n in range(4)]) for k in (1, 2, 3)]
    else:
        gathered = lax.all_gather(own, "brain")
        mates = [lax.dynamic_index_in_dim(gathered, partner[lax.axis_index("brain")], 0, keepdims=False)]
    return mate_part(planes, partner, offsets, mates, own_part(planes, own), velocity[0])[None]


def solution(mesh):
    return jax.shard_map(
        shards,
        mesh=mesh,
        in_specs=(
            P(("groups", "brain"), "slab", None, None),
            P(("groups", "brain"), None, "slab", None, None),
            P("groups"),
            P("groups", None),
        ),
        out_specs=P(("groups", "brain"), None, "slab", None, None),
        check_vma=False,
    )
```

time: 34.6 us -> 31.4 us (0.908)
  between operations: 2.62 us -> 0.08 us
  Pallas kernels: 15.1 us -> 15.9 us
  waiting for transfers between devices: 5.13 us -> 4.45 us
  local copies, waits for them, and re-layouts: 3.05 us -> 2.53 us
    ppermute x3, waiting for transfers between devices: 4.74 us -> 0.01 us  [shards(): lax.ppermute(own, 'brain', [(n, n ^ k) for n in range(4)])]
    ppermute x1, waiting for transfers between devices: 0.39 us -> 4.22 us  [shards(): above = lax.ppermute(down, 'slab', [(n + 1, n) for n in range(slabs - 1)])]
    pallas_call x1 -> x2, Pallas kernels: 14.9 us -> 15.8 us  [the longest x1 9.4 us: mate_part(): pl.pallas_call(functools.partial(mate_kernel, planes, count), out_shape=j...]
    dynamic_slice x1 -> x0, local copies, waits for them, and re-layouts: 0.61 us -> none  [shards(): mate = partner[me]]
    unnamed x12 -> x9, local copies, waits for them, and re-layouts: 2.44 us -> 2.53 us
  transfers between devices with their start and end apart: 5 -> 5, of which waited for: 3 -> 2; matrix products, arithmetic and copies ran while one was open for 3% -> 2% of each run, Pallas kernels for 0% -> 21%
where the time goes in v2:
time: 31.4 us; the launch traced here: 31.2 us
  Pallas kernels  15.9 us (51%)
  starting transfers between devices  8.14 us (26%)
  waiting for transfers between devices  4.45 us (14%)
  local copies, waits for them, and re-layouts  2.53 us (8%)
    pallas_call x1, Pallas kernels, mate_part(): pl.pallas_call(functools.partial(mate_kernel, planes, count), out_shape=j...  9.4 us
    pallas_call x1, Pallas kernels, own_part(): pl.pallas_call(functools.partial(own_kernel, planes), out_shape=(shape((1...  6.41 us
    ppermute x1, starting transfers between devices, shards(): below = lax.ppermute(up, 'slab', [(n, n + 1) for n in range(slabs - 1)])  4.93 us
    ppermute x1, waiting for transfers between devices, shards(): above = lax.ppermute(down, 'slab', [(n + 1, n) for n in range(slabs - 1)])  4.22 us
    unnamed x9, local copies, waits for them, and re-layouts  2.53 us
    ppermute x3, starting transfers between devices, shards(): lax.ppermute(own, 'brain', [(n, n ^ k) for n in range(4)])  1.92 us
    ppermute x1, starting transfers between devices, shards(): above = lax.ppermute(down, 'slab', [(n + 1, n) for n in range(slabs - 1)])  1.29 us
  transfers between devices with their start and end apart: 5, of which 2 were waited for; matrix products, arithmetic and copies ran while one was open for 2% of the time, Pallas kernels for 21%

profile of v2, /device:TPU:0, one launch (start us, length us, event | category | flops | bytes accessed | tf_op | source)
XLA Modules:
  0.0 31.2 jit_solution(3225243654994586924)
XLA Ops:
  0.0 0.0 copy-start
  0.0 1.0 %copy-done = f32[1,3,24,8,128]{4,3,2,1,0:T(8,128)S(1)} copy-done((f32[1,3,24,8,128]{4,3,2,1,0:T(8,128)S(1)}, f32[1,3,24,8,128]{4,3,2,1,0:T(8,128)}, u32[]{:S(2)}) %copy-start) | copy-done | bytes 294936
  1.0 0.0 copy-start.2
  1.0 0.8 %copy-done.2 = bf16[1,24,8,128]{3,2,1,0:T(8,128)(2,1)S(1)} copy-done((bf16[1,24,8,128]{3,2,1,0:T(8,128)(2,1)S(1)}, bf16[1,24,8,128]{3,2,1,0:T(8,128)(2,1)}, u32[]{:S(2)}) %copy-start.2) | copy-done | bytes 49176
  1.8 0.0 copy-start.1
  1.8 0.0 copy-start.3
  1.8 0.1 advect.1
  1.9 4.9 %collective-permute-start = (bf16[13,8,128]{2,1,0:T(8,128)(2,1)S(1)}, bf16[13,8,128]{2,1,0:T(8,128)(2,1)S(1)}, u32[]{:S(2)}, u32[]{:S(2)}) collective-permute-start(bf16[13,8,128]{2,1,0:T(8,128)(2,1)S(1)} %get-tuple-element.13), channel_id=1, source_target_pairs={{0,1},{1,2},{2,3},{4,5},{5,6},{6,7},{8,9},{9,10},{10,11},{12,13},{... | collective-permute-start | bytes 79880 | tf_op jit(solution)/shard_map/ppermute | solution.py:416
  6.8 1.3 %collective-permute-start.1 = (bf16[13,8,128]{2,1,0:T(8,128)(2,1)S(1)}, bf16[13,8,128]{2,1,0:T(8,128)(2,1)S(1)}, u32[]{:S(2)}, u32[]{:S(2)}) collective-permute-start(bf16[13,8,128]{2,1,0:T(8,128)(2,1)S(1)} %get-tuple-element.14), channel_id=1, source_target_pairs={{1,0},{2,1},{3,2},{5,4},{6,5},{7,6},{9,8},{10,9},{11,10},{13,12},{... | collective-permute-start | bytes 79880 | tf_op jit(solution)/shard_map/ppermute | solution.py:417
  8.1 0.2 collective-permute-done.below
  8.4 4.2 %collective-permute-done.1.above = bf16[13,8,128]{2,1,0:T(8,128)(2,1)S(1)} collective-permute-done((bf16[13,8,128]{2,1,0:T(8,128)(2,1)S(1)}, bf16[13,8,128]{2,1,0:T(8,128)(2,1)S(1)}, u32[]{:S(2)}, u32[]{:S(2)}) %collective-permute-start.1) | collective-permute-done | bytes 26656 | tf_op jit(solution)/shard_map/ppermute | solution.py:417
  12.6 0.1 collective-permute-start.4
  12.7 1.6 %collective-permute-start.3 = (bf16[42,8,128]{2,1,0:T(8,128)(2,1)S(1)}, bf16[42,8,128]{2,1,0:T(8,128)(2,1)S(1)}, u32[]{:S(2)}, u32[]{:S(2)}) collective-permute-start(bf16[42,8,128]{2,1,0:T(8,128)(2,1)S(1)} %widen.1), channel_id=1, source_target_pairs={{0,8},{4,12},{8,0},{12,4},{1,9},{5,13},{9,1},{13,5},{2,10},{6,14},... | collective-permute-start | bytes 258056 | tf_op jit(solution)/shard_map/ppermute | solution.py:427
  14.2 0.3 collective-permute-start.2
  14.5 0.8 %copy.5.offsets = s32[4,2]{1,0:T(4,128)S(1)} copy(s32[4,2]{0,1:T(2,128)} %param.7) | data formatting | bytes 64 | tf_op args[3]
  15.3 6.4 %own.1 = (f32[12,320,128]{2,1,0:T(8,128)S(1)}, f32[12,256,128]{2,1,0:T(8,128)S(1)}, f32[12,256,128]{2,1,0:T(8,128)S(1)}, f32[3,12,256,128]{3,2,1,0:T(8,128)S(1)}) custom-call(bf16[336,128]{1,0:T(8,128)(2,1)S(1)} %bitcast.7), custom_call_target="tpu_custom_call" | custom-call | flops 600000000 | bytes 16777216 | tf_op jit(solution)/shard_map/own/pallas_call | solution.py:306
  21.7 0.0 collective-permute-done.4
  21.7 0.0 collective-permute-done.3
  21.7 0.0 collective-permute-done.2
  21.7 0.0 copy-done.1
  21.7 0.0 copy-done.3
  21.8 9.4 %mate.1 = f32[3,24,8,128]{3,2,1,0:T(8,128)} custom-call(s32[4]{0:T(128)S(1)} %copy-done.3, s32[4,2]{1,0:T(4,128)S(1)} %copy.5.offsets, bf16[336,128]{1,0:T(8,128)(2,1)S(1)} %bitcast.10, bf16[336,128]{1,0:T(8,128)(2,1)S(1)} %bitcast.9, bf16[336,128]{1,0:T(8,128)(2,1)S(1)} %bitcast.8, f32[12,320,128]{2,1,0:T(8,128)S(1)} %get-tuple-element.15.refs_3_, ...), custom_call_target="tpu_custom_call" | custom-call | tf_op jit(solution)/shard_map/mate/pallas_call | solution.py:336
  (1 shorter events, 0.0 us)
Async XLA Ops:
  0.0 1.0 %copy-start = (f32[1,3,24,8,128]{4,3,2,1,0:T(8,128)S(1)}, f32[1,3,24,8,128]{4,3,2,1,0:T(8,128)}, u32[]{:S(2)}) copy-start(f32[1,3,24,8,128]{4,3,2,1,0:T(8,128)} %vel.3) | copy-start | bytes 884740
  1.0 0.8 %copy-start.2 = (bf16[1,24,8,128]{3,2,1,0:T(8,128)(2,1)S(1)}, bf16[1,24,8,128]{3,2,1,0:T(8,128)(2,1)}, u32[]{:S(2)}) copy-start(bf16[1,24,8,128]{3,2,1,0:T(8,128)(2,1)} %image.3) | copy-start | bytes 147460
  1.8 20.0 %copy-start.1 = (f32[1,3,24,8,128]{4,3,2,1,0:T(8,128)S(1)}, f32[1,3,24,8,128]{4,3,2,1,0:T(8,128)}, u32[]{:S(2)}) copy-start(f32[1,3,24,8,128]{4,3,2,1,0:T(8,128)} %vel.3) | copy-start | bytes 884740
  1.8 20.0 %copy-start.3 = (s32[4]{0:T(128)S(1)}, s32[4]{0:T(128)}, u32[]{:S(2)}) copy-start(s32[4]{0:T(128)} %partner.1) | copy-start | bytes 52
  1.9 6.5 %collective-permute-start = (bf16[13,8,128]{2,1,0:T(8,128)(2,1)S(1)}, bf16[13,8,128]{2,1,0:T(8,128)(2,1)S(1)}, u32[]{:S(2)}, u32[]{:S(2)}) collective-permute-start(bf16[13,8,128]{2,1,0:T(8,128)(2,1)S(1)} %get-tuple-element.13), channel_id=1, source_target_pairs={{0,1},{1,2},{2,3},{4,5},{5,6},{6,7},{8,9},{9,10},{10,11},{12,13},{... | collective-permute-start | bytes 79880 | tf_op jit(solution)/shard_map/ppermute | solution.py:416
  6.8 5.7 %collective-permute-start.1 = (bf16[13,8,128]{2,1,0:T(8,128)(2,1)S(1)}, bf16[13,8,128]{2,1,0:T(8,128)(2,1)S(1)}, u32[]{:S(2)}, u32[]{:S(2)}) collective-permute-start(bf16[13,8,128]{2,1,0:T(8,128)(2,1)S(1)} %get-tuple-element.14), channel_id=1, source_target_pairs={{1,0},{2,1},{3,2},{5,4},{6,5},{7,6},{9,8},{10,9},{11,10},{13,12},{... | collective-permute-start | bytes 79880 | tf_op jit(solution)/shard_map/ppermute | solution.py:417
  12.6 9.1 %collective-permute-start.4 = (bf16[42,8,128]{2,1,0:T(8,128)(2,1)S(1)}, bf16[42,8,128]{2,1,0:T(8,128)(2,1)S(1)}, u32[]{:S(2)}, u32[]{:S(2)}) collective-permute-start(bf16[42,8,128]{2,1,0:T(8,128)(2,1)S(1)} %widen.1), channel_id=1, source_target_pairs={{0,12},{4,8},{8,4},{12,0},{1,13},{5,9},{9,5},{13,1},{2,14},{6,10},... | collective-permute-start | bytes 258056 | tf_op jit(solution)/shard_map/ppermute | solution.py:427
  12.7 9.0 %collective-permute-start.3 = (bf16[42,8,128]{2,1,0:T(8,128)(2,1)S(1)}, bf16[42,8,128]{2,1,0:T(8,128)(2,1)S(1)}, u32[]{:S(2)}, u32[]{:S(2)}) collective-permute-start(bf16[42,8,128]{2,1,0:T(8,128)(2,1)S(1)} %widen.1), channel_id=1, source_target_pairs={{0,8},{4,12},{8,0},{12,4},{1,9},{5,13},{9,1},{13,5},{2,10},{6,14},... | collective-permute-start | bytes 258056 | tf_op jit(solution)/shard_map/ppermute | solution.py:427
  14.2 7.5 %collective-permute-start.2 = (bf16[42,8,128]{2,1,0:T(8,128)(2,1)S(1)}, bf16[42,8,128]{2,1,0:T(8,128)(2,1)S(1)}, u32[]{:S(2)}, u32[]{:S(2)}) collective-permute-start(bf16[42,8,128]{2,1,0:T(8,128)(2,1)S(1)} %widen.1), channel_id=1, source_target_pairs={{0,4},{4,0},{8,12},{12,8},{1,5},{5,1},{9,13},{13,9},{2,6},{6,2},{1... | collective-permute-start | bytes 258056 | tf_op jit(solution)/shard_map/ppermute | solution.py:427

commit v3 on v2

--- a/solution.py
+++ b/solution.py
@@ -11,6 +11,7 @@
 LOG2E = 1.4426950408889634
 EDGE = 13
 VOLUME = 729.0
+UNROLL = 2
 FLOOR = 1e-5 * VOLUME * VOLUME
 
 
@@ -27,11 +28,8 @@
     return jnp.where(cond, 1.0, 0.0).astype(bf16)
 
 
-def put_split(lhs, start, parts):
-    hi, lo = split(jnp.concatenate(parts, axis=0))
-    at = pl.ds(start, 8 * len(parts))
-    lhs[at, 0:128] = hi
-    lhs[at, 128:256] = lo
+def halves(parts):
+    return jnp.concatenate(split(jnp.concatenate(parts, axis=0)), axis=1)
 
 
 def dot(a, b):
@@ -50,7 +48,7 @@
     return (row + d >= 0) & (row + d < 8)
 
 
-def describe(planes, xs, box3, tb, lhs, dst, desc, low, high):
+def describe(planes, xs, box3, tb, desc, low, high):
     nd = planes + 16
     ng = nd // 8
 
@@ -75,21 +73,15 @@
     for k in range(12):
         tb[k, pl.ds(nd * 8, 8), :] = c2[k]
 
-    def rows(g):
-        for k in range(12):
-            t = [tb[k, pl.ds(g * 64 + 8 + r, 8, stride=8), :] for r in range(8)]
-            p = [t[r] + t[r + 1] for r in range(7)]
-            w = [p[0]] + [p[r - 1] + t[r + 1] for r in range(1, 7)] + [p[6]]
-            put_split(lhs, (g % 2) * 768 + k * 64, w)
-
-    rows(0)
     for g in range(ng):
-        h = g % 2
-        if g + 1 < ng:
-            rows(g + 1)
-        dst[h * 768:h * 768 + 768] = dot(lhs[h * 768:h * 768 + 768], box3[...])
+        parts = []
         for r in range(8):
-            v = [dst[pl.ds(h * 768 + k * 64 + r * 8, 8), :] for k in range(12)]
+            for k in range(12):
+                t = [tb[k, pl.ds(g * 64 + 8 + n, 8, stride=8), :] for n in (r - 1, r, r + 1) if 0 <= n < 8]
+                parts.append(functools.reduce(jnp.add, t))
+        box = dot(halves(parts), box3[...])
+        for r in range(8):
+            v = [box[(r * 12 + k) * 8:(r * 12 + k) * 8 + 8] for k in range(12)]
             total = functools.reduce(jnp.add, v)
             inv = (-LOG2E / 27.0) / (total * (1.0 / 324.0) + 0.1)
             for k in range(12):
@@ -104,47 +96,27 @@
 def depth_sums(planes, value, ys, q):
     nd, nf = planes + 16, planes + 8
     d = [value(t) for t in range(nd)]
-    s2 = [d[t] + d[t + 1] for t in range(nd - 1)]
-    s4 = [s2[t] + s2[t + 2] for t in range(nd - 3)]
     for f in range(nf):
-        ys[q, pl.ds(f * 8, 8), :] = s4[f] + s4[f + 4] + d[f + 8]
-
-
-def row_sums(planes, ys, lhs, count):
-    nf = planes + 8
-    for g in range(nf // 8):
-        for q in range(count):
-            t = [ys[q, pl.ds(g * 64 + r, 8, stride=8), :] for r in range(8)]
-            lo = (t[0] + t[1]) + (t[2] + t[3])
-            hi = (t[4] + t[5]) + (t[6] + t[7])
-            w = [None] * 8
-            w[0] = lo + t[4]
-            w[1] = w[0] + t[5]
-            w[2] = w[1] + t[6]
-            w[3] = lo + hi
-            w[4] = w[3]
-            w[7] = hi + t[3]
-            w[6] = w[7] + t[2]
-            w[5] = w[6] + t[1]
-            put_split(lhs, q * nf * 8 + g * 64, w)
-
-
-def over_channels(sums, rows, product, use):
-    sums(0)
-    rows(0)
-
-    def step(k, _):
-        product(k)
-        sums(k + 1)
-        use(k)
-        rows(k + 1)
-        return 0
-    lax.fori_loop(0, 11, step, 0)
-    product(11)
-    use(11)
-
-
-def own_kernel(planes, own, desc, mean, slope, grads, box3, box9, grad, xs, tb, ys, lhs, dst, res):
+        if f % 16 == 0:
+            s2 = [d[f + t] + d[f + t + 1] for t in (0, 2, 4, 6)]
+            total = ((s2[0] + s2[1]) + (s2[2] + s2[3])) + d[f + 8]
+        else:
+            total = (total - d[f - 1]) + d[f + 8]
+        ys[q, pl.ds(f * 8, 8), :] = total
+
+
+def row_sums(ys, q, g):
+    t = [ys[q, pl.ds(g * 64 + r, 8, stride=8), :] for r in range(8)]
+    lo = (t[0] + t[1]) + (t[2] + t[3])
+    hi = (t[4] + t[5]) + (t[6] + t[7])
+    w0 = lo + t[4]
+    w1 = w0 + t[5]
+    w7 = hi + t[3]
+    w6 = w7 + t[2]
+    return [w0, w1, w1 + t[6], lo + hi, lo + hi, w6 + t[1], w6, w7]
+
+
+def own_kernel(planes, own, desc, mean, slope, grads, box3, box9, grad, xs, tb, ys):
     nx, nd, nf = planes + 18, planes + 16, planes + 8
     low, high = faces()
     i, j = lanes()
@@ -164,29 +136,30 @@
         xs[2, at, :] = jnp.where(row_inside(-1), pltpu.roll(v, 1, 0), 0.0)
         return 0
     lax.fori_loop(0, nx, prep, 0, unroll=6)
-    describe(planes, xs, box3, tb, lhs, dst, desc, low, high)
-
-    def sums(k):
+    describe(planes, xs, box3, tb, desc, low, high)
+
+    def channels(k, _):
+        for h in range(UNROLL):
+            one_channel(UNROLL * k + h, h)
+        return 0
+
+    def one_channel(k, h):
         ld = lambda t: desc[k, pl.ds(t * 8, 8), :]
-        depth_sums(planes, ld, ys, 0)
-        depth_sums(planes, lambda t: ld(t) * ld(t), ys, 1)
-
-    def rows(k):
-        row_sums(planes, ys, lhs, 2)
+        depth_sums(planes, ld, ys, 2 * h)
+        depth_sums(planes, lambda t: ld(t) * ld(t), ys, 2 * h + 1)
+        parts, centre = [], []
         for g in range(nf // 8):
-            put_split(lhs, 2 * nf * 8 + g * 64, [desc[k, pl.ds(g * 64 + 32 + r, 8, stride=8), :] for r in range(8)])
-
-    def product(k):
-        n = 2 * nf * 8
-        res[0:n] = dot(lhs[0:n], box9[...])
-        res[n:n + nf * 8] = dot(lhs[n:n + nf * 8], grad[...])
-
-    def use(k):
+            for q in range(2):
+                parts += row_sums(ys, 2 * h + q, g)
+            centre += [desc[k, pl.ds(g * 64 + 32 + r, 8, stride=8), :] for r in range(8)]
+        sums = dot(halves(parts), box9[...])
+        across = dot(halves(centre), grad[...])
         for g in range(nf // 8):
-            a = [desc[k, pl.ds(g * 64 + 32 + r, 8, stride=8), :] for r in range(8)]
+            a = centre[g * 8:g * 8 + 8]
             for r in range(8):
                 at = pl.ds(g * 64 + r * 8, 8)
-                mo, so, gc = [res[pl.ds(q * nf * 8 + g * 64 + r * 8, 8), :] for q in range(3)]
+                mo, so = [sums[(g * 16 + q * 8 + r) * 8:(g * 16 + q * 8 + r) * 8 + 8] for q in range(2)]
+                gc = across[(g * 8 + r) * 8:(g * 8 + r) * 8 + 8]
                 inv = lax.rsqrt(VOLUME * so - mo * mo + FLOOR)
                 gz = desc[k, pl.ds(g * 64 + 40 + r, 8, stride=8), :] - desc[k, pl.ds(g * 64 + 24 + r, 8, stride=8), :]
                 gr = a[1] if r == 0 else -a[6] if r == 7 else a[r + 1] - a[r - 1]
@@ -194,18 +167,18 @@
                 slope[k, at, :] = (inv * inv) * (VOLUME * a[r] - mo)
                 for c, gg in enumerate((gz, gr, gc)):
                     grads[c, k, at, :] = gg * inv
-    over_channels(sums, rows, product, use)
+    lax.fori_loop(0, 12 // UNROLL, channels, 0)
 
 
 def mate_kernel(planes, count, partner, offsets, *refs):
     mates = refs[:count]
-    adesc, mean, slope, grads, vel, out, box3, box9, smooth, xs, raw, tb, desc, ys, lhs, dst, res, frc = refs[count:]
+    adesc, mean, slope, grads, vel, out, box3, box9, smooth, xs, raw, tb, desc, ys, frc = refs[count:]
     nx, nd, nf = planes + 18, planes + 16, planes + 8
     low, high = faces()
     me = lax.axis_index("brain")
     mate = partner[me]
-    dr = offsets[mate, 0] - offsets[me, 0]
-    dc = offsets[mate, 1] - offsets[me, 1]
+    dr = offsets[0, mate] - offsets[0, me]
+    dc = offsets[1, mate] - offsets[1, me]
     i, j = lanes()
     weights = jnp.zeros((128, 128), f32)
     for d in range(4):
@@ -232,26 +205,28 @@
             xs[n, pl.ds(at, 8), :] = jnp.where(row_inside(d) & row_inside(d + dr), v, 0.0)
         return 0
     lax.fori_loop(0, nx, prep, 0, unroll=6)
-    describe(planes, xs, box3, tb, lhs, dst, desc, low, high)
-
-    def sums(k):
+    describe(planes, xs, box3, tb, desc, low, high)
+
+    def channels(k, _):
+        for h in range(UNROLL):
+            one_channel(UNROLL * k + h, h)
+        return 0
+
+    def one_channel(k, h):
         lda = lambda t: adesc[k, pl.ds(t * 8, 8), :]
         ldb = lambda t: desc[k, pl.ds(t * 8, 8), :]
-        depth_sums(planes, ldb, ys, 0)
-        depth_sums(planes, lambda t: ldb(t) * ldb(t), ys, 1)
-        depth_sums(planes, lambda t: lda(t) * ldb(t), ys, 2)
-
-    def rows(k):
-        row_sums(planes, ys, lhs, 3)
-
-    def product(k):
-        res[0:3 * nf * 8] = dot(lhs[0:3 * nf * 8], box9[...])
-
-    def use(k):
+        depth_sums(planes, ldb, ys, 3 * h)
+        depth_sums(planes, lambda t: ldb(t) * ldb(t), ys, 3 * h + 1)
+        depth_sums(planes, lambda t: lda(t) * ldb(t), ys, 3 * h + 2)
+        parts = []
+        for g in range(nf // 8):
+            for q in range(3):
+                parts += row_sums(ys, 3 * h + q, g)
+        sums = dot(halves(parts), box9[...])
         for g in range(nf // 8):
             for r in range(8):
                 at = pl.ds(g * 64 + r * 8, 8)
-                mm, sm, sc = [res[pl.ds(q * nf * 8 + g * 64 + r * 8, 8), :] for q in range(3)]
+                mm, sm, sc = [sums[(g * 24 + q * 8 + r) * 8:(g * 24 + q * 8 + r) * 8 + 8] for q in range(3)]
                 b = desc[k, pl.ds(g * 64 + 32 + r, 8, stride=8), :]
                 inv = lax.rsqrt(VOLUME * sm - mm * mm + FLOOR)
                 cov = VOLUME * sc - mean[k, at, :] * mm
@@ -259,8 +234,9 @@
                 for c in range(3):
                     frc[c, at, :] = frc[c, at, :] + coef * grads[c, k, at, :]
     frc[...] = jnp.zeros_like(frc)
-    over_channels(sums, rows, product, use)
-
+    lax.fori_loop(0, 12 // UNROLL, channels, 0)
+
+    parts = []
     for c in range(3):
         for g in range(nf // 8):
             for r in range(8):
@@ -278,20 +254,19 @@
             ys[1, pl.ds(o * 8, 8), :] = v
         for g in range(planes // 8):
             t = [ys[1, pl.ds(g * 64 + r, 8, stride=8), :] for r in range(8)]
-            w = []
             for r in range(8):
                 v = TAPS[3] * t[r]
                 for n in range(1, 4):
                     s = [t[q] for q in (r - n, r + n) if 0 <= q < 8]
                     v = v + TAPS[3 + n] * (s[0] + s[1] if len(s) == 2 else s[0])
-                w.append(v)
-            put_split(lhs, (c * planes + g * 8) * 8, w)
-    n3 = 3 * planes * 8
-    res[0:n3] = dot(lhs[0:n3], smooth[0:256]) + dot(lhs[0:n3, 0:128], smooth[256:384])
+                parts.append(v)
+    both = halves(parts)
+    res = dot(both, smooth[0:256]) + dot(both[:, 0:128], smooth[256:384])
     for c in range(3):
         for g in range(planes // 8):
             for r in range(8):
-                ys[0, pl.ds(g * 64 + r, 8, stride=8), :] = res[pl.ds((c * planes + g * 8 + r) * 8, 8), :]
+                n = ((c * planes + g * 8) + r) * 8
+                ys[0, pl.ds(g * 64 + r, 8, stride=8), :] = res[n:n + 8]
         for o in range(planes):
             out[c, o] = vel[c, o] + (8.0 * VOLUME / 24.0) * ys[0, pl.ds(o * 8, 8), :]
 
@@ -319,10 +294,7 @@
             pltpu.VMEM((256, 128), bf16),
             pltpu.VMEM((5, nx * 8, 128), f32),
             pltpu.VMEM((12, (nd + 1) * 8, 128), f32),
-            pltpu.VMEM((2, nf * 8, 128), f32),
-            pltpu.VMEM((max(1536, 3 * nf * 8), 256), bf16),
-            pltpu.VMEM((1536, 128), f32),
-            pltpu.VMEM((3 * nf * 8, 128), f32),
+            pltpu.VMEM((2 * UNROLL, nf * 8, 128), f32),
         ],
         compiler_params=pltpu.CompilerParams(vmem_limit_bytes=16 * 2**20),
         cost_estimate=pl.CostEstimate(flops=6 * 10**8, bytes_accessed=16 * 2**20, transcendentals=10**6),
@@ -346,18 +318,23 @@
             pltpu.VMEM((3, nx * 8 + 16, 128), f32),
             pltpu.VMEM((12, (nd + 1) * 8, 128), f32),
             pltpu.VMEM((12, nd * 8, 128), f32),
-            pltpu.VMEM((3, nf * 8, 128), f32),
-            pltpu.VMEM((max(1536, 3 * nf * 8), 256), bf16),
-            pltpu.VMEM((1536, 128), f32),
-            pltpu.VMEM((3 * nf * 8, 128), f32),
+            pltpu.VMEM((3 * UNROLL, nf * 8, 128), f32),
             pltpu.VMEM((3, nf * 8, 128), f32),
         ],
         compiler_params=pltpu.CompilerParams(vmem_limit_bytes=16 * 2**20),
         name="mate",
-    )(partner, offsets, *[m.reshape(-1, 128) for m in mates], *owned, vel)
-
-
-def advect_kernel(planes, image, vel, warp, down, up):
+    )(partner, offsets.T, *[m.reshape(-1, 128) for m in mates], *owned, vel)
+
+
+def advect_kernel(planes, image_hbm, vel_hbm, warp, first, second, image, vel, down, up, sems):
+    copies = [
+        pltpu.make_async_copy(vel_hbm, vel, sems.at[0]),
+        pltpu.make_async_copy(image_hbm, image, sems.at[1]),
+    ]
+    for copy in copies:
+        copy.start()
+    for copy in copies:
+        copy.wait()
     lane = lax.broadcasted_iota(jnp.int32, (8, 128), 1)
 
     for z in range(planes):
@@ -376,20 +353,27 @@
         y = x - moved
         warp[z] = y
         if z == 0 or z == planes - 1:
-            ref, v = (down, jnp.maximum(vel[0, 0, z], 0.0)) if z == 0 else (up, jnp.minimum(vel[0, 0, z], 0.0))
-            for n, part in enumerate(split(y) + split(v) + (image[0, z],)):
-                ref[8 + n] = part
+            v = jnp.maximum(vel[0, 0, z], 0.0) if z == 0 else jnp.minimum(vel[0, 0, z], 0.0)
+            edge = split(y) + split(v) + (image[0, z],)
+            for n, part in enumerate(edge):
+                (down if z == 0 else up)[8 + n] = part
         if 1 <= z <= 8:
             down[z - 1] = y.astype(bf16)
         if planes - 9 <= z < planes - 1:
             up[z - (planes - 9)] = y.astype(bf16)
-
-
-def widen_kernel(planes, warp, below, above, image, vel, out):
+    even = lax.rem(lax.axis_index("slab"), 2) == 0
+    for n in range(EDGE):
+        first[n] = jnp.where(even, up[n], down[n])
+        second[n] = jnp.where(even, down[n], up[n])
+
+
+def widen_kernel(planes, warp, sent1, sent2, got1, got2, out):
     low, high = faces()
-    ld = lambda ref, n: ref[n].astype(f32)
-    first, last = image[0, 0].astype(f32), image[0, planes - 1].astype(f32)
+    even = lax.rem(lax.axis_index("slab"), 2) == 0
+    down, up, below, above = (sent2, sent1), (sent1, sent2), (got2, got1), (got1, got2)
+    ld = lambda pair, n: jnp.where(even, pair[0][n], pair[1][n]).astype(f32)
     top = planes - 1
+    first, last = ld(down, 12), ld(up, 12)
     for n in range(8):
         out[n] = (ld(below, n) * low).astype(bf16)
         out[planes + 10 + n] = (ld(above, n) * high).astype(bf16)
@@ -397,24 +381,34 @@
     out[planes + 9] = (high * ((ld(above, 8) + ld(above, 9)) - (ld(above, 10) + ld(above, 11)) * (ld(above, 12) - last))).astype(bf16)
     for z in range(1, top):
         out[9 + z] = warp[z].astype(bf16)
-    out[9] = (warp[0] - jnp.maximum(vel[0, 0, 0], 0.0) * (first - ld(below, 12))).astype(bf16)
-    out[9 + top] = (warp[top] - jnp.minimum(vel[0, 0, top], 0.0) * (ld(above, 12) - last)).astype(bf16)
+    out[9] = (warp[0] - (ld(down, 10) + ld(down, 11)) * (first - ld(below, 12))).astype(bf16)
+    out[9 + top] = (warp[top] - (ld(up, 10) + ld(up, 11)) * (ld(above, 12) - last)).astype(bf16)
 
 
 def shards(intensity, velocity, partner, offsets):
     planes = intensity.shape[1]
     slabs, brains = lax.axis_size("slab"), lax.axis_size("brain")
     edge = jax.ShapeDtypeStruct((EDGE, 8, 128), bf16)
-    warp, down, up = pl.pallas_call(
+    warp, first, second = pl.pallas_call(
         functools.partial(advect_kernel, planes),
         out_shape=(jax.ShapeDtypeStruct((planes, 8, 128), f32), edge, edge),
-        in_specs=[VM, VM],
+        in_specs=[pl.BlockSpec(memory_space=pltpu.HBM)] * 2,
         out_specs=(VM,) * 3,
+        scratch_shapes=[
+            pltpu.VMEM(intensity.shape, bf16),
+            pltpu.VMEM(velocity.shape, f32),
+            pltpu.VMEM(edge.shape, bf16),
+            pltpu.VMEM(edge.shape, bf16),
+            pltpu.SemaphoreType.DMA((2,)),
+        ],
         compiler_params=pltpu.CompilerParams(vmem_limit_bytes=8 * 2**20),
         name="advect",
     )(intensity, velocity)
-    below = lax.ppermute(up, "slab", [(n, n + 1) for n in range(slabs - 1)])
-    above = lax.ppermute(down, "slab", [(n + 1, n) for n in range(slabs - 1)])
+    odd_pairs = [(n, n + 1) for n in range(1, slabs - 1, 2)]
+    even_pairs = [(n, n + 1) for n in range(0, slabs - 1, 2)]
+    both_ways = lambda pairs: pairs + [(b, a) for a, b in pairs]
+    from_odd = lax.ppermute(second, "slab", both_ways(odd_pairs))
+    from_even = lax.ppermute(first, "slab", both_ways(even_pairs))
     own = pl.pallas_call(
         functools.partial(widen_kernel, planes),
         out_shape=jax.ShapeDtypeStruct((planes + 18, 8, 128), bf16),
@@ -422,7 +416,7 @@
         out_specs=VM,
         compiler_params=pltpu.CompilerParams(vmem_limit_bytes=8 * 2**20),
         name="widen",
-    )(warp, below, above, intensity, velocity)
+    )(warp, first, second, from_even, from_odd)
     if brains == 4:
         mates = [lax.ppermute(own, "brain", [(n, n ^ k) for n in range(4)]) for k in (1, 2, 3)]
     else:

time: 31.4 us -> 24.2 us (0.77)
  the two profiles are of different devices: /device:TPU:0 before, /device:TPU:17 now
where the time goes in v3:
time: 24.2 us; the launch traced here: 24 us
  Pallas kernels  12.4 us (51%)
  starting transfers between devices  7.01 us (29%)
  waiting for transfers between devices  2.72 us (11%)
  local copies, waits for them, and re-layouts  1.77 us (7%)
    pallas_call x1, Pallas kernels, mate_part(): pl.pallas_call(functools.partial(mate_kernel, planes, count), out_shape=j...  7.52 us
    pallas_call x1, Pallas kernels, own_part(): pl.pallas_call(functools.partial(own_kernel, planes), out_shape=(shape((1...  4.58 us
    ppermute x3, starting transfers between devices, shards(): lax.ppermute(own, 'brain', [(n, n ^ k) for n in range(4)])  3.74 us
    ppermute x1, waiting for transfers between devices, shards(): from_odd = lax.ppermute(second, 'slab', both_ways(odd_pairs))  2.65 us
    ppermute x1, starting transfers between devices, shards(): from_odd = lax.ppermute(second, 'slab', both_ways(odd_pairs))  1.91 us
    unnamed x10, local copies, waits for them, and re-layouts  1.77 us
    ppermute x1, starting transfers between devices, shards(): from_even = lax.ppermute(first, 'slab', both_ways(even_pairs))  1.36 us
  transfers between devices with their start and end apart: 5, of which 2 were waited for; matrix products, arithmetic and copies ran while one was open for 0% of the time, Pallas kernels for 19%

profile of v3, /device:TPU:17, one launch (start us, length us, event | category | flops | bytes accessed | tf_op | source)
XLA Modules:
  0.0 24.0 jit_solution(4784413777946161261)
XLA Ops:
  0.0 0.0 copy-start
  0.0 1.0 %copy-done = f32[1,3,24,8,128]{4,3,2,1,0:T(8,128)S(1)} copy-done((f32[1,3,24,8,128]{4,3,2,1,0:T(8,128)S(1)}, f32[1,3,24,8,128]{4,3,2,1,0:T(8,128)}, u32[]{:S(2)}) %copy-start) | copy-done | bytes 294936
  1.0 0.0 copy-start.2
  1.0 0.8 %copy-done.2 = bf16[1,24,8,128]{3,2,1,0:T(8,128)(2,1)S(1)} copy-done((bf16[1,24,8,128]{3,2,1,0:T(8,128)(2,1)S(1)}, bf16[1,24,8,128]{3,2,1,0:T(8,128)(2,1)}, u32[]{:S(2)}) %copy-start.2) | copy-done | bytes 49176
  1.8 0.0 copy-start.1
  1.8 0.0 copy-start.3
  1.8 0.0 copy-start.4
  1.8 0.3 %advect.1 = (f32[24,8,128]{2,1,0:T(8,128)S(1)}, bf16[13,8,128]{2,1,0:T(8,128)(2,1)S(1)}, bf16[13,8,128]{2,1,0:T(8,128)(2,1)S(1)}) custom-call(bf16[1,24,8,128]{3,2,1,0:T(8,128)(2,1)S(1)} %copy-done.2, f32[1,3,24,8,128]{4,3,2,1,0:T(8,128)S(1)} %copy-done), custom_call_target="tpu_custom_call" | custom-call | tf_op jit(solution)/shard_map/advect/pallas_call | solution.py:392
  2.0 1.4 %collective-permute-start = (bf16[13,8,128]{2,1,0:T(8,128)(2,1)S(1)}, bf16[13,8,128]{2,1,0:T(8,128)(2,1)S(1)}, u32[]{:S(2)}, u32[]{:S(2)}) collective-permute-start(bf16[13,8,128]{2,1,0:T(8,128)(2,1)S(1)} %get-tuple-element.13.sent1), channel_id=1, source_target_pairs={{0,1},{2,3},{1,0},{3,2},{4,5},{6,7},{5,4},{7,6},{8,9},{10,11},{9,8... | collective-permute-start | bytes 79880 | tf_op jit(solution)/shard_map/ppermute | solution.py:411
  3.4 1.9 %collective-permute-start.1 = (bf16[13,8,128]{2,1,0:T(8,128)(2,1)S(1)}, bf16[13,8,128]{2,1,0:T(8,128)(2,1)S(1)}, u32[]{:S(2)}, u32[]{:S(2)}) collective-permute-start(bf16[13,8,128]{2,1,0:T(8,128)(2,1)S(1)} %get-tuple-element.14.sent2), channel_id=1, source_target_pairs={{1,2},{2,1},{5,6},{6,5},{9,10},{10,9},{13,14},{14,13},{17,18},{18,... | collective-permute-start | bytes 79880 | tf_op jit(solution)/shard_map/ppermute | solution.py:410
  5.3 0.0 collective-permute-done.got1
  5.3 2.7 %collective-permute-done.1.got2 = bf16[13,8,128]{2,1,0:T(8,128)(2,1)S(1)} collective-permute-done((bf16[13,8,128]{2,1,0:T(8,128)(2,1)S(1)}, bf16[13,8,128]{2,1,0:T(8,128)(2,1)S(1)}, u32[]{:S(2)}, u32[]{:S(2)}) %collective-permute-start.1) | collective-permute-done | bytes 26656 | tf_op jit(solution)/shard_map/ppermute | solution.py:410
  8.0 3.3 %collective-permute-start.4 = (bf16[42,8,128]{2,1,0:T(8,128)(2,1)S(1)}, bf16[42,8,128]{2,1,0:T(8,128)(2,1)S(1)}, u32[]{:S(2)}, u32[]{:S(2)}) collective-permute-start(bf16[42,8,128]{2,1,0:T(8,128)(2,1)S(1)} %widen.1), channel_id=1, source_target_pairs={{0,12},{4,8},{8,4},{12,0},{1,13},{5,9},{9,5},{13,1},{2,14},{6,10},... | collective-permute-start | bytes 258056 | tf_op jit(solution)/shard_map/ppermute | solution.py:421
  11.3 0.3 %collective-permute-start.3 = (bf16[42,8,128]{2,1,0:T(8,128)(2,1)S(1)}, bf16[42,8,128]{2,1,0:T(8,128)(2,1)S(1)}, u32[]{:S(2)}, u32[]{:S(2)}) collective-permute-start(bf16[42,8,128]{2,1,0:T(8,128)(2,1)S(1)} %widen.1), channel_id=1, source_target_pairs={{0,8},{4,12},{8,0},{12,4},{1,9},{5,13},{9,1},{13,5},{2,10},{6,14},... | collective-permute-start | bytes 258056 | tf_op jit(solution)/shard_map/ppermute | solution.py:421
  11.6 0.2 collective-permute-start.2
  11.8 4.6 %own.1 = (f32[12,320,128]{2,1,0:T(8,128)S(1)}, f32[12,256,128]{2,1,0:T(8,128)S(1)}, f32[12,256,128]{2,1,0:T(8,128)S(1)}, f32[3,12,256,128]{3,2,1,0:T(8,128)S(1)}) custom-call(bf16[336,128]{1,0:T(8,128)(2,1)S(1)} %bitcast.8), custom_call_target="tpu_custom_call" | custom-call | flops 600000000 | bytes 16777216 | tf_op jit(solution)/shard_map/own/pallas_call | solution.py:281
  16.4 0.0 collective-permute-done.4
  16.4 0.1 collective-permute-done.3
  16.4 0.0 collective-permute-done.2
  16.4 0.0 copy-done.1
  16.4 0.0 copy-done.3
  16.4 0.0 copy-done.4
  16.5 7.5 %mate.1 = f32[3,24,8,128]{3,2,1,0:T(8,128)} custom-call(s32[4]{0:T(128)S(1)} %copy-done.4, s32[2,4]{1,0:T(2,128)S(1)} %bitcast.12, bf16[336,128]{1,0:T(8,128)(2,1)S(1)} %bitcast.11, bf16[336,128]{1,0:T(8,128)(2,1)S(1)} %bitcast.10, bf16[336,128]{1,0:T(8,128)(2,1)S(1)} %bitcast.9, f32[12,320,128]{2,1,0:T(8,128)S(1)} %get-tuple-element.15.refs_3_, ...), custom_call_target="tpu_custom_call" | custom-call | tf_op jit(solution)/shard_map/mate/pallas_call | solution.py:308
  (1 shorter events, 0.0 us)
Async XLA Ops:
  0.0 1.0 %copy-start = (f32[1,3,24,8,128]{4,3,2,1,0:T(8,128)S(1)}, f32[1,3,24,8,128]{4,3,2,1,0:T(8,128)}, u32[]{:S(2)}) copy-start(f32[1,3,24,8,128]{4,3,2,1,0:T(8,128)} %vel_hbm.1) | copy-start | bytes 884740
  1.0 0.8 %copy-start.2 = (bf16[1,24,8,128]{3,2,1,0:T(8,128)(2,1)S(1)}, bf16[1,24,8,128]{3,2,1,0:T(8,128)(2,1)}, u32[]{:S(2)}) copy-start(bf16[1,24,8,128]{3,2,1,0:T(8,128)(2,1)} %image_hbm.1) | copy-start | bytes 147460
  1.8 14.7 %copy-start.1 = (f32[1,3,24,8,128]{4,3,2,1,0:T(8,128)S(1)}, f32[1,3,24,8,128]{4,3,2,1,0:T(8,128)}, u32[]{:S(2)}) copy-start(f32[1,3,24,8,128]{4,3,2,1,0:T(8,128)} %vel_hbm.1) | copy-start | bytes 884740
  1.8 14.7 %copy-start.3 = (s32[4,2]{0,1:T(2,128)S(1)}, s32[4,2]{0,1:T(2,128)}, u32[]{:S(2)}) copy-start(s32[4,2]{0,1:T(2,128)} %param.7) | copy-start | bytes 100
  1.8 14.7 %copy-start.4 = (s32[4]{0:T(128)S(1)}, s32[4]{0:T(128)}, u32[]{:S(2)}) copy-start(s32[4]{0:T(128)} %partner.1) | copy-start | bytes 52
  2.0 3.3 %collective-permute-start = (bf16[13,8,128]{2,1,0:T(8,128)(2,1)S(1)}, bf16[13,8,128]{2,1,0:T(8,128)(2,1)S(1)}, u32[]{:S(2)}, u32[]{:S(2)}) collective-permute-start(bf16[13,8,128]{2,1,0:T(8,128)(2,1)S(1)} %get-tuple-element.13.sent1), channel_id=1, source_target_pairs={{0,1},{2,3},{1,0},{3,2},{4,5},{6,7},{5,4},{7,6},{8,9},{10,11},{9,8... | collective-permute-start | bytes 79880 | tf_op jit(solution)/shard_map/ppermute | solution.py:411
  3.4 4.6 %collective-permute-start.1 = (bf16[13,8,128]{2,1,0:T(8,128)(2,1)S(1)}, bf16[13,8,128]{2,1,0:T(8,128)(2,1)S(1)}, u32[]{:S(2)}, u32[]{:S(2)}) collective-permute-start(bf16[13,8,128]{2,1,0:T(8,128)(2,1)S(1)} %get-tuple-element.14.sent2), channel_id=1, source_target_pairs={{1,2},{2,1},{5,6},{6,5},{9,10},{10,9},{13,14},{14,13},{17,18},{18,... | collective-permute-start | bytes 79880 | tf_op jit(solution)/shard_map/ppermute | solution.py:410
  8.0 8.3 %collective-permute-start.4 = (bf16[42,8,128]{2,1,0:T(8,128)(2,1)S(1)}, bf16[42,8,128]{2,1,0:T(8,128)(2,1)S(1)}, u32[]{:S(2)}, u32[]{:S(2)}) collective-permute-start(bf16[42,8,128]{2,1,0:T(8,128)(2,1)S(1)} %widen.1), channel_id=1, source_target_pairs={{0,12},{4,8},{8,4},{12,0},{1,13},{5,9},{9,5},{13,1},{2,14},{6,10},... | collective-permute-start | bytes 258056 | tf_op jit(solution)/shard_map/ppermute | solution.py:421
  11.3 5.1 %collective-permute-start.3 = (bf16[42,8,128]{2,1,0:T(8,128)(2,1)S(1)}, bf16[42,8,128]{2,1,0:T(8,128)(2,1)S(1)}, u32[]{:S(2)}, u32[]{:S(2)}) collective-permute-start(bf16[42,8,128]{2,1,0:T(8,128)(2,1)S(1)} %widen.1), channel_id=1, source_target_pairs={{0,8},{4,12},{8,0},{12,4},{1,9},{5,13},{9,1},{13,5},{2,10},{6,14},... | collective-permute-start | bytes 258056 | tf_op jit(solution)/shard_map/ppermute | solution.py:421
  11.6 4.9 %collective-permute-start.2 = (bf16[42,8,128]{2,1,0:T(8,128)(2,1)S(1)}, bf16[42,8,128]{2,1,0:T(8,128)(2,1)S(1)}, u32[]{:S(2)}, u32[]{:S(2)}) collective-permute-start(bf16[42,8,128]{2,1,0:T(8,128)(2,1)S(1)} %widen.1), channel_id=1, source_target_pairs={{0,4},{4,0},{8,12},{12,8},{1,5},{5,1},{9,13},{13,9},{2,6},{6,2},{1... | collective-permute-start | bytes 258056 | tf_op jit(solution)/shard_map/ppermute | solution.py:421

commit v4 on v3

--- a/solution.py
+++ b/solution.py
@@ -52,40 +52,52 @@
     nd = planes + 16
     ng = nd // 8
 
-    def squares(g, carry):
+    def squares(g, carry, scale=None):
         c1, c2 = carry
-        scale = jnp.where(g == 0, low, jnp.where(g == ng - 1, high, 1.0))
         for i in range(8):
             s = g * 8 + i
             ld = lambda n, p: xs[n, pl.ds(pl.multiple_of(p * 8, 8), 8), :]
             near = [ld(0, s + 2), ld(0, s)] + [ld(j, s + 1) for j in (1, 2, 3, 4)]
             n1, n2 = [], []
+            done = []
             for k, (a, b) in enumerate(PAIRS):
                 d = near[a] - near[b]
-                q = d * d * scale
-                tb[k, pl.ds(pl.multiple_of(s * 8, 8), 8), :] = c2[k] + q
+                q = d * d
+                if scale is not None:
+                    q = q * scale
+                done.append(c2[k] + q)
                 n2.append(c1[k] + q)
                 n1.append(q)
+            put(s, done)
             c1, c2 = n1, n2
         return c1, c2
+
+    def put(s, done):
+        at = pl.ds(s * 8 if isinstance(s, int) else pl.multiple_of(s * 8, 8), 8)
+        for k in range(12):
+            tb[k, at, :] = done[k]
+        while len(done) > 1:
+            done = [done[n] + done[n + 1] for n in range(0, len(done) - 1, 2)] + done[len(done) // 2 * 2:]
+        tb[12, at, :] = done[0]
+
     zero = [jnp.zeros((8, 128), f32)] * 12
-    c1, c2 = lax.fori_loop(0, ng, squares, (zero, zero))
-    for k in range(12):
-        tb[k, pl.ds(nd * 8, 8), :] = c2[k]
+    carry = squares(0, (zero, zero), low)
+    carry = lax.fori_loop(1, ng - 1, squares, carry)
+    c1, c2 = squares(ng - 1, carry, high)
+    put(nd, c2)
 
     for g in range(ng):
         parts = []
-        for r in range(8):
-            for k in range(12):
-                t = [tb[k, pl.ds(g * 64 + 8 + n, 8, stride=8), :] for n in (r - 1, r, r + 1) if 0 <= n < 8]
-                parts.append(functools.reduce(jnp.add, t))
+        for k in (12,) + tuple(range(12)):
+            t = [tb[k, pl.ds(g * 64 + 8 + r, 8, stride=8), :] for r in range(8)]
+            p = [t[r] + t[r + 1] for r in range(7)]
+            parts += [p[0]] + [p[r - 1] + t[r + 1] for r in range(1, 7)] + [p[6]]
         box = dot(halves(parts), box3[...])
-        for r in range(8):
-            v = [box[(r * 12 + k) * 8:(r * 12 + k) * 8 + 8] for k in range(12)]
-            total = functools.reduce(jnp.add, v)
-            inv = (-LOG2E / 27.0) / (total * (1.0 / 324.0) + 0.1)
-            for k in range(12):
-                e = jnp.exp2(v[k] * inv)
+        inv = [(-LOG2E / 27.0) / (box[r * 8:r * 8 + 8] * (1.0 / 324.0) + 0.1) for r in range(8)]
+        for k in range(12):
+            for r in range(8):
+                n = (k + 1) * 64 + r * 8
+                e = jnp.exp2(box[n:n + 8] * inv[r])
                 if g == 0:
                     e = e * low
                 if g == ng - 1:
@@ -170,15 +182,13 @@
     lax.fori_loop(0, 12 // UNROLL, channels, 0)
 
 
-def mate_kernel(planes, count, partner, offsets, *refs):
+def mate_kernel(planes, count, *refs):
     mates = refs[:count]
-    adesc, mean, slope, grads, vel, out, box3, box9, smooth, xs, raw, tb, desc, ys, frc = refs[count:]
+    meta, adesc, mean, slope, grads, vel, out, box3, box9, smooth, xs, raw, tb, desc, ys, frc = refs[count:]
     nx, nd, nf = planes + 18, planes + 16, planes + 8
     low, high = faces()
-    me = lax.axis_index("brain")
-    mate = partner[me]
-    dr = offsets[0, mate] - offsets[0, me]
-    dc = offsets[1, mate] - offsets[1, me]
+    which, dc = meta[0:1, :], meta[16:17, :]
+    dr = jnp.max(meta[8:16, :])
     i, j = lanes()
     weights = jnp.zeros((128, 128), f32)
     for d in range(4):
@@ -193,7 +203,7 @@
 
     x = mates[0][...]
     for n in range(1, count):
-        x = jnp.where((me ^ mate) == n + 1, mates[n][...], x)
+        x = jnp.where(which == n + 1, mates[n][...], x)
     for n, d in ((0, 0), (1, 1), (2, -1)):
         take = ones_where((i == j + d + dc) & (j + d >= 0) & (j + d < 128))
         raw[n, pl.ds(8, nx * 8), :] = dot(x, take)
@@ -207,32 +217,34 @@
     lax.fori_loop(0, nx, prep, 0, unroll=6)
     describe(planes, xs, box3, tb, desc, low, high)
 
-    def channels(k, _):
-        for h in range(UNROLL):
-            one_channel(UNROLL * k + h, h)
+    def channels(step, _):
+        ks = [UNROLL * step + h for h in range(UNROLL)]
+        sums = []
+        for h, k in enumerate(ks):
+            lda = lambda t: adesc[k, pl.ds(t * 8, 8), :]
+            ldb = lambda t: desc[k, pl.ds(t * 8, 8), :]
+            depth_sums(planes, ldb, ys, 3 * h)
+            depth_sums(planes, lambda t: ldb(t) * ldb(t), ys, 3 * h + 1)
+            depth_sums(planes, lambda t: lda(t) * ldb(t), ys, 3 * h + 2)
+            parts = []
+            for g in range(nf // 8):
+                for q in range(3):
+                    parts += row_sums(ys, 3 * h + q, g)
+            sums.append(dot(halves(parts), box9[...]))
+        for g in range(nf // 8):
+            for r in range(8):
+                at = pl.ds(g * 64 + r * 8, 8)
+                acc = [frc[c, at, :] for c in range(3)]
+                for h, k in enumerate(ks):
+                    mm, sm, sc = [sums[h][(g * 24 + q * 8 + r) * 8:(g * 24 + q * 8 + r) * 8 + 8] for q in range(3)]
+                    b = desc[k, pl.ds(g * 64 + 32 + r, 8, stride=8), :]
+                    inv = lax.rsqrt(VOLUME * sm - mm * mm + FLOOR)
+                    cov = VOLUME * sc - mean[k, at, :] * mm
+                    coef = (VOLUME * b - mm - cov * slope[k, at, :]) * inv
+                    acc = [acc[c] + coef * grads[c, k, at, :] for c in range(3)]
+                for c in range(3):
+                    frc[c, at, :] = acc[c]
         return 0
-
-    def one_channel(k, h):
-        lda = lambda t: adesc[k, pl.ds(t * 8, 8), :]
-        ldb = lambda t: desc[k, pl.ds(t * 8, 8), :]
-        depth_sums(planes, ldb, ys, 3 * h)
-        depth_sums(planes, lambda t: ldb(t) * ldb(t), ys, 3 * h + 1)
-        depth_sums(planes, lambda t: lda(t) * ldb(t), ys, 3 * h + 2)
-        parts = []
-        for g in range(nf // 8):
-            for q in range(3):
-                parts += row_sums(ys, 3 * h + q, g)
-        sums = dot(halves(parts), box9[...])
-        for g in range(nf // 8):
-            for r in range(8):
-                at = pl.ds(g * 64 + r * 8, 8)
-                mm, sm, sc = [sums[(g * 24 + q * 8 + r) * 8:(g * 24 + q * 8 + r) * 8 + 8] for q in range(3)]
-                b = desc[k, pl.ds(g * 64 + 32 + r, 8, stride=8), :]
-                inv = lax.rsqrt(VOLUME * sm - mm * mm + FLOOR)
-                cov = VOLUME * sc - mean[k, at, :] * mm
-                coef = (VOLUME * b - mm - cov * slope[k, at, :]) * inv
-                for c in range(3):
-                    frc[c, at, :] = frc[c, at, :] + coef * grads[c, k, at, :]
     frc[...] = jnp.zeros_like(frc)
     lax.fori_loop(0, 12 // UNROLL, channels, 0)
 
@@ -272,7 +284,7 @@
 
 
 VM = pl.BlockSpec(memory_space=pltpu.VMEM)
-SM = pl.BlockSpec(memory_space=pltpu.SMEM)
+HBM = pl.BlockSpec(memory_space=pltpu.HBM)
 
 
 def own_part(planes, own):
@@ -293,7 +305,7 @@
             pltpu.VMEM((256, 128), bf16),
             pltpu.VMEM((256, 128), bf16),
             pltpu.VMEM((5, nx * 8, 128), f32),
-            pltpu.VMEM((12, (nd + 1) * 8, 128), f32),
+            pltpu.VMEM((13, (nd + 1) * 8, 128), f32),
             pltpu.VMEM((2 * UNROLL, nf * 8, 128), f32),
         ],
         compiler_params=pltpu.CompilerParams(vmem_limit_bytes=16 * 2**20),
@@ -302,13 +314,13 @@
     )(own.reshape(-1, 128))
 
 
-def mate_part(planes, partner, offsets, mates, owned, vel):
+def mate_part(planes, mates, meta, owned, vel):
     nx, nd, nf = planes + 18, planes + 16, planes + 8
     count = len(mates)
     return pl.pallas_call(
         functools.partial(mate_kernel, planes, count),
         out_shape=jax.ShapeDtypeStruct(vel.shape, f32),
-        in_specs=[SM, SM] + [VM] * (count + 5),
+        in_specs=[VM] * (count + 6),
         out_specs=VM,
         scratch_shapes=[
             pltpu.VMEM((256, 128), bf16),
@@ -316,20 +328,22 @@
             pltpu.VMEM((384, 128), bf16),
             pltpu.VMEM((5, nx * 8, 128), f32),
             pltpu.VMEM((3, nx * 8 + 16, 128), f32),
-            pltpu.VMEM((12, (nd + 1) * 8, 128), f32),
+            pltpu.VMEM((13, (nd + 1) * 8, 128), f32),
             pltpu.VMEM((12, nd * 8, 128), f32),
             pltpu.VMEM((3 * UNROLL, nf * 8, 128), f32),
             pltpu.VMEM((3, nf * 8, 128), f32),
         ],
         compiler_params=pltpu.CompilerParams(vmem_limit_bytes=16 * 2**20),
         name="mate",
-    )(partner, offsets.T, *[m.reshape(-1, 128) for m in mates], *owned, vel)
-
-
-def advect_kernel(planes, image_hbm, vel_hbm, warp, first, second, image, vel, down, up, sems):
+    )(*[m.reshape(-1, 128) for m in mates], meta, *owned, vel)
+
+
+def advect_kernel(planes, image_hbm, vel_hbm, partner_hbm, offsets_hbm, warp, first, second, meta, image, vel, down, up, partner, offsets, sems):
     copies = [
         pltpu.make_async_copy(vel_hbm, vel, sems.at[0]),
         pltpu.make_async_copy(image_hbm, image, sems.at[1]),
+        pltpu.make_async_copy(partner_hbm, partner, sems.at[2]),
+        pltpu.make_async_copy(offsets_hbm, offsets, sems.at[3]),
     ]
     for copy in copies:
         copy.start()
@@ -361,6 +375,10 @@
             down[z - 1] = y.astype(bf16)
         if planes - 9 <= z < planes - 1:
             up[z - (planes - 9)] = y.astype(bf16)
+    me = lax.axis_index("brain")
+    mate = partner[me]
+    for n, value in enumerate((me ^ mate, offsets[0, mate] - offsets[0, me], offsets[1, mate] - offsets[1, me])):
+        meta[n * 8:n * 8 + 8, :] = jnp.full((8, 128), value, jnp.int32)
     even = lax.rem(lax.axis_index("slab"), 2) == 0
     for n in range(EDGE):
         first[n] = jnp.where(even, up[n], down[n])
@@ -389,21 +407,23 @@
     planes = intensity.shape[1]
     slabs, brains = lax.axis_size("slab"), lax.axis_size("brain")
     edge = jax.ShapeDtypeStruct((EDGE, 8, 128), bf16)
-    warp, first, second = pl.pallas_call(
+    warp, first, second, meta = pl.pallas_call(
         functools.partial(advect_kernel, planes),
-        out_shape=(jax.ShapeDtypeStruct((planes, 8, 128), f32), edge, edge),
-        in_specs=[pl.BlockSpec(memory_space=pltpu.HBM)] * 2,
-        out_specs=(VM,) * 3,
+        out_shape=(jax.ShapeDtypeStruct((planes, 8, 128), f32), edge, edge, jax.ShapeDtypeStruct((24, 128), jnp.int32)),
+        in_specs=[HBM] * 4,
+        out_specs=(VM,) * 4,
         scratch_shapes=[
             pltpu.VMEM(intensity.shape, bf16),
             pltpu.VMEM(velocity.shape, f32),
             pltpu.VMEM(edge.shape, bf16),
             pltpu.VMEM(edge.shape, bf16),
-            pltpu.SemaphoreType.DMA((2,)),
+            pltpu.SMEM(partner.shape, jnp.int32),
+            pltpu.SMEM(offsets.shape[::-1], jnp.int32),
+            pltpu.SemaphoreType.DMA((4,)),
         ],
         compiler_params=pltpu.CompilerParams(vmem_limit_bytes=8 * 2**20),
         name="advect",
-    )(intensity, velocity)
+    )(*[pltpu.with_memory_space_constraint(v, pltpu.HBM) for v in (intensity, velocity, partner, offsets.T)])
     odd_pairs = [(n, n + 1) for n in range(1, slabs - 1, 2)]
     even_pairs = [(n, n + 1) for n in range(0, slabs - 1, 2)]
     both_ways = lambda pairs: pairs + [(b, a) for a, b in pairs]
@@ -422,7 +442,7 @@
     else:
         gathered = lax.all_gather(own, "brain")
         mates = [lax.dynamic_index_in_dim(gathered, partner[lax.axis_index("brain")], 0, keepdims=False)]
-    return mate_part(planes, partner, offsets, mates, own_part(planes, own), velocity[0])[None]
+    return mate_part(planes, mates, meta, own_part(planes, own), velocity[0])[None]
 
 
 def solution(mesh):

time: 24.2 us -> 22.6 us (0.934)
  local copies, waits for them, and re-layouts: 1.77 us -> 0.01 us
  waiting for transfers between devices: 2.72 us -> 3 us
    unnamed x10 -> x2, local copies, waits for them, and re-layouts: 1.77 us -> 0.01 us
    pallas_call x1, Pallas kernels: 0.27 us -> 1.22 us  [shards(): pl.pallas_call(functools.partial(advect_kernel, planes), out_shape=(jax.S...]
    pallas_call x1, Pallas kernels: 7.52 us -> 6.82 us  [mate_part(): pl.pallas_call(functools.partial(mate_kernel, planes, count), out_shape=j...]
    ppermute x3, waiting for transfers between devices: 0.07 us -> 0.35 us  [shards(): lax.ppermute(own, 'brain', [(n, n ^ k) for n in range(4)])]
    pallas_call x1, Pallas kernels: 4.58 us -> 4.3 us  [own_part(): pl.pallas_call(functools.partial(own_kernel, planes), out_shape=(shape((1...]
where the time goes in v4:
time: 22.6 us; the launch traced here: 22.4 us
  Pallas kernels  12.4 us (55%)
  starting transfers between devices  7.01 us (31%)
  waiting for transfers between devices  3 us (13%)
    pallas_call x1, Pallas kernels, mate_part(): pl.pallas_call(functools.partial(mate_kernel, planes, count), out_shape=j...  6.82 us
    pallas_call x1, Pallas kernels, own_part(): pl.pallas_call(functools.partial(own_kernel, planes), out_shape=(shape((1...  4.3 us
    ppermute x3, starting transfers between devices, shards(): lax.ppermute(own, 'brain', [(n, n ^ k) for n in range(4)])  3.74 us
    ppermute x1, waiting for transfers between devices, shards(): from_odd = lax.ppermute(second, 'slab', both_ways(odd_pairs))  2.65 us
    ppermute x1, starting transfers between devices, shards(): from_odd = lax.ppermute(second, 'slab', both_ways(odd_pairs))  1.91 us
    ppermute x1, starting transfers between devices, shards(): from_even = lax.ppermute(first, 'slab', both_ways(even_pairs))  1.36 us
    pallas_call x1, Pallas kernels, shards(): pl.pallas_call(functools.partial(advect_kernel, planes), out_shape=(jax.S...  1.22 us
  transfers between devices with their start and end apart: 5, of which 2 were waited for; matrix products, arithmetic and copies ran while one was open for 0% of the time, Pallas kernels for 19%

profile of v4, /device:TPU:17, one launch (start us, length us, event | category | flops | bytes accessed | tf_op | source)
XLA Modules:
  0.0 22.4 jit_solution(9966979255229688034)
XLA Ops:
  0.0 0.0 copy-start
  0.0 1.2 %advect.1 = (f32[24,8,128]{2,1,0:T(8,128)S(1)}, bf16[13,8,128]{2,1,0:T(8,128)(2,1)S(1)}, bf16[13,8,128]{2,1,0:T(8,128)(2,1)S(1)}, s32[24,128]{1,0:T(8,128)S(1)}) custom-call(bf16[1,24,8,128]{3,2,1,0:T(8,128)(2,1)} %image_hbm.1, f32[1,3,24,8,128]{4,3,2,1,0:T(8,128)} %vel_hbm.1, s32[4]{0:T(128)} %partner_hbm.1, s32[2,4]{1,0:T(2,128)} %bitcast.12), custom_call_target="tpu_custom_call" | custom-call | tf_op jit(solution)/shard_map/advect/pallas_call | solution.py:410
  1.2 1.4 %collective-permute-start = (bf16[13,8,128]{2,1,0:T(8,128)(2,1)S(1)}, bf16[13,8,128]{2,1,0:T(8,128)(2,1)S(1)}, u32[]{:S(2)}, u32[]{:S(2)}) collective-permute-start(bf16[13,8,128]{2,1,0:T(8,128)(2,1)S(1)} %get-tuple-element.14.sent1), channel_id=1, source_target_pairs={{0,1},{2,3},{1,0},{3,2},{4,5},{6,7},{5,4},{7,6},{8,9},{10,11},{9,8... | collective-permute-start | bytes 79880 | tf_op jit(solution)/shard_map/ppermute | solution.py:431
  2.6 1.9 %collective-permute-start.1 = (bf16[13,8,128]{2,1,0:T(8,128)(2,1)S(1)}, bf16[13,8,128]{2,1,0:T(8,128)(2,1)S(1)}, u32[]{:S(2)}, u32[]{:S(2)}) collective-permute-start(bf16[13,8,128]{2,1,0:T(8,128)(2,1)S(1)} %get-tuple-element.15.sent2), channel_id=1, source_target_pairs={{1,2},{2,1},{5,6},{6,5},{9,10},{10,9},{13,14},{14,13},{17,18},{18,... | collective-permute-start | bytes 79880 | tf_op jit(solution)/shard_map/ppermute | solution.py:430
  4.5 0.0 collective-permute-done.got1
  4.5 2.7 %collective-permute-done.1.got2 = bf16[13,8,128]{2,1,0:T(8,128)(2,1)S(1)} collective-permute-done((bf16[13,8,128]{2,1,0:T(8,128)(2,1)S(1)}, bf16[13,8,128]{2,1,0:T(8,128)(2,1)S(1)}, u32[]{:S(2)}, u32[]{:S(2)}) %collective-permute-start.1) | collective-permute-done | bytes 26656 | tf_op jit(solution)/shard_map/ppermute | solution.py:430
  7.2 3.3 %collective-permute-start.4 = (bf16[42,8,128]{2,1,0:T(8,128)(2,1)S(1)}, bf16[42,8,128]{2,1,0:T(8,128)(2,1)S(1)}, u32[]{:S(2)}, u32[]{:S(2)}) collective-permute-start(bf16[42,8,128]{2,1,0:T(8,128)(2,1)S(1)} %widen.1), channel_id=1, source_target_pairs={{0,12},{4,8},{8,4},{12,0},{1,13},{5,9},{9,5},{13,1},{2,14},{6,10},... | collective-permute-start | bytes 258056 | tf_op jit(solution)/shard_map/ppermute | solution.py:441
  10.5 0.3 %collective-permute-start.3 = (bf16[42,8,128]{2,1,0:T(8,128)(2,1)S(1)}, bf16[42,8,128]{2,1,0:T(8,128)(2,1)S(1)}, u32[]{:S(2)}, u32[]{:S(2)}) collective-permute-start(bf16[42,8,128]{2,1,0:T(8,128)(2,1)S(1)} %widen.1), channel_id=1, source_target_pairs={{0,8},{4,12},{8,0},{12,4},{1,9},{5,13},{9,1},{13,5},{2,10},{6,14},... | collective-permute-start | bytes 258056 | tf_op jit(solution)/shard_map/ppermute | solution.py:441
  10.7 0.2 collective-permute-start.2
  11.0 4.3 %own.1 = (f32[12,320,128]{2,1,0:T(8,128)S(1)}, f32[12,256,128]{2,1,0:T(8,128)S(1)}, f32[12,256,128]{2,1,0:T(8,128)S(1)}, f32[3,12,256,128]{3,2,1,0:T(8,128)S(1)}) custom-call(bf16[336,128]{1,0:T(8,128)(2,1)S(1)} %bitcast.8), custom_call_target="tpu_custom_call" | custom-call | flops 600000000 | bytes 16777216 | tf_op jit(solution)/shard_map/own/pallas_call | solution.py:293
  15.3 0.0 collective-permute-done.4
  15.3 0.3 %collective-permute-done.3 = bf16[42,8,128]{2,1,0:T(8,128)(2,1)S(1)} collective-permute-done((bf16[42,8,128]{2,1,0:T(8,128)(2,1)S(1)}, bf16[42,8,128]{2,1,0:T(8,128)(2,1)S(1)}, u32[]{:S(2)}, u32[]{:S(2)}) %collective-permute-start.3) | collective-permute-done | bytes 86048 | tf_op jit(solution)/shard_map/ppermute | solution.py:441
  15.6 0.0 collective-permute-done.2
  15.6 0.0 copy-done
  15.6 6.8 %mate.1 = f32[3,24,8,128]{3,2,1,0:T(8,128)} custom-call(bf16[336,128]{1,0:T(8,128)(2,1)S(1)} %bitcast.11, bf16[336,128]{1,0:T(8,128)(2,1)S(1)} %bitcast.10, bf16[336,128]{1,0:T(8,128)(2,1)S(1)} %bitcast.9, s32[24,128]{1,0:T(8,128)S(1)} %get-tuple-element.16.refs_3_, f32[12,320,128]{2,1,0:T(8,128)S(1)} %get-tuple-element.17.refs_4_, ...), custom_call_target="tpu_custom_call" | custom-call | tf_op jit(solution)/shard_map/mate/pallas_call | solution.py:320
  (1 shorter events, 0.0 us)
Async XLA Ops:
  0.0 15.6 %copy-start = (f32[1,3,24,8,128]{4,3,2,1,0:T(8,128)S(1)}, f32[1,3,24,8,128]{4,3,2,1,0:T(8,128)}, u32[]{:S(2)}) copy-start(f32[1,3,24,8,128]{4,3,2,1,0:T(8,128)} %vel_hbm.1) | copy-start | bytes 884740
  1.2 3.3 %collective-permute-start = (bf16[13,8,128]{2,1,0:T(8,128)(2,1)S(1)}, bf16[13,8,128]{2,1,0:T(8,128)(2,1)S(1)}, u32[]{:S(2)}, u32[]{:S(2)}) collective-permute-start(bf16[13,8,128]{2,1,0:T(8,128)(2,1)S(1)} %get-tuple-element.14.sent1), channel_id=1, source_target_pairs={{0,1},{2,3},{1,0},{3,2},{4,5},{6,7},{5,4},{7,6},{8,9},{10,11},{9,8... | collective-permute-start | bytes 79880 | tf_op jit(solution)/shard_map/ppermute | solution.py:431
  2.6 4.6 %collective-permute-start.1 = (bf16[13,8,128]{2,1,0:T(8,128)(2,1)S(1)}, bf16[13,8,128]{2,1,0:T(8,128)(2,1)S(1)}, u32[]{:S(2)}, u32[]{:S(2)}) collective-permute-start(bf16[13,8,128]{2,1,0:T(8,128)(2,1)S(1)} %get-tuple-element.15.sent2), channel_id=1, source_target_pairs={{1,2},{2,1},{5,6},{6,5},{9,10},{10,9},{13,14},{14,13},{17,18},{18,... | collective-permute-start | bytes 79880 | tf_op jit(solution)/shard_map/ppermute | solution.py:430
  7.2 8.1 %collective-permute-start.4 = (bf16[42,8,128]{2,1,0:T(8,128)(2,1)S(1)}, bf16[42,8,128]{2,1,0:T(8,128)(2,1)S(1)}, u32[]{:S(2)}, u32[]{:S(2)}) collective-permute-start(bf16[42,8,128]{2,1,0:T(8,128)(2,1)S(1)} %widen.1), channel_id=1, source_target_pairs={{0,12},{4,8},{8,4},{12,0},{1,13},{5,9},{9,5},{13,1},{2,14},{6,10},... | collective-permute-start | bytes 258056 | tf_op jit(solution)/shard_map/ppermute | solution.py:441
  10.5 5.1 %collective-permute-start.3 = (bf16[42,8,128]{2,1,0:T(8,128)(2,1)S(1)}, bf16[42,8,128]{2,1,0:T(8,128)(2,1)S(1)}, u32[]{:S(2)}, u32[]{:S(2)}) collective-permute-start(bf16[42,8,128]{2,1,0:T(8,128)(2,1)S(1)} %widen.1), channel_id=1, source_target_pairs={{0,8},{4,12},{8,0},{12,4},{1,9},{5,13},{9,1},{13,5},{2,10},{6,14},... | collective-permute-start | bytes 258056 | tf_op jit(solution)/shard_map/ppermute | solution.py:441
  10.7 4.9 %collective-permute-start.2 = (bf16[42,8,128]{2,1,0:T(8,128)(2,1)S(1)}, bf16[42,8,128]{2,1,0:T(8,128)(2,1)S(1)}, u32[]{:S(2)}, u32[]{:S(2)}) collective-permute-start(bf16[42,8,128]{2,1,0:T(8,128)(2,1)S(1)} %widen.1), channel_id=1, source_target_pairs={{0,4},{4,0},{8,12},{12,8},{1,5},{5,1},{9,13},{13,9},{2,6},{6,2},{1... | collective-permute-start | bytes 258056 | tf_op jit(solution)/shard_map/ppermute | solution.py:441

commit v5 on v4

--- a/solution.py
+++ b/solution.py
@@ -12,6 +12,8 @@
 EDGE = 13
 VOLUME = 729.0
 UNROLL = 2
+PITCH = 9
+SPARE = 16
 FLOOR = 1e-5 * VOLUME * VOLUME
 
 
@@ -73,7 +75,7 @@
         return c1, c2
 
     def put(s, done):
-        at = pl.ds(s * 8 if isinstance(s, int) else pl.multiple_of(s * 8, 8), 8)
+        at = pl.ds(s * PITCH, 8)
         for k in range(12):
             tb[k, at, :] = done[k]
         while len(done) > 1:
@@ -89,7 +91,7 @@
     for g in range(ng):
         parts = []
         for k in (12,) + tuple(range(12)):
-            t = [tb[k, pl.ds(g * 64 + 8 + r, 8, stride=8), :] for r in range(8)]
+            t = [tb[k, pl.ds((g * 8 + 1) * PITCH + r, 8, stride=PITCH), :] for r in range(8)]
             p = [t[r] + t[r + 1] for r in range(7)]
             parts += [p[0]] + [p[r - 1] + t[r + 1] for r in range(1, 7)] + [p[6]]
         box = dot(halves(parts), box3[...])
@@ -102,7 +104,7 @@
                     e = e * low
                 if g == ng - 1:
                     e = e * high
-                desc[k, pl.ds(g * 64 + r, 8, stride=8), :] = e
+                desc[k, pl.ds(g * 8 * PITCH + r, 8, stride=PITCH), :] = e
 
 
 def depth_sums(planes, value, ys, q):
@@ -114,11 +116,11 @@
             total = ((s2[0] + s2[1]) + (s2[2] + s2[3])) + d[f + 8]
         else:
             total = (total - d[f - 1]) + d[f + 8]
-        ys[q, pl.ds(f * 8, 8), :] = total
+        ys[q, pl.ds(f * PITCH, 8), :] = total
 
 
 def row_sums(ys, q, g):
-    t = [ys[q, pl.ds(g * 64 + r, 8, stride=8), :] for r in range(8)]
+    t = [ys[q, pl.ds(g * 8 * PITCH + r, 8, stride=PITCH), :] for r in range(8)]
     lo = (t[0] + t[1]) + (t[2] + t[3])
     hi = (t[4] + t[5]) + (t[6] + t[7])
     w0 = lo + t[4]
@@ -156,14 +158,14 @@
         return 0
 
     def one_channel(k, h):
-        ld = lambda t: desc[k, pl.ds(t * 8, 8), :]
+        ld = lambda t: desc[k, pl.ds(t * PITCH, 8), :]
         depth_sums(planes, ld, ys, 2 * h)
         depth_sums(planes, lambda t: ld(t) * ld(t), ys, 2 * h + 1)
         parts, centre = [], []
         for g in range(nf // 8):
             for q in range(2):
                 parts += row_sums(ys, 2 * h + q, g)
-            centre += [desc[k, pl.ds(g * 64 + 32 + r, 8, stride=8), :] for r in range(8)]
+            centre += [desc[k, pl.ds((g * 8 + 4) * PITCH + r, 8, stride=PITCH), :] for r in range(8)]
         sums = dot(halves(parts), box9[...])
         across = dot(halves(centre), grad[...])
         for g in range(nf // 8):
@@ -173,7 +175,7 @@
                 mo, so = [sums[(g * 16 + q * 8 + r) * 8:(g * 16 + q * 8 + r) * 8 + 8] for q in range(2)]
                 gc = across[(g * 8 + r) * 8:(g * 8 + r) * 8 + 8]
                 inv = lax.rsqrt(VOLUME * so - mo * mo + FLOOR)
-                gz = desc[k, pl.ds(g * 64 + 40 + r, 8, stride=8), :] - desc[k, pl.ds(g * 64 + 24 + r, 8, stride=8), :]
+                gz = desc[k, pl.ds((g * 8 + 5) * PITCH + r, 8, stride=PITCH), :] - desc[k, pl.ds((g * 8 + 3) * PITCH + r, 8, stride=PITCH), :]
                 gr = a[1] if r == 0 else -a[6] if r == 7 else a[r + 1] - a[r - 1]
                 mean[k, at, :] = mo
                 slope[k, at, :] = (inv * inv) * (VOLUME * a[r] - mo)
@@ -221,8 +223,8 @@
         ks = [UNROLL * step + h for h in range(UNROLL)]
         sums = []
         for h, k in enumerate(ks):
-            lda = lambda t: adesc[k, pl.ds(t * 8, 8), :]
-            ldb = lambda t: desc[k, pl.ds(t * 8, 8), :]
+            lda = lambda t: adesc[k, pl.ds(t * PITCH, 8), :]
+            ldb = lambda t: desc[k, pl.ds(t * PITCH, 8), :]
             depth_sums(planes, ldb, ys, 3 * h)
             depth_sums(planes, lambda t: ldb(t) * ldb(t), ys, 3 * h + 1)
             depth_sums(planes, lambda t: lda(t) * ldb(t), ys, 3 * h + 2)
@@ -237,7 +239,7 @@
                 acc = [frc[c, at, :] for c in range(3)]
                 for h, k in enumerate(ks):
                     mm, sm, sc = [sums[h][(g * 24 + q * 8 + r) * 8:(g * 24 + q * 8 + r) * 8 + 8] for q in range(3)]
-                    b = desc[k, pl.ds(g * 64 + 32 + r, 8, stride=8), :]
+                    b = desc[k, pl.ds((g * 8 + 4) * PITCH + r, 8, stride=PITCH), :]
                     inv = lax.rsqrt(VOLUME * sm - mm * mm + FLOOR)
                     cov = VOLUME * sc - mean[k, at, :] * mm
                     coef = (VOLUME * b - mm - cov * slope[k, at, :]) * inv
@@ -257,15 +259,15 @@
                     v = jnp.where(row >= 4, v, v * low)
                 if g == nf // 8 - 1:
                     v = jnp.where(row < 4, v, v * high)
-                ys[0, pl.ds(g * 64 + r, 8, stride=8), :] = v
+                ys[0, pl.ds(g * 8 * PITCH + r, 8, stride=PITCH), :] = v
         for o in range(planes):
-            p = [ys[0, pl.ds((o + 1 + n) * 8, 8), :] for n in range(7)]
+            p = [ys[0, pl.ds((o + 1 + n) * PITCH, 8), :] for n in range(7)]
             v = TAPS[3] * p[3]
             for n in range(3):
                 v = v + TAPS[n] * (p[n] + p[6 - n])
-            ys[1, pl.ds(o * 8, 8), :] = v
+            ys[1, pl.ds(o * PITCH, 8), :] = v
         for g in range(planes // 8):
-            t = [ys[1, pl.ds(g * 64 + r, 8, stride=8), :] for r in range(8)]
+            t = [ys[1, pl.ds(g * 8 * PITCH + r, 8, stride=PITCH), :] for r in range(8)]
             for r in range(8):
                 v = TAPS[3] * t[r]
                 for n in range(1, 4):
@@ -278,9 +280,9 @@
         for g in range(planes // 8):
             for r in range(8):
                 n = ((c * planes + g * 8) + r) * 8
-                ys[0, pl.ds(g * 64 + r, 8, stride=8), :] = res[n:n + 8]
+                ys[0, pl.ds(g * 8 * PITCH + r, 8, stride=PITCH), :] = res[n:n + 8]
         for o in range(planes):
-            out[c, o] = vel[c, o] + (8.0 * VOLUME / 24.0) * ys[0, pl.ds(o * 8, 8), :]
+            out[c, o] = vel[c, o] + (8.0 * VOLUME / 24.0) * ys[0, pl.ds(o * PITCH, 8), :]
 
 
 VM = pl.BlockSpec(memory_space=pltpu.VMEM)
@@ -293,7 +295,7 @@
     return pl.pallas_call(
         functools.partial(own_kernel, planes),
         out_shape=(
-            shape((12, nd * 8, 128), f32),
+            shape((12, nd * PITCH + SPARE, 128), f32),
             shape((12, nf * 8, 128), f32),
             shape((12, nf * 8, 128), f32),
             shape((3, 12, nf * 8, 128), f32),
@@ -305,8 +307,8 @@
             pltpu.VMEM((256, 128), bf16),
             pltpu.VMEM((256, 128), bf16),
             pltpu.VMEM((5, nx * 8, 128), f32),
-            pltpu.VMEM((13, (nd + 1) * 8, 128), f32),
-            pltpu.VMEM((2 * UNROLL, nf * 8, 128), f32),
+            pltpu.VMEM((13, (nd + 1) * PITCH + SPARE, 128), f32),
+            pltpu.VMEM((2 * UNROLL, nf * PITCH + SPARE, 128), f32),
         ],
         compiler_params=pltpu.CompilerParams(vmem_limit_bytes=16 * 2**20),
         cost_estimate=pl.CostEstimate(flops=6 * 10**8, bytes_accessed=16 * 2**20, transcendentals=10**6),
@@ -328,9 +330,9 @@
             pltpu.VMEM((384, 128), bf16),
             pltpu.VMEM((5, nx * 8, 128), f32),
             pltpu.VMEM((3, nx * 8 + 16, 128), f32),
-            pltpu.VMEM((13, (nd + 1) * 8, 128), f32),
-            pltpu.VMEM((12, nd * 8, 128), f32),
-            pltpu.VMEM((3 * UNROLL, nf * 8, 128), f32),
+            pltpu.VMEM((13, (nd + 1) * PITCH + SPARE, 128), f32),
+            pltpu.VMEM((12, nd * PITCH + SPARE, 128), f32),
+            pltpu.VMEM((3 * UNROLL, nf * PITCH + SPARE, 128), f32),
             pltpu.VMEM((3, nf * 8, 128), f32),
         ],
         compiler_params=pltpu.CompilerParams(vmem_limit_bytes=16 * 2**20),

time: 22.6 us -> 21.9 us (0.969)
  Pallas kernels: 12.4 us -> 11.3 us
  waiting for transfers between devices: 3 us -> 3.48 us
    pallas_call x1, Pallas kernels: 6.82 us -> 6.17 us  [mate_part(): pl.pallas_call(functools.partial(mate_kernel, planes, count), out_shape=j...]
    ppermute x3, waiting for transfers between devices: 0.35 us -> 0.82 us  [shards(): lax.ppermute(own, 'brain', [(n, n ^ k) for n in range(4)])]
    pallas_call x1, Pallas kernels: 4.3 us -> 3.83 us  [own_part(): pl.pallas_call(functools.partial(own_kernel, planes), out_shape=(shape((1...]
  transfers between devices with their start and end apart: 5 -> 5, of which waited for: 2 -> 2; matrix products, arithmetic and copies ran while one was open for 0% -> 0% of each run, Pallas kernels for 19% -> 18%
where the time goes in v5:
time: 21.9 us; the launch traced here: 21.8 us
  Pallas kernels  11.3 us (52%)
  starting transfers between devices  7.01 us (32%)
  waiting for transfers between devices  3.48 us (16%)
    pallas_call x1, Pallas kernels, mate_part(): pl.pallas_call(functools.partial(mate_kernel, planes, count), out_shape=j...  6.17 us
    pallas_call x1, Pallas kernels, own_part(): pl.pallas_call(functools.partial(own_kernel, planes), out_shape=(shape((1...  3.83 us
    ppermute x3, starting transfers between devices, shards(): lax.ppermute(own, 'brain', [(n, n ^ k) for n in range(4)])  3.74 us
    ppermute x1, waiting for transfers between devices, shards(): from_odd = lax.ppermute(second, 'slab', both_ways(odd_pairs))  2.65 us
    ppermute x1, starting transfers between devices, shards(): from_odd = lax.ppermute(second, 'slab', both_ways(odd_pairs))  1.91 us
    ppermute x1, starting transfers between devices, shards(): from_even = lax.ppermute(first, 'slab', both_ways(even_pairs))  1.36 us
    pallas_call x1, Pallas kernels, shards(): pl.pallas_call(functools.partial(advect_kernel, planes), out_shape=(jax.S...  1.22 us
    ppermute x3, waiting for transfers between devices, shards(): lax.ppermute(own, 'brain', [(n, n ^ k) for n in range(4)])  0.82 us
  transfers between devices with their start and end apart: 5, of which 2 were waited for; matrix products, arithmetic and copies ran while one was open for 0% of the time, Pallas kernels for 18%

profile of v5, /device:TPU:17, one launch (start us, length us, event | category | flops | bytes accessed | tf_op | source)
XLA Modules:
  0.0 21.8 jit_solution(6505098506829601926)
XLA Ops:
  0.0 0.0 copy-start
  0.0 1.2 %advect.1 = (f32[24,8,128]{2,1,0:T(8,128)S(1)}, bf16[13,8,128]{2,1,0:T(8,128)(2,1)S(1)}, bf16[13,8,128]{2,1,0:T(8,128)(2,1)S(1)}, s32[24,128]{1,0:T(8,128)S(1)}) custom-call(bf16[1,24,8,128]{3,2,1,0:T(8,128)(2,1)} %image_hbm.1, f32[1,3,24,8,128]{4,3,2,1,0:T(8,128)} %vel_hbm.1, s32[4]{0:T(128)} %partner_hbm.1, s32[2,4]{1,0:T(2,128)} %bitcast.12), custom_call_target="tpu_custom_call" | custom-call | tf_op jit(solution)/shard_map/advect/pallas_call | solution.py:412
  1.2 1.4 %collective-permute-start = (bf16[13,8,128]{2,1,0:T(8,128)(2,1)S(1)}, bf16[13,8,128]{2,1,0:T(8,128)(2,1)S(1)}, u32[]{:S(2)}, u32[]{:S(2)}) collective-permute-start(bf16[13,8,128]{2,1,0:T(8,128)(2,1)S(1)} %get-tuple-element.14.sent1), channel_id=1, source_target_pairs={{0,1},{2,3},{1,0},{3,2},{4,5},{6,7},{5,4},{7,6},{8,9},{10,11},{9,8... | collective-permute-start | bytes 79880 | tf_op jit(solution)/shard_map/ppermute | solution.py:433
  2.6 1.9 %collective-permute-start.1 = (bf16[13,8,128]{2,1,0:T(8,128)(2,1)S(1)}, bf16[13,8,128]{2,1,0:T(8,128)(2,1)S(1)}, u32[]{:S(2)}, u32[]{:S(2)}) collective-permute-start(bf16[13,8,128]{2,1,0:T(8,128)(2,1)S(1)} %get-tuple-element.15.sent2), channel_id=1, source_target_pairs={{1,2},{2,1},{5,6},{6,5},{9,10},{10,9},{13,14},{14,13},{17,18},{18,... | collective-permute-start | bytes 79880 | tf_op jit(solution)/shard_map/ppermute | solution.py:432
  4.5 0.0 collective-permute-done.got1
  4.5 2.7 %collective-permute-done.1.got2 = bf16[13,8,128]{2,1,0:T(8,128)(2,1)S(1)} collective-permute-done((bf16[13,8,128]{2,1,0:T(8,128)(2,1)S(1)}, bf16[13,8,128]{2,1,0:T(8,128)(2,1)S(1)}, u32[]{:S(2)}, u32[]{:S(2)}) %collective-permute-start.1) | collective-permute-done | bytes 26656 | tf_op jit(solution)/shard_map/ppermute | solution.py:432
  7.2 3.3 %collective-permute-start.4 = (bf16[42,8,128]{2,1,0:T(8,128)(2,1)S(1)}, bf16[42,8,128]{2,1,0:T(8,128)(2,1)S(1)}, u32[]{:S(2)}, u32[]{:S(2)}) collective-permute-start(bf16[42,8,128]{2,1,0:T(8,128)(2,1)S(1)} %widen.1), channel_id=1, source_target_pairs={{0,12},{4,8},{8,4},{12,0},{1,13},{5,9},{9,5},{13,1},{2,14},{6,10},... | collective-permute-start | bytes 258056 | tf_op jit(solution)/shard_map/ppermute | solution.py:443
  10.5 0.3 %collective-permute-start.3 = (bf16[42,8,128]{2,1,0:T(8,128)(2,1)S(1)}, bf16[42,8,128]{2,1,0:T(8,128)(2,1)S(1)}, u32[]{:S(2)}, u32[]{:S(2)}) collective-permute-start(bf16[42,8,128]{2,1,0:T(8,128)(2,1)S(1)} %widen.1), channel_id=1, source_target_pairs={{0,8},{4,12},{8,0},{12,4},{1,9},{5,13},{9,1},{13,5},{2,10},{6,14},... | collective-permute-start | bytes 258056 | tf_op jit(solution)/shard_map/ppermute | solution.py:443
  10.7 0.2 %collective-permute-start.2 = (bf16[42,8,128]{2,1,0:T(8,128)(2,1)S(1)}, bf16[42,8,128]{2,1,0:T(8,128)(2,1)S(1)}, u32[]{:S(2)}, u32[]{:S(2)}) collective-permute-start(bf16[42,8,128]{2,1,0:T(8,128)(2,1)S(1)} %widen.1), channel_id=1, source_target_pairs={{0,4},{4,0},{8,12},{12,8},{1,5},{5,1},{9,13},{13,9},{2,6},{6,2},{1... | collective-permute-start | bytes 258056 | tf_op jit(solution)/shard_map/ppermute | solution.py:443
  11.0 3.8 %own.1 = (f32[12,376,128]{2,1,0:T(8,128)S(1)}, f32[12,256,128]{2,1,0:T(8,128)S(1)}, f32[12,256,128]{2,1,0:T(8,128)S(1)}, f32[3,12,256,128]{3,2,1,0:T(8,128)S(1)}) custom-call(bf16[336,128]{1,0:T(8,128)(2,1)S(1)} %bitcast.8), custom_call_target="tpu_custom_call" | custom-call | flops 600000000 | bytes 16777216 | tf_op jit(solution)/shard_map/own/pallas_call | solution.py:295
  14.8 0.0 collective-permute-done.4
  14.8 0.8 %collective-permute-done.3 = bf16[42,8,128]{2,1,0:T(8,128)(2,1)S(1)} collective-permute-done((bf16[42,8,128]{2,1,0:T(8,128)(2,1)S(1)}, bf16[42,8,128]{2,1,0:T(8,128)(2,1)S(1)}, u32[]{:S(2)}, u32[]{:S(2)}) %collective-permute-start.3) | collective-permute-done | bytes 86048 | tf_op jit(solution)/shard_map/ppermute | solution.py:443
  15.6 0.0 collective-permute-done.2
  15.6 0.0 copy-done
  15.6 6.2 %mate.1 = f32[3,24,8,128]{3,2,1,0:T(8,128)} custom-call(bf16[336,128]{1,0:T(8,128)(2,1)S(1)} %bitcast.11, bf16[336,128]{1,0:T(8,128)(2,1)S(1)} %bitcast.10, bf16[336,128]{1,0:T(8,128)(2,1)S(1)} %bitcast.9, s32[24,128]{1,0:T(8,128)S(1)} %get-tuple-element.16.refs_3_, f32[12,376,128]{2,1,0:T(8,128)S(1)} %get-tuple-element.17.refs_4_, ...), custom_call_target="tpu_custom_call" | custom-call | tf_op jit(solution)/shard_map/mate/pallas_call | solution.py:322
  (1 shorter events, 0.0 us)
Async XLA Ops:
  0.0 15.6 %copy-start = (f32[1,3,24,8,128]{4,3,2,1,0:T(8,128)S(1)}, f32[1,3,24,8,128]{4,3,2,1,0:T(8,128)}, u32[]{:S(2)}) copy-start(f32[1,3,24,8,128]{4,3,2,1,0:T(8,128)} %vel_hbm.1) | copy-start | bytes 884740
  1.2 3.3 %collective-permute-start = (bf16[13,8,128]{2,1,0:T(8,128)(2,1)S(1)}, bf16[13,8,128]{2,1,0:T(8,128)(2,1)S(1)}, u32[]{:S(2)}, u32[]{:S(2)}) collective-permute-start(bf16[13,8,128]{2,1,0:T(8,128)(2,1)S(1)} %get-tuple-element.14.sent1), channel_id=1, source_target_pairs={{0,1},{2,3},{1,0},{3,2},{4,5},{6,7},{5,4},{7,6},{8,9},{10,11},{9,8... | collective-permute-start | bytes 79880 | tf_op jit(solution)/shard_map/ppermute | solution.py:433
  2.6 4.6 %collective-permute-start.1 = (bf16[13,8,128]{2,1,0:T(8,128)(2,1)S(1)}, bf16[13,8,128]{2,1,0:T(8,128)(2,1)S(1)}, u32[]{:S(2)}, u32[]{:S(2)}) collective-permute-start(bf16[13,8,128]{2,1,0:T(8,128)(2,1)S(1)} %get-tuple-element.15.sent2), channel_id=1, source_target_pairs={{1,2},{2,1},{5,6},{6,5},{9,10},{10,9},{13,14},{14,13},{17,18},{18,... | collective-permute-start | bytes 79880 | tf_op jit(solution)/shard_map/ppermute | solution.py:432
  7.2 7.6 %collective-permute-start.4 = (bf16[42,8,128]{2,1,0:T(8,128)(2,1)S(1)}, bf16[42,8,128]{2,1,0:T(8,128)(2,1)S(1)}, u32[]{:S(2)}, u32[]{:S(2)}) collective-permute-start(bf16[42,8,128]{2,1,0:T(8,128)(2,1)S(1)} %widen.1), channel_id=1, source_target_pairs={{0,12},{4,8},{8,4},{12,0},{1,13},{5,9},{9,5},{13,1},{2,14},{6,10},... | collective-permute-start | bytes 258056 | tf_op jit(solution)/shard_map/ppermute | solution.py:443
  10.5 5.1 %collective-permute-start.3 = (bf16[42,8,128]{2,1,0:T(8,128)(2,1)S(1)}, bf16[42,8,128]{2,1,0:T(8,128)(2,1)S(1)}, u32[]{:S(2)}, u32[]{:S(2)}) collective-permute-start(bf16[42,8,128]{2,1,0:T(8,128)(2,1)S(1)} %widen.1), channel_id=1, source_target_pairs={{0,8},{4,12},{8,0},{12,4},{1,9},{5,13},{9,1},{13,5},{2,10},{6,14},... | collective-permute-start | bytes 258056 | tf_op jit(solution)/shard_map/ppermute | solution.py:443
  10.7 4.9 %collective-permute-start.2 = (bf16[42,8,128]{2,1,0:T(8,128)(2,1)S(1)}, bf16[42,8,128]{2,1,0:T(8,128)(2,1)S(1)}, u32[]{:S(2)}, u32[]{:S(2)}) collective-permute-start(bf16[42,8,128]{2,1,0:T(8,128)(2,1)S(1)} %widen.1), channel_id=1, source_target_pairs={{0,4},{4,0},{8,12},{12,8},{1,5},{5,1},{9,13},{13,9},{2,6},{6,2},{1... | collective-permute-start | bytes 258056 | tf_op jit(solution)/shard_map/ppermute | solution.py:443

commit v6 on v5

--- a/solution.py
+++ b/solution.py
@@ -185,8 +185,8 @@
 
 
 def mate_kernel(planes, count, *refs):
-    mates = refs[:count]
-    meta, adesc, mean, slope, grads, vel, out, box3, box9, smooth, xs, raw, tb, desc, ys, frc = refs[count:]
+    inner, outer = refs[:count], refs[count:2 * count]
+    meta, adesc, mean, slope, grads, vel, out, box3, box9, smooth, xs, raw, tb, desc, ys, frc = refs[2 * count:]
     nx, nd, nf = planes + 18, planes + 16, planes + 8
     low, high = faces()
     which, dc = meta[0:1, :], meta[16:17, :]
@@ -203,9 +203,11 @@
     smooth[256:384] = wlo
     row = lax.broadcasted_iota(jnp.int32, (8, 128), 0)
 
-    x = mates[0][...]
+    x, y = inner[0][...], outer[0][...]
     for n in range(1, count):
-        x = jnp.where(which == n + 1, mates[n][...], x)
+        x = jnp.where(which == n + 1, inner[n][...], x)
+        y = jnp.where(which == n + 1, outer[n][...], y)
+    x = jnp.concatenate([y[0:80], x, y[80:160]], axis=0)
     for n, d in ((0, 0), (1, 1), (2, -1)):
         take = ones_where((i == j + d + dc) & (j + d >= 0) & (j + d < 128))
         raw[n, pl.ds(8, nx * 8), :] = dot(x, take)
@@ -316,13 +318,13 @@
     )(own.reshape(-1, 128))
 
 
-def mate_part(planes, mates, meta, owned, vel):
+def mate_part(planes, inner, outer, meta, owned, vel):
     nx, nd, nf = planes + 18, planes + 16, planes + 8
-    count = len(mates)
+    count = len(inner)
     return pl.pallas_call(
         functools.partial(mate_kernel, planes, count),
         out_shape=jax.ShapeDtypeStruct(vel.shape, f32),
-        in_specs=[VM] * (count + 6),
+        in_specs=[VM] * (2 * count + 6),
         out_specs=VM,
         scratch_shapes=[
             pltpu.VMEM((256, 128), bf16),
@@ -337,10 +339,10 @@
         ],
         compiler_params=pltpu.CompilerParams(vmem_limit_bytes=16 * 2**20),
         name="mate",
-    )(*[m.reshape(-1, 128) for m in mates], meta, *owned, vel)
-
-
-def advect_kernel(planes, image_hbm, vel_hbm, partner_hbm, offsets_hbm, warp, first, second, meta, image, vel, down, up, partner, offsets, sems):
+    )(*[m.reshape(-1, 128) for m in inner + outer], meta, *owned, vel)
+
+
+def advect_kernel(planes, image_hbm, vel_hbm, partner_hbm, offsets_hbm, warp, inner, first, second, meta, image, vel, down, up, partner, offsets, sems):
     copies = [
         pltpu.make_async_copy(vel_hbm, vel, sems.at[0]),
         pltpu.make_async_copy(image_hbm, image, sems.at[1]),
@@ -373,6 +375,8 @@
             edge = split(y) + split(v) + (image[0, z],)
             for n, part in enumerate(edge):
                 (down if z == 0 else up)[8 + n] = part
+        else:
+            inner[z - 1] = y.astype(bf16)
         if 1 <= z <= 8:
             down[z - 1] = y.astype(bf16)
         if planes - 9 <= z < planes - 1:
@@ -387,7 +391,7 @@
         second[n] = jnp.where(even, down[n], up[n])
 
 
-def widen_kernel(planes, warp, sent1, sent2, got1, got2, out):
+def widen_kernel(planes, warp, sent1, sent2, got1, got2, out, outer):
     low, high = faces()
     even = lax.rem(lax.axis_index("slab"), 2) == 0
     down, up, below, above = (sent2, sent1), (sent1, sent2), (got2, got1), (got1, got2)
@@ -404,16 +408,27 @@
     out[9] = (warp[0] - (ld(down, 10) + ld(down, 11)) * (first - ld(below, 12))).astype(bf16)
     out[9 + top] = (warp[top] - (ld(up, 10) + ld(up, 11)) * (ld(above, 12) - last)).astype(bf16)
 
+    for n in range(10):
+        outer[n] = out[n]
+        outer[10 + n] = out[planes + 8 + n]
+
+
+def from_brains(x, partner):
+    if lax.axis_size("brain") == 4:
+        return [lax.ppermute(x, "brain", [(n, n ^ k) for n in range(4)]) for k in (1, 2, 3)]
+    gathered = lax.all_gather(x, "brain")
+    return [lax.dynamic_index_in_dim(gathered, partner[lax.axis_index("brain")], 0, keepdims=False)]
+
 
 def shards(intensity, velocity, partner, offsets):
     planes = intensity.shape[1]
     slabs, brains = lax.axis_size("slab"), lax.axis_size("brain")
     edge = jax.ShapeDtypeStruct((EDGE, 8, 128), bf16)
-    warp, first, second, meta = pl.pallas_call(
+    warp, inner, first, second, meta = pl.pallas_call(
         functools.partial(advect_kernel, planes),
-        out_shape=(jax.ShapeDtypeStruct((planes, 8, 128), f32), edge, edge, jax.ShapeDtypeStruct((24, 128), jnp.int32)),
+        out_shape=(jax.ShapeDtypeStruct((planes, 8, 128), f32), jax.ShapeDtypeStruct((planes - 2, 8, 128), bf16), edge, edge, jax.ShapeDtypeStruct((24, 128), jnp.int32)),
         in_specs=[HBM] * 4,
-        out_specs=(VM,) * 4,
+        out_specs=(VM,) * 5,
         scratch_shapes=[
             pltpu.VMEM(intensity.shape, bf16),
             pltpu.VMEM(velocity.shape, f32),
@@ -431,20 +446,17 @@
     both_ways = lambda pairs: pairs + [(b, a) for a, b in pairs]
     from_odd = lax.ppermute(second, "slab", both_ways(odd_pairs))
     from_even = lax.ppermute(first, "slab", both_ways(even_pairs))
-    own = pl.pallas_call(
+    inners = from_brains(inner, partner)
+    own, outer = pl.pallas_call(
         functools.partial(widen_kernel, planes),
-        out_shape=jax.ShapeDtypeStruct((planes + 18, 8, 128), bf16),
+        out_shape=(jax.ShapeDtypeStruct((planes + 18, 8, 128), bf16), jax.ShapeDtypeStruct((20, 8, 128), bf16)),
         in_specs=[VM] * 5,
-        out_specs=VM,
+        out_specs=(VM,) * 2,
         compiler_params=pltpu.CompilerParams(vmem_limit_bytes=8 * 2**20),
         name="widen",
     )(warp, first, second, from_even, from_odd)
-    if brains == 4:
-        mates = [lax.ppermute(own, "brain", [(n, n ^ k) for n in range(4)]) for k in (1, 2, 3)]
-    else:
-        gathered = lax.all_gather(own, "brain")
-        mates = [lax.dynamic_index_in_dim(gathered, partner[lax.axis_index("brain")], 0, keepdims=False)]
-    return mate_part(planes, mates, meta, own_part(planes, own), velocity[0])[None]
+    outers = from_brains(outer, partner)
+    return mate_part(planes, inners, outers, meta, own_part(planes, own), velocity[0])[None]
 
 
 def solution(mesh):

time: 21.9 us -> 21.9 us (level)
  waiting for transfers between devices: 3.48 us -> 1.89 us
  starting transfers between devices: 7.01 us -> 8.51 us
    ppermute x3 -> x6, starting transfers between devices: 3.74 us -> 5.3 us  [from_brains(): lax.ppermute(x, 'brain', [(n, n ^ k) for n in range(4)])]
    ppermute x3 -> x6, waiting for transfers between devices: 0.82 us -> 0.02 us  [from_brains(): lax.ppermute(x, 'brain', [(n, n ^ k) for n in range(4)])]
    ppermute x1, waiting for transfers between devices: 2.65 us -> 1.88 us  [shards(): from_odd = lax.ppermute(second, 'slab', both_ways(odd_pairs))]
  transfers between devices with their start and end apart: 5 -> 8, of which waited for: 2 -> 1; matrix products, arithmetic and copies ran while one was open for 0% -> 0% of each run, Pallas kernels for 18% -> 18%
where the time goes in v6:
time: 21.9 us; the launch traced here: 21.7 us
  Pallas kernels  11.3 us (52%)
  starting transfers between devices  8.51 us (39%)
  waiting for transfers between devices  1.89 us (9%)
    pallas_call x1, Pallas kernels, mate_part(): pl.pallas_call(functools.partial(mate_kernel, planes, count), out_shape=j...  6.18 us
    ppermute x6, starting transfers between devices, from_brains(): lax.ppermute(x, 'brain', [(n, n ^ k) for n in range(4)])  5.3 us
    pallas_call x1, Pallas kernels, own_part(): pl.pallas_call(functools.partial(own_kernel, planes), out_shape=(shape((1...  3.82 us
    ppermute x1, starting transfers between devices, shards(): from_odd = lax.ppermute(second, 'slab', both_ways(odd_pairs))  1.91 us
    ppermute x1, waiting for transfers between devices, shards(): from_odd = lax.ppermute(second, 'slab', both_ways(odd_pairs))  1.88 us
    ppermute x1, starting transfers between devices, shards(): from_even = lax.ppermute(first, 'slab', both_ways(even_pairs))  1.3 us
    pallas_call x1, Pallas kernels, shards(): pl.pallas_call(functools.partial(advect_kernel, planes), out_shape=(jax.S...  1.22 us
  transfers between devices with their start and end apart: 8, of which 1 were waited for; matrix products, arithmetic and copies ran while one was open for 0% of the time, Pallas kernels for 18%

profile of v6, /device:TPU:17, one launch (start us, length us, event | category | flops | bytes accessed | tf_op | source)
XLA Modules:
  0.0 21.7 jit_solution(15329505451989700566)
XLA Ops:
  0.0 0.0 copy-start
  0.0 1.2 %advect.1 = (f32[24,8,128]{2,1,0:T(8,128)S(1)}, bf16[22,8,128]{2,1,0:T(8,128)(2,1)S(1)}, bf16[13,8,128]{2,1,0:T(8,128)(2,1)S(1)}, bf16[13,8,128]{2,1,0:T(8,128)(2,1)S(1)}, s32[24,128]{1,0:T(8,128)S(1)}) custom-call(bf16[1,24,8,128]{3,2,1,0:T(8,128)(2,1)} %image_hbm.1, f32[1,3,24,8,128]{4,3,2,1,0:T(8,128)} %vel_hbm.1, s32[4]{0:T(128)} %partner_hbm.1, ...), custom_call_target="tpu_custom_call" | custom-call | tf_op jit(solution)/shard_map/advect/pallas_call | solution.py:427
  1.2 1.8 %collective-permute-start.2 = (bf16[22,8,128]{2,1,0:T(8,128)(2,1)S(1)}, bf16[22,8,128]{2,1,0:T(8,128)(2,1)S(1)}, u32[]{:S(2)}, u32[]{:S(2)}) collective-permute-start(bf16[22,8,128]{2,1,0:T(8,128)(2,1)S(1)} %get-tuple-element.16), channel_id=1, source_target_pairs={{0,12},{4,8},{8,4},{12,0},{1,13},{5,9},{9,5},{13,1},{2,14},{6,10},... | collective-permute-start | bytes 135176 | tf_op jit(solution)/shard_map/ppermute | solution.py:418
  3.1 1.3 %collective-permute-start.3 = (bf16[13,8,128]{2,1,0:T(8,128)(2,1)S(1)}, bf16[13,8,128]{2,1,0:T(8,128)(2,1)S(1)}, u32[]{:S(2)}, u32[]{:S(2)}) collective-permute-start(bf16[13,8,128]{2,1,0:T(8,128)(2,1)S(1)} %get-tuple-element.18.sent1), channel_id=1, source_target_pairs={{0,1},{2,3},{1,0},{3,2},{4,5},{6,7},{5,4},{7,6},{8,9},{10,11},{9,8... | collective-permute-start | bytes 79880 | tf_op jit(solution)/shard_map/ppermute | solution.py:448
  4.4 1.9 %collective-permute-start.4 = (bf16[13,8,128]{2,1,0:T(8,128)(2,1)S(1)}, bf16[13,8,128]{2,1,0:T(8,128)(2,1)S(1)}, u32[]{:S(2)}, u32[]{:S(2)}) collective-permute-start(bf16[13,8,128]{2,1,0:T(8,128)(2,1)S(1)} %get-tuple-element.19.sent2), channel_id=1, source_target_pairs={{1,2},{2,1},{5,6},{6,5},{9,10},{10,9},{13,14},{14,13},{17,18},{18,... | collective-permute-start | bytes 79880 | tf_op jit(solution)/shard_map/ppermute | solution.py:447
  6.3 0.3 %collective-permute-start.1 = (bf16[22,8,128]{2,1,0:T(8,128)(2,1)S(1)}, bf16[22,8,128]{2,1,0:T(8,128)(2,1)S(1)}, u32[]{:S(2)}, u32[]{:S(2)}) collective-permute-start(bf16[22,8,128]{2,1,0:T(8,128)(2,1)S(1)} %get-tuple-element.16), channel_id=1, source_target_pairs={{0,8},{4,12},{8,0},{12,4},{1,9},{5,13},{9,1},{13,5},{2,10},{6,14},... | collective-permute-start | bytes 135176 | tf_op jit(solution)/shard_map/ppermute | solution.py:418
  6.6 0.5 %collective-permute-start = (bf16[22,8,128]{2,1,0:T(8,128)(2,1)S(1)}, bf16[22,8,128]{2,1,0:T(8,128)(2,1)S(1)}, u32[]{:S(2)}, u32[]{:S(2)}) collective-permute-start(bf16[22,8,128]{2,1,0:T(8,128)(2,1)S(1)} %get-tuple-element.16), channel_id=1, source_target_pairs={{0,4},{4,0},{8,12},{12,8},{1,5},{5,1},{9,13},{13,9},{2,6},{6,2},{1... | collective-permute-start | bytes 135176 | tf_op jit(solution)/shard_map/ppermute | solution.py:418
  7.1 0.0 collective-permute-done.3.got1
  7.1 1.9 %collective-permute-done.4.got2 = bf16[13,8,128]{2,1,0:T(8,128)(2,1)S(1)} collective-permute-done((bf16[13,8,128]{2,1,0:T(8,128)(2,1)S(1)}, bf16[13,8,128]{2,1,0:T(8,128)(2,1)S(1)}, u32[]{:S(2)}, u32[]{:S(2)}) %collective-permute-start.4) | collective-permute-done | bytes 26656 | tf_op jit(solution)/shard_map/ppermute | solution.py:447
  9.0 1.5 %collective-permute-start.7 = (bf16[20,8,128]{2,1,0:T(8,128)(2,1)S(1)}, bf16[20,8,128]{2,1,0:T(8,128)(2,1)S(1)}, u32[]{:S(2)}, u32[]{:S(2)}) collective-permute-start(bf16[20,8,128]{2,1,0:T(8,128)(2,1)S(1)} %get-tuple-element.20), channel_id=1, source_target_pairs={{0,12},{4,8},{8,4},{12,0},{1,13},{5,9},{9,5},{13,1},{2,14},{6,10},... | collective-permute-start | bytes 122888 | tf_op jit(solution)/shard_map/ppermute | solution.py:418
  10.6 1.1 %collective-permute-start.6 = (bf16[20,8,128]{2,1,0:T(8,128)(2,1)S(1)}, bf16[20,8,128]{2,1,0:T(8,128)(2,1)S(1)}, u32[]{:S(2)}, u32[]{:S(2)}) collective-permute-start(bf16[20,8,128]{2,1,0:T(8,128)(2,1)S(1)} %get-tuple-element.20), channel_id=1, source_target_pairs={{0,8},{4,12},{8,0},{12,4},{1,9},{5,13},{9,1},{13,5},{2,10},{6,14},... | collective-permute-start | bytes 122888 | tf_op jit(solution)/shard_map/ppermute | solution.py:418
  11.7 0.0 collective-permute-done.2
  11.7 0.0 collective-permute-start.5
  11.7 3.8 %own.1 = (f32[12,376,128]{2,1,0:T(8,128)S(1)}, f32[12,256,128]{2,1,0:T(8,128)S(1)}, f32[12,256,128]{2,1,0:T(8,128)S(1)}, f32[3,12,256,128]{3,2,1,0:T(8,128)S(1)}) custom-call(bf16[336,128]{1,0:T(8,128)(2,1)S(1)} %bitcast.17), custom_call_target="tpu_custom_call" | custom-call | flops 600000000 | bytes 16777216 | tf_op jit(solution)/shard_map/own/pallas_call | solution.py:297
  15.5 0.0 collective-permute-done.1
  15.5 0.0 collective-permute-done
  15.5 0.0 collective-permute-done.7
  15.5 0.0 collective-permute-done.6
  15.5 0.0 collective-permute-done.5
  15.6 0.0 copy-done
  15.6 6.2 %mate.1 = f32[3,24,8,128]{3,2,1,0:T(8,128)} custom-call(bf16[176,128]{1,0:T(8,128)(2,1)S(1)} %bitcast.13, bf16[176,128]{1,0:T(8,128)(2,1)S(1)} %bitcast.12, bf16[176,128]{1,0:T(8,128)(2,1)S(1)} %bitcast.11, bf16[160,128]{1,0:T(8,128)(2,1)S(1)} %bitcast.16, bf16[160,128]{1,0:T(8,128)(2,1)S(1)} %bitcast.15, bf16[160,128]{1,0:T(8,128)(2,1)S(1)} %bitcast.14, ...), custom_call_target="tpu_custom_call" | custom-call | tf_op jit(solution)/shard_map/mate/pallas_call | solution.py:324
  (1 shorter events, 0.0 us)
Async XLA Ops:
  0.0 15.6 %copy-start = (f32[1,3,24,8,128]{4,3,2,1,0:T(8,128)S(1)}, f32[1,3,24,8,128]{4,3,2,1,0:T(8,128)}, u32[]{:S(2)}) copy-start(f32[1,3,24,8,128]{4,3,2,1,0:T(8,128)} %vel_hbm.1) | copy-start | bytes 884740
  1.2 10.4 %collective-permute-start.2 = (bf16[22,8,128]{2,1,0:T(8,128)(2,1)S(1)}, bf16[22,8,128]{2,1,0:T(8,128)(2,1)S(1)}, u32[]{:S(2)}, u32[]{:S(2)}) collective-permute-start(bf16[22,8,128]{2,1,0:T(8,128)(2,1)S(1)} %get-tuple-element.16), channel_id=1, source_target_pairs={{0,12},{4,8},{8,4},{12,0},{1,13},{5,9},{9,5},{13,1},{2,14},{6,10},... | collective-permute-start | bytes 135176 | tf_op jit(solution)/shard_map/ppermute | solution.py:418
  3.1 4.0 %collective-permute-start.3 = (bf16[13,8,128]{2,1,0:T(8,128)(2,1)S(1)}, bf16[13,8,128]{2,1,0:T(8,128)(2,1)S(1)}, u32[]{:S(2)}, u32[]{:S(2)}) collective-permute-start(bf16[13,8,128]{2,1,0:T(8,128)(2,1)S(1)} %get-tuple-element.18.sent1), channel_id=1, source_target_pairs={{0,1},{2,3},{1,0},{3,2},{4,5},{6,7},{5,4},{7,6},{8,9},{10,11},{9,8... | collective-permute-start | bytes 79880 | tf_op jit(solution)/shard_map/ppermute | solution.py:448
  4.4 4.6 %collective-permute-start.4 = (bf16[13,8,128]{2,1,0:T(8,128)(2,1)S(1)}, bf16[13,8,128]{2,1,0:T(8,128)(2,1)S(1)}, u32[]{:S(2)}, u32[]{:S(2)}) collective-permute-start(bf16[13,8,128]{2,1,0:T(8,128)(2,1)S(1)} %get-tuple-element.19.sent2), channel_id=1, source_target_pairs={{1,2},{2,1},{5,6},{6,5},{9,10},{10,9},{13,14},{14,13},{17,18},{18,... | collective-permute-start | bytes 79880 | tf_op jit(solution)/shard_map/ppermute | solution.py:447
  6.3 9.2 %collective-permute-start.1 = (bf16[22,8,128]{2,1,0:T(8,128)(2,1)S(1)}, bf16[22,8,128]{2,1,0:T(8,128)(2,1)S(1)}, u32[]{:S(2)}, u32[]{:S(2)}) collective-permute-start(bf16[22,8,128]{2,1,0:T(8,128)(2,1)S(1)} %get-tuple-element.16), channel_id=1, source_target_pairs={{0,8},{4,12},{8,0},{12,4},{1,9},{5,13},{9,1},{13,5},{2,10},{6,14},... | collective-permute-start | bytes 135176 | tf_op jit(solution)/shard_map/ppermute | solution.py:418
  6.6 8.9 %collective-permute-start = (bf16[22,8,128]{2,1,0:T(8,128)(2,1)S(1)}, bf16[22,8,128]{2,1,0:T(8,128)(2,1)S(1)}, u32[]{:S(2)}, u32[]{:S(2)}) collective-permute-start(bf16[22,8,128]{2,1,0:T(8,128)(2,1)S(1)} %get-tuple-element.16), channel_id=1, source_target_pairs={{0,4},{4,0},{8,12},{12,8},{1,5},{5,1},{9,13},{13,9},{2,6},{6,2},{1... | collective-permute-start | bytes 135176 | tf_op jit(solution)/shard_map/ppermute | solution.py:418
  9.0 6.5 %collective-permute-start.7 = (bf16[20,8,128]{2,1,0:T(8,128)(2,1)S(1)}, bf16[20,8,128]{2,1,0:T(8,128)(2,1)S(1)}, u32[]{:S(2)}, u32[]{:S(2)}) collective-permute-start(bf16[20,8,128]{2,1,0:T(8,128)(2,1)S(1)} %get-tuple-element.20), channel_id=1, source_target_pairs={{0,12},{4,8},{8,4},{12,0},{1,13},{5,9},{9,5},{13,1},{2,14},{6,10},... | collective-permute-start | bytes 122888 | tf_op jit(solution)/shard_map/ppermute | solution.py:418
  10.6 5.0 %collective-permute-start.6 = (bf16[20,8,128]{2,1,0:T(8,128)(2,1)S(1)}, bf16[20,8,128]{2,1,0:T(8,128)(2,1)S(1)}, u32[]{:S(2)}, u32[]{:S(2)}) collective-permute-start(bf16[20,8,128]{2,1,0:T(8,128)(2,1)S(1)} %get-tuple-element.20), channel_id=1, source_target_pairs={{0,8},{4,12},{8,0},{12,4},{1,9},{5,13},{9,1},{13,5},{2,10},{6,14},... | collective-permute-start | bytes 122888 | tf_op jit(solution)/shard_map/ppermute | solution.py:418
  11.7 3.9 %collective-permute-start.5 = (bf16[20,8,128]{2,1,0:T(8,128)(2,1)S(1)}, bf16[20,8,128]{2,1,0:T(8,128)(2,1)S(1)}, u32[]{:S(2)}, u32[]{:S(2)}) collective-permute-start(bf16[20,8,128]{2,1,0:T(8,128)(2,1)S(1)} %get-tuple-element.20), channel_id=1, source_target_pairs={{0,4},{4,0},{8,12},{12,8},{1,5},{5,1},{9,13},{13,9},{2,6},{6,2},{1... | collective-permute-start | bytes 122888 | tf_op jit(solution)/shard_map/ppermute | solution.py:418

commit v7 on v6

--- a/solution.py
+++ b/solution.py
@@ -43,6 +43,10 @@
     one = jnp.float32(1.0)
     zero = jnp.float32(0.0)
     return jnp.where(slab > 0, one, zero), jnp.where(slab < lax.axis_size("slab") - 1, one, zero)
+
+
+def even_slab():
+    return lax.rem(lax.axis_index("slab"), 2) == 0
 
 
 def row_inside(d):
@@ -207,7 +211,10 @@
     for n in range(1, count):
         x = jnp.where(which == n + 1, inner[n][...], x)
         y = jnp.where(which == n + 1, outer[n][...], y)
-    x = jnp.concatenate([y[0:80], x, y[80:160]], axis=0)
+    middle = (planes - 2) * 8
+    even = even_slab()
+    x, side = x[0:middle], x[middle:middle + 80]
+    x = jnp.concatenate([jnp.where(even, y, side), x, jnp.where(even, side, y)], axis=0)
     for n, d in ((0, 0), (1, 1), (2, -1)):
         take = ones_where((i == j + d + dc) & (j + d >= 0) & (j + d < 128))
         raw[n, pl.ds(8, nx * 8), :] = dot(x, take)
@@ -313,7 +320,7 @@
             pltpu.VMEM((2 * UNROLL, nf * PITCH + SPARE, 128), f32),
         ],
         compiler_params=pltpu.CompilerParams(vmem_limit_bytes=16 * 2**20),
-        cost_estimate=pl.CostEstimate(flops=6 * 10**8, bytes_accessed=16 * 2**20, transcendentals=10**6),
+        cost_estimate=pl.CostEstimate(flops=10**6, bytes_accessed=2**16, transcendentals=0),
         name="own",
     )(own.reshape(-1, 128))
 
@@ -342,7 +349,7 @@
     )(*[m.reshape(-1, 128) for m in inner + outer], meta, *owned, vel)
 
 
-def advect_kernel(planes, image_hbm, vel_hbm, partner_hbm, offsets_hbm, warp, inner, first, second, meta, image, vel, down, up, partner, offsets, sems):
+def advect_kernel(planes, image_hbm, vel_hbm, partner_hbm, offsets_hbm, warp, first, second, meta, image, vel, down, up, partner, offsets, sems):
     copies = [
         pltpu.make_async_copy(vel_hbm, vel, sems.at[0]),
         pltpu.make_async_copy(image_hbm, image, sems.at[1]),
@@ -375,8 +382,6 @@
             edge = split(y) + split(v) + (image[0, z],)
             for n, part in enumerate(edge):
                 (down if z == 0 else up)[8 + n] = part
-        else:
-            inner[z - 1] = y.astype(bf16)
         if 1 <= z <= 8:
             down[z - 1] = y.astype(bf16)
         if planes - 9 <= z < planes - 1:
@@ -385,37 +390,56 @@
     mate = partner[me]
     for n, value in enumerate((me ^ mate, offsets[0, mate] - offsets[0, me], offsets[1, mate] - offsets[1, me])):
         meta[n * 8:n * 8 + 8, :] = jnp.full((8, 128), value, jnp.int32)
-    even = lax.rem(lax.axis_index("slab"), 2) == 0
+    even = even_slab()
     for n in range(EDGE):
         first[n] = jnp.where(even, up[n], down[n])
         second[n] = jnp.where(even, down[n], up[n])
 
 
-def widen_kernel(planes, warp, sent1, sent2, got1, got2, out, outer):
+def face_planes(planes, warp, mine, got, put, bottom):
+    ld = lambda ref, n: ref[n].astype(f32)
+    v, x0, x1 = ld(mine, 10) + ld(mine, 11), ld(mine, 12), ld(got, 12)
+    w = ld(got, 10) + ld(got, 11)
+    here = jnp.where(bottom, warp[0], warp[planes - 1])
+    step = jnp.where(bottom, x0 - x1, x1 - x0)
+    near = here - v * step
+    far = (ld(got, 8) + ld(got, 9)) - w * step
     low, high = faces()
-    even = lax.rem(lax.axis_index("slab"), 2) == 0
-    down, up, below, above = (sent2, sent1), (sent1, sent2), (got2, got1), (got1, got2)
-    ld = lambda pair, n: jnp.where(even, pair[0][n], pair[1][n]).astype(f32)
-    top = planes - 1
-    first, last = ld(down, 12), ld(up, 12)
-    for n in range(8):
-        out[n] = (ld(below, n) * low).astype(bf16)
-        out[planes + 10 + n] = (ld(above, n) * high).astype(bf16)
-    out[8] = (low * ((ld(below, 8) + ld(below, 9)) - (ld(below, 10) + ld(below, 11)) * (first - ld(below, 12)))).astype(bf16)
-    out[planes + 9] = (high * ((ld(above, 8) + ld(above, 9)) - (ld(above, 10) + ld(above, 11)) * (ld(above, 12) - last))).astype(bf16)
-    for z in range(1, top):
-        out[9 + z] = warp[z].astype(bf16)
-    out[9] = (warp[0] - (ld(down, 10) + ld(down, 11)) * (first - ld(below, 12))).astype(bf16)
-    out[9 + top] = (warp[top] - (ld(up, 10) + ld(up, 11)) * (ld(above, 12) - last)).astype(bf16)
-
+    scale = jnp.where(bottom, low, high)
+    planes_got = [ld(got, n) * scale for n in range(8)]
+    up = [near, far * scale] + planes_got
+    down = planes_got + [far * scale, near]
     for n in range(10):
-        outer[n] = out[n]
-        outer[10 + n] = out[planes + 8 + n]
-
-
-def from_brains(x, partner):
+        put(n, jnp.where(bottom, down[n], up[n]).astype(bf16))
+
+
+def widen_even_kernel(planes, warp, mine, got, out):
+    for z in range(1, planes - 1):
+        out[z - 1] = warp[z].astype(bf16)
+
+    def put(n, value):
+        out[planes - 2 + n] = value
+    face_planes(planes, warp, mine, got, put, jnp.logical_not(even_slab()))
+
+
+def widen_odd_kernel(planes, warp, mine, got, most, own, outer):
+    even = even_slab()
+
+    def put(n, value):
+        outer[n] = value
+    face_planes(planes, warp, mine, got, put, even)
+    for z in range(planes - 2):
+        own[10 + z] = most[z]
+    for n in range(10):
+        a, b = outer[n], most[planes - 2 + n]
+        own[n] = jnp.where(even, a, b)
+        own[planes + 8 + n] = jnp.where(even, b, a)
+
+
+def from_brains(x, partner, order=(1, 2, 3)):
     if lax.axis_size("brain") == 4:
-        return [lax.ppermute(x, "brain", [(n, n ^ k) for n in range(4)]) for k in (1, 2, 3)]
+        got = {k: lax.ppermute(x, "brain", [(n, n ^ k) for n in range(4)]) for k in order}
+        return [got[k] for k in (1, 2, 3)]
     gathered = lax.all_gather(x, "brain")
     return [lax.dynamic_index_in_dim(gathered, partner[lax.axis_index("brain")], 0, keepdims=False)]
 
@@ -424,11 +448,11 @@
     planes = intensity.shape[1]
     slabs, brains = lax.axis_size("slab"), lax.axis_size("brain")
     edge = jax.ShapeDtypeStruct((EDGE, 8, 128), bf16)
-    warp, inner, first, second, meta = pl.pallas_call(
+    warp, first, second, meta = pl.pallas_call(
         functools.partial(advect_kernel, planes),
-        out_shape=(jax.ShapeDtypeStruct((planes, 8, 128), f32), jax.ShapeDtypeStruct((planes - 2, 8, 128), bf16), edge, edge, jax.ShapeDtypeStruct((24, 128), jnp.int32)),
+        out_shape=(jax.ShapeDtypeStruct((planes, 8, 128), f32), edge, edge, jax.ShapeDtypeStruct((24, 128), jnp.int32)),
         in_specs=[HBM] * 4,
-        out_specs=(VM,) * 5,
+        out_specs=(VM,) * 4,
         scratch_shapes=[
             pltpu.VMEM(intensity.shape, bf16),
             pltpu.VMEM(velocity.shape, f32),
@@ -446,16 +470,25 @@
     both_ways = lambda pairs: pairs + [(b, a) for a, b in pairs]
     from_odd = lax.ppermute(second, "slab", both_ways(odd_pairs))
     from_even = lax.ppermute(first, "slab", both_ways(even_pairs))
-    inners = from_brains(inner, partner)
+    small = pltpu.CompilerParams(vmem_limit_bytes=8 * 2**20)
+    most = pl.pallas_call(
+        functools.partial(widen_even_kernel, planes),
+        out_shape=jax.ShapeDtypeStruct((planes + 8, 8, 128), bf16),
+        in_specs=[VM] * 3,
+        out_specs=VM,
+        compiler_params=small,
+        name="widen_even",
+    )(warp, first, from_even)
+    inners = from_brains(most, partner)
     own, outer = pl.pallas_call(
-        functools.partial(widen_kernel, planes),
-        out_shape=(jax.ShapeDtypeStruct((planes + 18, 8, 128), bf16), jax.ShapeDtypeStruct((20, 8, 128), bf16)),
-        in_specs=[VM] * 5,
+        functools.partial(widen_odd_kernel, planes),
+        out_shape=(jax.ShapeDtypeStruct((planes + 18, 8, 128), bf16), jax.ShapeDtypeStruct((10, 8, 128), bf16)),
+        in_specs=[VM] * 4,
         out_specs=(VM,) * 2,
-        compiler_params=pltpu.CompilerParams(vmem_limit_bytes=8 * 2**20),
-        name="widen",
-    )(warp, first, second, from_even, from_odd)
-    outers = from_brains(outer, partner)
+        compiler_params=small,
+        name="widen_odd",
+    )(warp, second, from_odd, most)
+    outers = from_brains(outer, partner, (3, 2, 1))
     return mate_part(planes, inners, outers, meta, own_part(planes, own), velocity[0])[None]
 
 

time: 21.9 us -> 24.4 us (1.11)
  the two profiles are of different devices: /device:TPU:17 before, /device:TPU:13 now
where the time goes in v7:
time: 24.4 us; the launch traced here: 24.3 us
  Pallas kernels  11.2 us (46%)
  starting transfers between devices  9.53 us (39%)
  waiting for transfers between devices  2.5 us (10%)
  local copies, waits for them, and re-layouts  0.96 us (4%)
    pallas_call x1, Pallas kernels, mate_part(): pl.pallas_call(functools.partial(mate_kernel, planes, count), out_shape=j...  6.17 us
    ppermute x6, starting transfers between devices, from_brains(): lax.ppermute(x, 'brain', [(n, n ^ k) for n in range(4)])  4.97 us
    ppermute x1, starting transfers between devices, shards(): from_odd = lax.ppermute(second, 'slab', both_ways(odd_pairs))  4.32 us
    pallas_call x1, Pallas kernels, own_part(): pl.pallas_call(functools.partial(own_kernel, planes), out_shape=(shape((1...  3.83 us
    ppermute x6, waiting for transfers between devices, from_brains(): lax.ppermute(x, 'brain', [(n, n ^ k) for n in range(4)])  2.49 us
    pallas_call x1, Pallas kernels, shards(): pl.pallas_call(functools.partial(advect_kernel, planes), out_shape=(jax.S...  1.15 us
    unnamed x2, local copies, waits for them, and re-layouts  0.96 us
  transfers between devices with their start and end apart: 8, of which 1 were waited for; matrix products, arithmetic and copies ran while one was open for 0% of the time, Pallas kernels for 16%

profile of v7, /device:TPU:13, one launch (start us, length us, event | category | flops | bytes accessed | tf_op | source)
XLA Modules:
  0.0 24.3 jit_solution(17304495067878475467)
XLA Ops:
  0.0 1.2 %advect.1 = (f32[24,8,128]{2,1,0:T(8,128)S(1)}, bf16[13,8,128]{2,1,0:T(8,128)(2,1)S(1)}, bf16[13,8,128]{2,1,0:T(8,128)(2,1)S(1)}, s32[24,128]{1,0:T(8,128)S(1)}) custom-call(bf16[1,24,8,128]{3,2,1,0:T(8,128)(2,1)} %image_hbm.1, f32[1,3,24,8,128]{4,3,2,1,0:T(8,128)} %vel_hbm.1, s32[4]{0:T(128)} %partner_hbm.1, s32[2,4]{1,0:T(2,128)} %bitcast.18), custom_call_target="tpu_custom_call" | custom-call | tf_op jit(solution)/shard_map/advect/pallas_call | solution.py:451
  1.2 0.2 collective-permute-start
  1.4 4.3 %collective-permute-start.4 = (bf16[13,8,128]{2,1,0:T(8,128)(2,1)S(1)}, bf16[13,8,128]{2,1,0:T(8,128)(2,1)S(1)}, u32[]{:S(2)}, u32[]{:S(2)}) collective-permute-start(bf16[13,8,128]{2,1,0:T(8,128)(2,1)S(1)} %get-tuple-element.17.mine), channel_id=1, source_target_pairs={{1,2},{2,1},{5,6},{6,5},{9,10},{10,9},{13,14},{14,13},{17,18},{18,... | collective-permute-start | bytes 79880 | tf_op jit(solution)/shard_map/ppermute | solution.py:471
  5.7 0.0 collective-permute-done.got
  5.8 2.4 %collective-permute-start.3 = (bf16[32,8,128]{2,1,0:T(8,128)(2,1)S(1)}, bf16[32,8,128]{2,1,0:T(8,128)(2,1)S(1)}, u32[]{:S(2)}, u32[]{:S(2)}) collective-permute-start(bf16[32,8,128]{2,1,0:T(8,128)(2,1)S(1)} %widen_even.1.most), channel_id=1, source_target_pairs={{0,12},{4,8},{8,4},{12,0},{1,13},{5,9},{9,5},{13,1},{2,14},{6,10},... | collective-permute-start | bytes 196616 | tf_op jit(solution)/shard_map/ppermute | solution.py:441
  8.2 0.3 %collective-permute-start.2 = (bf16[32,8,128]{2,1,0:T(8,128)(2,1)S(1)}, bf16[32,8,128]{2,1,0:T(8,128)(2,1)S(1)}, u32[]{:S(2)}, u32[]{:S(2)}) collective-permute-start(bf16[32,8,128]{2,1,0:T(8,128)(2,1)S(1)} %widen_even.1.most), channel_id=1, source_target_pairs={{0,8},{4,12},{8,0},{12,4},{1,9},{5,13},{9,1},{13,5},{2,10},{6,14},... | collective-permute-start | bytes 196616 | tf_op jit(solution)/shard_map/ppermute | solution.py:441
  8.4 0.2 collective-permute-start.1
  8.6 0.0 collective-permute-done.4.got
  8.7 1.5 %collective-permute-start.7 = (bf16[10,8,128]{2,1,0:T(8,128)(2,1)S(1)}, bf16[10,8,128]{2,1,0:T(8,128)(2,1)S(1)}, u32[]{:S(2)}, u32[]{:S(2)}) collective-permute-start(bf16[10,8,128]{2,1,0:T(8,128)(2,1)S(1)} %get-tuple-element.18), channel_id=1, source_target_pairs={{0,12},{4,8},{8,4},{12,0},{1,13},{5,9},{9,5},{13,1},{2,14},{6,10},... | collective-permute-start | bytes 61448 | tf_op jit(solution)/shard_map/ppermute | solution.py:441
  10.1 0.3 %collective-permute-start.6 = (bf16[10,8,128]{2,1,0:T(8,128)(2,1)S(1)}, bf16[10,8,128]{2,1,0:T(8,128)(2,1)S(1)}, u32[]{:S(2)}, u32[]{:S(2)}) collective-permute-start(bf16[10,8,128]{2,1,0:T(8,128)(2,1)S(1)} %get-tuple-element.18), channel_id=1, source_target_pairs={{0,8},{4,12},{8,0},{12,4},{1,9},{5,13},{9,1},{13,5},{2,10},{6,14},... | collective-permute-start | bytes 61448 | tf_op jit(solution)/shard_map/ppermute | solution.py:441
  10.4 2.5 %collective-permute-done.7 = bf16[10,8,128]{2,1,0:T(8,128)(2,1)S(1)} collective-permute-done((bf16[10,8,128]{2,1,0:T(8,128)(2,1)S(1)}, bf16[10,8,128]{2,1,0:T(8,128)(2,1)S(1)}, u32[]{:S(2)}, u32[]{:S(2)}) %collective-permute-start.7) | collective-permute-done | bytes 20512 | tf_op jit(solution)/shard_map/ppermute | solution.py:441
  12.9 0.4 %collective-permute-start.5 = (bf16[10,8,128]{2,1,0:T(8,128)(2,1)S(1)}, bf16[10,8,128]{2,1,0:T(8,128)(2,1)S(1)}, u32[]{:S(2)}, u32[]{:S(2)}) collective-permute-start(bf16[10,8,128]{2,1,0:T(8,128)(2,1)S(1)} %get-tuple-element.18), channel_id=1, source_target_pairs={{0,4},{4,0},{8,12},{12,8},{1,5},{5,1},{9,13},{13,9},{2,6},{6,2},{1... | collective-permute-start | bytes 61448 | tf_op jit(solution)/shard_map/ppermute | solution.py:441
  13.2 3.8 %own.1 = (f32[12,376,128]{2,1,0:T(8,128)S(1)}, f32[12,256,128]{2,1,0:T(8,128)S(1)}, f32[12,256,128]{2,1,0:T(8,128)S(1)}, f32[3,12,256,128]{3,2,1,0:T(8,128)S(1)}) custom-call(bf16[336,128]{1,0:T(8,128)(2,1)S(1)} %bitcast.11), custom_call_target="tpu_custom_call" | custom-call | flops 1000000 | bytes 65536 | tf_op jit(solution)/shard_map/own/pallas_call | solution.py:304
  17.1 0.0 collective-permute-done.6
  17.1 0.0 collective-permute-done.5
  17.1 0.0 collective-permute-done.3
  17.1 0.0 collective-permute-done.2
  17.1 0.0 collective-permute-done.1
  17.1 0.0 copy-start
  17.1 1.0 %copy-done = f32[1,3,24,8,128]{4,3,2,1,0:T(8,128)S(1)} copy-done((f32[1,3,24,8,128]{4,3,2,1,0:T(8,128)S(1)}, f32[1,3,24,8,128]{4,3,2,1,0:T(8,128)}, u32[]{:S(2)}) %copy-start) | copy-done | bytes 294936
  18.1 6.2 %mate.1 = f32[3,24,8,128]{3,2,1,0:T(8,128)} custom-call(bf16[256,128]{1,0:T(8,128)(2,1)S(1)} %bitcast.14, bf16[256,128]{1,0:T(8,128)(2,1)S(1)} %bitcast.13, bf16[256,128]{1,0:T(8,128)(2,1)S(1)} %bitcast.12, bf16[80,128]{1,0:T(8,128)(2,1)S(1)} %bitcast.17, bf16[80,128]{1,0:T(8,128)(2,1)S(1)} %bitcast.16, bf16[80,128]{1,0:T(8,128)(2,1)S(1)} %bitcast.15, ...), custom_call_target="tpu_custom_call" | custom-call | tf_op jit(solution)/shard_map/mate/pallas_call | solution.py:331
  (2 shorter events, 0.0 us)
Async XLA Ops:
  1.2 4.6 %collective-permute-start = (bf16[13,8,128]{2,1,0:T(8,128)(2,1)S(1)}, bf16[13,8,128]{2,1,0:T(8,128)(2,1)S(1)}, u32[]{:S(2)}, u32[]{:S(2)}) collective-permute-start(bf16[13,8,128]{2,1,0:T(8,128)(2,1)S(1)} %get-tuple-element.16.mine), channel_id=1, source_target_pairs={{0,1},{2,3},{1,0},{3,2},{4,5},{6,7},{5,4},{7,6},{8,9},{10,11},{9,8... | collective-permute-start | bytes 79880 | tf_op jit(solution)/shard_map/ppermute | solution.py:472
  1.4 7.2 %collective-permute-start.4 = (bf16[13,8,128]{2,1,0:T(8,128)(2,1)S(1)}, bf16[13,8,128]{2,1,0:T(8,128)(2,1)S(1)}, u32[]{:S(2)}, u32[]{:S(2)}) collective-permute-start(bf16[13,8,128]{2,1,0:T(8,128)(2,1)S(1)} %get-tuple-element.17.mine), channel_id=1, source_target_pairs={{1,2},{2,1},{5,6},{6,5},{9,10},{10,9},{13,14},{14,13},{17,18},{18,... | collective-permute-start | bytes 79880 | tf_op jit(solution)/shard_map/ppermute | solution.py:471
  5.8 11.3 %collective-permute-start.3 = (bf16[32,8,128]{2,1,0:T(8,128)(2,1)S(1)}, bf16[32,8,128]{2,1,0:T(8,128)(2,1)S(1)}, u32[]{:S(2)}, u32[]{:S(2)}) collective-permute-start(bf16[32,8,128]{2,1,0:T(8,128)(2,1)S(1)} %widen_even.1.most), channel_id=1, source_target_pairs={{0,12},{4,8},{8,4},{12,0},{1,13},{5,9},{9,5},{13,1},{2,14},{6,10},... | collective-permute-start | bytes 196616 | tf_op jit(solution)/shard_map/ppermute | solution.py:441
  8.2 9.0 %collective-permute-start.2 = (bf16[32,8,128]{2,1,0:T(8,128)(2,1)S(1)}, bf16[32,8,128]{2,1,0:T(8,128)(2,1)S(1)}, u32[]{:S(2)}, u32[]{:S(2)}) collective-permute-start(bf16[32,8,128]{2,1,0:T(8,128)(2,1)S(1)} %widen_even.1.most), channel_id=1, source_target_pairs={{0,8},{4,12},{8,0},{12,4},{1,9},{5,13},{9,1},{13,5},{2,10},{6,14},... | collective-permute-start | bytes 196616 | tf_op jit(solution)/shard_map/ppermute | solution.py:441
  8.4 8.7 %collective-permute-start.1 = (bf16[32,8,128]{2,1,0:T(8,128)(2,1)S(1)}, bf16[32,8,128]{2,1,0:T(8,128)(2,1)S(1)}, u32[]{:S(2)}, u32[]{:S(2)}) collective-permute-start(bf16[32,8,128]{2,1,0:T(8,128)(2,1)S(1)} %widen_even.1.most), channel_id=1, source_target_pairs={{0,4},{4,0},{8,12},{12,8},{1,5},{5,1},{9,13},{13,9},{2,6},{6,2},{1... | collective-permute-start | bytes 196616 | tf_op jit(solution)/shard_map/ppermute | solution.py:441
  8.7 4.2 %collective-permute-start.7 = (bf16[10,8,128]{2,1,0:T(8,128)(2,1)S(1)}, bf16[10,8,128]{2,1,0:T(8,128)(2,1)S(1)}, u32[]{:S(2)}, u32[]{:S(2)}) collective-permute-start(bf16[10,8,128]{2,1,0:T(8,128)(2,1)S(1)} %get-tuple-element.18), channel_id=1, source_target_pairs={{0,12},{4,8},{8,4},{12,0},{1,13},{5,9},{9,5},{13,1},{2,14},{6,10},... | collective-permute-start | bytes 61448 | tf_op jit(solution)/shard_map/ppermute | solution.py:441
  10.1 7.0 %collective-permute-start.6 = (bf16[10,8,128]{2,1,0:T(8,128)(2,1)S(1)}, bf16[10,8,128]{2,1,0:T(8,128)(2,1)S(1)}, u32[]{:S(2)}, u32[]{:S(2)}) collective-permute-start(bf16[10,8,128]{2,1,0:T(8,128)(2,1)S(1)} %get-tuple-element.18), channel_id=1, source_target_pairs={{0,8},{4,12},{8,0},{12,4},{1,9},{5,13},{9,1},{13,5},{2,10},{6,14},... | collective-permute-start | bytes 61448 | tf_op jit(solution)/shard_map/ppermute | solution.py:441
  12.9 4.2 %collective-permute-start.5 = (bf16[10,8,128]{2,1,0:T(8,128)(2,1)S(1)}, bf16[10,8,128]{2,1,0:T(8,128)(2,1)S(1)}, u32[]{:S(2)}, u32[]{:S(2)}) collective-permute-start(bf16[10,8,128]{2,1,0:T(8,128)(2,1)S(1)} %get-tuple-element.18), channel_id=1, source_target_pairs={{0,4},{4,0},{8,12},{12,8},{1,5},{5,1},{9,13},{13,9},{2,6},{6,2},{1... | collective-permute-start | bytes 61448 | tf_op jit(solution)/shard_map/ppermute | solution.py:441
  17.1 1.0 %copy-start = (f32[1,3,24,8,128]{4,3,2,1,0:T(8,128)S(1)}, f32[1,3,24,8,128]{4,3,2,1,0:T(8,128)}, u32[]{:S(2)}) copy-start(f32[1,3,24,8,128]{4,3,2,1,0:T(8,128)} %vel_hbm.1) | copy-start | bytes 884740

commit v8 on v7

--- a/solution.py
+++ b/solution.py
@@ -189,8 +189,10 @@
 
 
 def mate_kernel(planes, count, *refs):
-    inner, outer = refs[:count], refs[count:2 * count]
-    meta, adesc, mean, slope, grads, vel, out, box3, box9, smooth, xs, raw, tb, desc, ys, frc = refs[2 * count:]
+    inner, outer = refs[:count], refs[count:2 * count][::-1]
+    meta, adesc, mean, slope, grads, vel_hbm, out, box3, box9, smooth, xs, raw, tb, desc, ys, frc, vel, sem = refs[2 * count:]
+    fetch = pltpu.make_async_copy(vel_hbm, vel, sem)
+    fetch.start()
     nx, nd, nf = planes + 18, planes + 16, planes + 8
     low, high = faces()
     which, dc = meta[0:1, :], meta[16:17, :]
@@ -283,6 +285,7 @@
                     s = [t[q] for q in (r - n, r + n) if 0 <= q < 8]
                     v = v + TAPS[3 + n] * (s[0] + s[1] if len(s) == 2 else s[0])
                 parts.append(v)
+    fetch.wait()
     both = halves(parts)
     res = dot(both, smooth[0:256]) + dot(both[:, 0:128], smooth[256:384])
     for c in range(3):
@@ -331,7 +334,7 @@
     return pl.pallas_call(
         functools.partial(mate_kernel, planes, count),
         out_shape=jax.ShapeDtypeStruct(vel.shape, f32),
-        in_specs=[VM] * (2 * count + 6),
+        in_specs=[VM] * (2 * count + 5) + [HBM],
         out_specs=VM,
         scratch_shapes=[
             pltpu.VMEM((256, 128), bf16),
@@ -343,10 +346,12 @@
             pltpu.VMEM((12, nd * PITCH + SPARE, 128), f32),
             pltpu.VMEM((3 * UNROLL, nf * PITCH + SPARE, 128), f32),
             pltpu.VMEM((3, nf * 8, 128), f32),
+            pltpu.VMEM(vel.shape, f32),
+            pltpu.SemaphoreType.DMA,
         ],
         compiler_params=pltpu.CompilerParams(vmem_limit_bytes=16 * 2**20),
         name="mate",
-    )(*[m.reshape(-1, 128) for m in inner + outer], meta, *owned, vel)
+    )(*[m.reshape(-1, 128) for m in inner + outer[::-1]], meta, *owned, pltpu.with_memory_space_constraint(vel, pltpu.HBM))
 
 
 def advect_kernel(planes, image_hbm, vel_hbm, partner_hbm, offsets_hbm, warp, first, second, meta, image, vel, down, up, partner, offsets, sems):

time: 24.4 us -> 21.9 us (0.90)
  the two profiles are of different devices: /device:TPU:13 before, /device:TPU:17 now
where the time goes in v8:
time: 21.9 us; the launch traced here: 21.7 us
  Pallas kernels  11.3 us (52%)
  starting transfers between devices  10.3 us (47%)
    ppermute x6, starting transfers between devices, from_brains(): lax.ppermute(x, 'brain', [(n, n ^ k) for n in range(4)])  7.07 us
    pallas_call x1, Pallas kernels, mate_part(): pl.pallas_call(functools.partial(mate_kernel, planes, count), out_shape=j...  6.24 us
    pallas_call x1, Pallas kernels, own_part(): pl.pallas_call(functools.partial(own_kernel, planes), out_shape=(shape((1...  3.83 us
    ppermute x1, starting transfers between devices, shards(): from_odd = lax.ppermute(second, 'slab', both_ways(odd_pairs))  1.91 us
    ppermute x1, starting transfers between devices, shards(): from_even = lax.ppermute(first, 'slab', both_ways(even_pairs))  1.36 us
    pallas_call x1, Pallas kernels, shards(): pl.pallas_call(functools.partial(advect_kernel, planes), out_shape=(jax.S...  1.15 us
  transfers between devices with their start and end apart: 8, of which 0 were waited for; matrix products, arithmetic and copies ran while one was open for 0% of the time, Pallas kernels for 18%

profile of v8, /device:TPU:17, one launch (start us, length us, event | category | flops | bytes accessed | tf_op | source)
XLA Modules:
  0.0 21.7 jit_solution(962884551607198591)
XLA Ops:
  0.0 1.2 %advect.1 = (f32[24,8,128]{2,1,0:T(8,128)S(1)}, bf16[13,8,128]{2,1,0:T(8,128)(2,1)S(1)}, bf16[13,8,128]{2,1,0:T(8,128)(2,1)S(1)}, s32[24,128]{1,0:T(8,128)S(1)}) custom-call(bf16[1,24,8,128]{3,2,1,0:T(8,128)(2,1)} %image_hbm.1, f32[1,3,24,8,128]{4,3,2,1,0:T(8,128)} %vel_hbm.1, s32[4]{0:T(128)} %partner_hbm.1, s32[2,4]{1,0:T(2,128)} %bitcast.18), custom_call_target="tpu_custom_call" | custom-call | tf_op jit(solution)/shard_map/advect/pallas_call | solution.py:456
  1.2 1.4 %collective-permute-start = (bf16[13,8,128]{2,1,0:T(8,128)(2,1)S(1)}, bf16[13,8,128]{2,1,0:T(8,128)(2,1)S(1)}, u32[]{:S(2)}, u32[]{:S(2)}) collective-permute-start(bf16[13,8,128]{2,1,0:T(8,128)(2,1)S(1)} %get-tuple-element.16.mine), channel_id=1, source_target_pairs={{0,1},{2,3},{1,0},{3,2},{4,5},{6,7},{5,4},{7,6},{8,9},{10,11},{9,8... | collective-permute-start | bytes 79880 | tf_op jit(solution)/shard_map/ppermute | solution.py:477
  2.5 1.9 %collective-permute-start.4 = (bf16[13,8,128]{2,1,0:T(8,128)(2,1)S(1)}, bf16[13,8,128]{2,1,0:T(8,128)(2,1)S(1)}, u32[]{:S(2)}, u32[]{:S(2)}) collective-permute-start(bf16[13,8,128]{2,1,0:T(8,128)(2,1)S(1)} %get-tuple-element.17.mine), channel_id=1, source_target_pairs={{1,2},{2,1},{5,6},{6,5},{9,10},{10,9},{13,14},{14,13},{17,18},{18,... | collective-permute-start | bytes 79880 | tf_op jit(solution)/shard_map/ppermute | solution.py:476
  4.4 0.0 collective-permute-done.got
  4.5 2.5 %collective-permute-start.3 = (bf16[32,8,128]{2,1,0:T(8,128)(2,1)S(1)}, bf16[32,8,128]{2,1,0:T(8,128)(2,1)S(1)}, u32[]{:S(2)}, u32[]{:S(2)}) collective-permute-start(bf16[32,8,128]{2,1,0:T(8,128)(2,1)S(1)} %widen_even.1.most), channel_id=1, source_target_pairs={{0,12},{4,8},{8,4},{12,0},{1,13},{5,9},{9,5},{13,1},{2,14},{6,10},... | collective-permute-start | bytes 196616 | tf_op jit(solution)/shard_map/ppermute | solution.py:446
  6.9 0.3 %collective-permute-start.2 = (bf16[32,8,128]{2,1,0:T(8,128)(2,1)S(1)}, bf16[32,8,128]{2,1,0:T(8,128)(2,1)S(1)}, u32[]{:S(2)}, u32[]{:S(2)}) collective-permute-start(bf16[32,8,128]{2,1,0:T(8,128)(2,1)S(1)} %widen_even.1.most), channel_id=1, source_target_pairs={{0,8},{4,12},{8,0},{12,4},{1,9},{5,13},{9,1},{13,5},{2,10},{6,14},... | collective-permute-start | bytes 196616 | tf_op jit(solution)/shard_map/ppermute | solution.py:446
  7.2 0.2 %collective-permute-start.1 = (bf16[32,8,128]{2,1,0:T(8,128)(2,1)S(1)}, bf16[32,8,128]{2,1,0:T(8,128)(2,1)S(1)}, u32[]{:S(2)}, u32[]{:S(2)}) collective-permute-start(bf16[32,8,128]{2,1,0:T(8,128)(2,1)S(1)} %widen_even.1.most), channel_id=1, source_target_pairs={{0,4},{4,0},{8,12},{12,8},{1,5},{5,1},{9,13},{13,9},{2,6},{6,2},{1... | collective-permute-start | bytes 196616 | tf_op jit(solution)/shard_map/ppermute | solution.py:446
  7.4 0.0 collective-permute-done.4.got
  7.4 1.9 %collective-permute-start.7 = (bf16[10,8,128]{2,1,0:T(8,128)(2,1)S(1)}, bf16[10,8,128]{2,1,0:T(8,128)(2,1)S(1)}, u32[]{:S(2)}, u32[]{:S(2)}) collective-permute-start(bf16[10,8,128]{2,1,0:T(8,128)(2,1)S(1)} %get-tuple-element.18), channel_id=1, source_target_pairs={{0,4},{4,0},{8,12},{12,8},{1,5},{5,1},{9,13},{13,9},{2,6},{6,2},{1... | collective-permute-start | bytes 61448 | tf_op jit(solution)/shard_map/ppermute | solution.py:446
  9.3 1.2 %collective-permute-start.6 = (bf16[10,8,128]{2,1,0:T(8,128)(2,1)S(1)}, bf16[10,8,128]{2,1,0:T(8,128)(2,1)S(1)}, u32[]{:S(2)}, u32[]{:S(2)}) collective-permute-start(bf16[10,8,128]{2,1,0:T(8,128)(2,1)S(1)} %get-tuple-element.18), channel_id=1, source_target_pairs={{0,8},{4,12},{8,0},{12,4},{1,9},{5,13},{9,1},{13,5},{2,10},{6,14},... | collective-permute-start | bytes 61448 | tf_op jit(solution)/shard_map/ppermute | solution.py:446
  10.5 0.0 collective-permute-done.7
  10.5 1.1 %collective-permute-start.5 = (bf16[10,8,128]{2,1,0:T(8,128)(2,1)S(1)}, bf16[10,8,128]{2,1,0:T(8,128)(2,1)S(1)}, u32[]{:S(2)}, u32[]{:S(2)}) collective-permute-start(bf16[10,8,128]{2,1,0:T(8,128)(2,1)S(1)} %get-tuple-element.18), channel_id=1, source_target_pairs={{0,12},{4,8},{8,4},{12,0},{1,13},{5,9},{9,5},{13,1},{2,14},{6,10},... | collective-permute-start | bytes 61448 | tf_op jit(solution)/shard_map/ppermute | solution.py:446
  11.6 3.8 %own.1 = (f32[12,376,128]{2,1,0:T(8,128)S(1)}, f32[12,256,128]{2,1,0:T(8,128)S(1)}, f32[12,256,128]{2,1,0:T(8,128)S(1)}, f32[3,12,256,128]{3,2,1,0:T(8,128)S(1)}) custom-call(bf16[336,128]{1,0:T(8,128)(2,1)S(1)} %bitcast.10), custom_call_target="tpu_custom_call" | custom-call | flops 1000000 | bytes 65536 | tf_op jit(solution)/shard_map/own/pallas_call | solution.py:307
  15.4 0.0 collective-permute-done.6
  15.4 0.0 collective-permute-done.5
  15.4 0.0 collective-permute-done.3
  15.5 0.0 collective-permute-done.2
  15.5 0.0 collective-permute-done.1
  15.5 6.2 %mate.1 = f32[3,24,8,128]{3,2,1,0:T(8,128)} custom-call(bf16[256,128]{1,0:T(8,128)(2,1)S(1)} %bitcast.13, bf16[256,128]{1,0:T(8,128)(2,1)S(1)} %bitcast.12, bf16[256,128]{1,0:T(8,128)(2,1)S(1)} %bitcast.11, bf16[80,128]{1,0:T(8,128)(2,1)S(1)} %bitcast.16, bf16[80,128]{1,0:T(8,128)(2,1)S(1)} %bitcast.15, bf16[80,128]{1,0:T(8,128)(2,1)S(1)} %bitcast.14, ...), custom_call_target="tpu_custom_call" | custom-call | tf_op jit(solution)/shard_map/mate/pallas_call | solution.py:334
  (2 shorter events, 0.0 us)
Async XLA Ops:
  1.2 3.3 %collective-permute-start = (bf16[13,8,128]{2,1,0:T(8,128)(2,1)S(1)}, bf16[13,8,128]{2,1,0:T(8,128)(2,1)S(1)}, u32[]{:S(2)}, u32[]{:S(2)}) collective-permute-start(bf16[13,8,128]{2,1,0:T(8,128)(2,1)S(1)} %get-tuple-element.16.mine), channel_id=1, source_target_pairs={{0,1},{2,3},{1,0},{3,2},{4,5},{6,7},{5,4},{7,6},{8,9},{10,11},{9,8... | collective-permute-start | bytes 79880 | tf_op jit(solution)/shard_map/ppermute | solution.py:477
  2.5 4.9 %collective-permute-start.4 = (bf16[13,8,128]{2,1,0:T(8,128)(2,1)S(1)}, bf16[13,8,128]{2,1,0:T(8,128)(2,1)S(1)}, u32[]{:S(2)}, u32[]{:S(2)}) collective-permute-start(bf16[13,8,128]{2,1,0:T(8,128)(2,1)S(1)} %get-tuple-element.17.mine), channel_id=1, source_target_pairs={{1,2},{2,1},{5,6},{6,5},{9,10},{10,9},{13,14},{14,13},{17,18},{18,... | collective-permute-start | bytes 79880 | tf_op jit(solution)/shard_map/ppermute | solution.py:476
  4.5 11.0 %collective-permute-start.3 = (bf16[32,8,128]{2,1,0:T(8,128)(2,1)S(1)}, bf16[32,8,128]{2,1,0:T(8,128)(2,1)S(1)}, u32[]{:S(2)}, u32[]{:S(2)}) collective-permute-start(bf16[32,8,128]{2,1,0:T(8,128)(2,1)S(1)} %widen_even.1.most), channel_id=1, source_target_pairs={{0,12},{4,8},{8,4},{12,0},{1,13},{5,9},{9,5},{13,1},{2,14},{6,10},... | collective-permute-start | bytes 196616 | tf_op jit(solution)/shard_map/ppermute | solution.py:446
  6.9 8.5 %collective-permute-start.2 = (bf16[32,8,128]{2,1,0:T(8,128)(2,1)S(1)}, bf16[32,8,128]{2,1,0:T(8,128)(2,1)S(1)}, u32[]{:S(2)}, u32[]{:S(2)}) collective-permute-start(bf16[32,8,128]{2,1,0:T(8,128)(2,1)S(1)} %widen_even.1.most), channel_id=1, source_target_pairs={{0,8},{4,12},{8,0},{12,4},{1,9},{5,13},{9,1},{13,5},{2,10},{6,14},... | collective-permute-start | bytes 196616 | tf_op jit(solution)/shard_map/ppermute | solution.py:446
  7.2 8.3 %collective-permute-start.1 = (bf16[32,8,128]{2,1,0:T(8,128)(2,1)S(1)}, bf16[32,8,128]{2,1,0:T(8,128)(2,1)S(1)}, u32[]{:S(2)}, u32[]{:S(2)}) collective-permute-start(bf16[32,8,128]{2,1,0:T(8,128)(2,1)S(1)} %widen_even.1.most), channel_id=1, source_target_pairs={{0,4},{4,0},{8,12},{12,8},{1,5},{5,1},{9,13},{13,9},{2,6},{6,2},{1... | collective-permute-start | bytes 196616 | tf_op jit(solution)/shard_map/ppermute | solution.py:446
  7.4 3.1 %collective-permute-start.7 = (bf16[10,8,128]{2,1,0:T(8,128)(2,1)S(1)}, bf16[10,8,128]{2,1,0:T(8,128)(2,1)S(1)}, u32[]{:S(2)}, u32[]{:S(2)}) collective-permute-start(bf16[10,8,128]{2,1,0:T(8,128)(2,1)S(1)} %get-tuple-element.18), channel_id=1, source_target_pairs={{0,4},{4,0},{8,12},{12,8},{1,5},{5,1},{9,13},{13,9},{2,6},{6,2},{1... | collective-permute-start | bytes 61448 | tf_op jit(solution)/shard_map/ppermute | solution.py:446
  9.3 6.1 %collective-permute-start.6 = (bf16[10,8,128]{2,1,0:T(8,128)(2,1)S(1)}, bf16[10,8,128]{2,1,0:T(8,128)(2,1)S(1)}, u32[]{:S(2)}, u32[]{:S(2)}) collective-permute-start(bf16[10,8,128]{2,1,0:T(8,128)(2,1)S(1)} %get-tuple-element.18), channel_id=1, source_target_pairs={{0,8},{4,12},{8,0},{12,4},{1,9},{5,13},{9,1},{13,5},{2,10},{6,14},... | collective-permute-start | bytes 61448 | tf_op jit(solution)/shard_map/ppermute | solution.py:446
  10.5 4.9 %collective-permute-start.5 = (bf16[10,8,128]{2,1,0:T(8,128)(2,1)S(1)}, bf16[10,8,128]{2,1,0:T(8,128)(2,1)S(1)}, u32[]{:S(2)}, u32[]{:S(2)}) collective-permute-start(bf16[10,8,128]{2,1,0:T(8,128)(2,1)S(1)} %get-tuple-element.18), channel_id=1, source_target_pairs={{0,12},{4,8},{8,4},{12,0},{1,13},{5,9},{9,5},{13,1},{2,14},{6,10},... | collective-permute-start | bytes 61448 | tf_op jit(solution)/shard_map/ppermute | solution.py:446

commit v9 on v6

--- a/solution.py
+++ b/solution.py
@@ -185,7 +185,7 @@
 
 
 def mate_kernel(planes, count, *refs):
-    inner, outer = refs[:count], refs[count:2 * count]
+    inner, outer = refs[:count][::-1], refs[count:2 * count]
     meta, adesc, mean, slope, grads, vel, out, box3, box9, smooth, xs, raw, tb, desc, ys, frc = refs[2 * count:]
     nx, nd, nf = planes + 18, planes + 16, planes + 8
     low, high = faces()
@@ -339,7 +339,7 @@
         ],
         compiler_params=pltpu.CompilerParams(vmem_limit_bytes=16 * 2**20),
         name="mate",
-    )(*[m.reshape(-1, 128) for m in inner + outer], meta, *owned, vel)
+    )(*[m.reshape(-1, 128) for m in inner[::-1] + outer], meta, *owned, vel)
 
 
 def advect_kernel(planes, image_hbm, vel_hbm, partner_hbm, offsets_hbm, warp, inner, first, second, meta, image, vel, down, up, partner, offsets, sems):

time: 21.9 us -> 21.3 us (0.973)
  waiting for transfers between devices: 1.89 us -> 0.64 us
  starting transfers between devices: 8.51 us -> 9.13 us
    ppermute x1, waiting for transfers between devices: 1.88 us -> 0.62 us  [shards(): from_odd = lax.ppermute(second, 'slab', both_ways(odd_pairs))]
    ppermute x6, starting transfers between devices: 5.3 us -> 5.91 us  [from_brains(): lax.ppermute(x, 'brain', [(n, n ^ k) for n in range(4)])]
where the time goes in v9:
time: 21.3 us; the launch traced here: 21.1 us
  Pallas kernels  11.3 us (53%)
  starting transfers between devices  9.13 us (43%)
  waiting for transfers between devices  0.64 us (3%)
    pallas_call x1, Pallas kernels, mate_part(): pl.pallas_call(functools.partial(mate_kernel, planes, count), out_shape=j...  6.18 us
    ppermute x6, starting transfers between devices, from_brains(): lax.ppermute(x, 'brain', [(n, n ^ k) for n in range(4)])  5.91 us
    pallas_call x1, Pallas kernels, own_part(): pl.pallas_call(functools.partial(own_kernel, planes), out_shape=(shape((1...  3.84 us
    ppermute x1, starting transfers between devices, shards(): from_odd = lax.ppermute(second, 'slab', both_ways(odd_pairs))  1.91 us
    ppermute x1, starting transfers between devices, shards(): from_even = lax.ppermute(first, 'slab', both_ways(even_pairs))  1.31 us
    pallas_call x1, Pallas kernels, shards(): pl.pallas_call(functools.partial(advect_kernel, planes), out_shape=(jax.S...  1.22 us
    ppermute x1, waiting for transfers between devices, shards(): from_odd = lax.ppermute(second, 'slab', both_ways(odd_pairs))  0.62 us
  transfers between devices with their start and end apart: 8, of which 1 were waited for; matrix products, arithmetic and copies ran while one was open for 0% of the time, Pallas kernels for 18%

profile of v9, /device:TPU:17, one launch (start us, length us, event | category | flops | bytes accessed | tf_op | source)
XLA Modules:
  0.0 21.1 jit_solution(1698172060602562648)
XLA Ops:
  0.0 0.0 copy-start
  0.0 1.2 %advect.1 = (f32[24,8,128]{2,1,0:T(8,128)S(1)}, bf16[22,8,128]{2,1,0:T(8,128)(2,1)S(1)}, bf16[13,8,128]{2,1,0:T(8,128)(2,1)S(1)}, bf16[13,8,128]{2,1,0:T(8,128)(2,1)S(1)}, s32[24,128]{1,0:T(8,128)S(1)}) custom-call(bf16[1,24,8,128]{3,2,1,0:T(8,128)(2,1)} %image_hbm.1, f32[1,3,24,8,128]{4,3,2,1,0:T(8,128)} %vel_hbm.1, s32[4]{0:T(128)} %partner_hbm.1, ...), custom_call_target="tpu_custom_call" | custom-call | tf_op jit(solution)/shard_map/advect/pallas_call | solution.py:427
  1.2 0.7 %collective-permute-start.2 = (bf16[22,8,128]{2,1,0:T(8,128)(2,1)S(1)}, bf16[22,8,128]{2,1,0:T(8,128)(2,1)S(1)}, u32[]{:S(2)}, u32[]{:S(2)}) collective-permute-start(bf16[22,8,128]{2,1,0:T(8,128)(2,1)S(1)} %get-tuple-element.16), channel_id=1, source_target_pairs={{0,4},{4,0},{8,12},{12,8},{1,5},{5,1},{9,13},{13,9},{2,6},{6,2},{1... | collective-permute-start | bytes 135176 | tf_op jit(solution)/shard_map/ppermute | solution.py:418
  2.0 1.3 %collective-permute-start.3 = (bf16[13,8,128]{2,1,0:T(8,128)(2,1)S(1)}, bf16[13,8,128]{2,1,0:T(8,128)(2,1)S(1)}, u32[]{:S(2)}, u32[]{:S(2)}) collective-permute-start(bf16[13,8,128]{2,1,0:T(8,128)(2,1)S(1)} %get-tuple-element.18.sent1), channel_id=1, source_target_pairs={{0,1},{2,3},{1,0},{3,2},{4,5},{6,7},{5,4},{7,6},{8,9},{10,11},{9,8... | collective-permute-start | bytes 79880 | tf_op jit(solution)/shard_map/ppermute | solution.py:448
  3.3 1.9 %collective-permute-start.4 = (bf16[13,8,128]{2,1,0:T(8,128)(2,1)S(1)}, bf16[13,8,128]{2,1,0:T(8,128)(2,1)S(1)}, u32[]{:S(2)}, u32[]{:S(2)}) collective-permute-start(bf16[13,8,128]{2,1,0:T(8,128)(2,1)S(1)} %get-tuple-element.19.sent2), channel_id=1, source_target_pairs={{1,2},{2,1},{5,6},{6,5},{9,10},{10,9},{13,14},{14,13},{17,18},{18,... | collective-permute-start | bytes 79880 | tf_op jit(solution)/shard_map/ppermute | solution.py:447
  5.2 1.3 %collective-permute-start.1 = (bf16[22,8,128]{2,1,0:T(8,128)(2,1)S(1)}, bf16[22,8,128]{2,1,0:T(8,128)(2,1)S(1)}, u32[]{:S(2)}, u32[]{:S(2)}) collective-permute-start(bf16[22,8,128]{2,1,0:T(8,128)(2,1)S(1)} %get-tuple-element.16), channel_id=1, source_target_pairs={{0,8},{4,12},{8,0},{12,4},{1,9},{5,13},{9,1},{13,5},{2,10},{6,14},... | collective-permute-start | bytes 135176 | tf_op jit(solution)/shard_map/ppermute | solution.py:418
  6.5 0.8 %collective-permute-start = (bf16[22,8,128]{2,1,0:T(8,128)(2,1)S(1)}, bf16[22,8,128]{2,1,0:T(8,128)(2,1)S(1)}, u32[]{:S(2)}, u32[]{:S(2)}) collective-permute-start(bf16[22,8,128]{2,1,0:T(8,128)(2,1)S(1)} %get-tuple-element.16), channel_id=1, source_target_pairs={{0,12},{4,8},{8,4},{12,0},{1,13},{5,9},{9,5},{13,1},{2,14},{6,10},... | collective-permute-start | bytes 135176 | tf_op jit(solution)/shard_map/ppermute | solution.py:418
  7.2 0.0 collective-permute-done.3.got1
  7.2 0.6 %collective-permute-done.4.got2 = bf16[13,8,128]{2,1,0:T(8,128)(2,1)S(1)} collective-permute-done((bf16[13,8,128]{2,1,0:T(8,128)(2,1)S(1)}, bf16[13,8,128]{2,1,0:T(8,128)(2,1)S(1)}, u32[]{:S(2)}, u32[]{:S(2)}) %collective-permute-start.4) | collective-permute-done | bytes 26656 | tf_op jit(solution)/shard_map/ppermute | solution.py:447
  7.9 2.7 %collective-permute-start.7 = (bf16[20,8,128]{2,1,0:T(8,128)(2,1)S(1)}, bf16[20,8,128]{2,1,0:T(8,128)(2,1)S(1)}, u32[]{:S(2)}, u32[]{:S(2)}) collective-permute-start(bf16[20,8,128]{2,1,0:T(8,128)(2,1)S(1)} %get-tuple-element.20), channel_id=1, source_target_pairs={{0,12},{4,8},{8,4},{12,0},{1,13},{5,9},{9,5},{13,1},{2,14},{6,10},... | collective-permute-start | bytes 122888 | tf_op jit(solution)/shard_map/ppermute | solution.py:418
  10.6 0.3 %collective-permute-start.6 = (bf16[20,8,128]{2,1,0:T(8,128)(2,1)S(1)}, bf16[20,8,128]{2,1,0:T(8,128)(2,1)S(1)}, u32[]{:S(2)}, u32[]{:S(2)}) collective-permute-start(bf16[20,8,128]{2,1,0:T(8,128)(2,1)S(1)} %get-tuple-element.20), channel_id=1, source_target_pairs={{0,8},{4,12},{8,0},{12,4},{1,9},{5,13},{9,1},{13,5},{2,10},{6,14},... | collective-permute-start | bytes 122888 | tf_op jit(solution)/shard_map/ppermute | solution.py:418
  10.8 0.0 collective-permute-done.2
  10.8 0.2 %collective-permute-start.5 = (bf16[20,8,128]{2,1,0:T(8,128)(2,1)S(1)}, bf16[20,8,128]{2,1,0:T(8,128)(2,1)S(1)}, u32[]{:S(2)}, u32[]{:S(2)}) collective-permute-start(bf16[20,8,128]{2,1,0:T(8,128)(2,1)S(1)} %get-tuple-element.20), channel_id=1, source_target_pairs={{0,4},{4,0},{8,12},{12,8},{1,5},{5,1},{9,13},{13,9},{2,6},{6,2},{1... | collective-permute-start | bytes 122888 | tf_op jit(solution)/shard_map/ppermute | solution.py:418
  11.0 3.8 %own.1 = (f32[12,376,128]{2,1,0:T(8,128)S(1)}, f32[12,256,128]{2,1,0:T(8,128)S(1)}, f32[12,256,128]{2,1,0:T(8,128)S(1)}, f32[3,12,256,128]{3,2,1,0:T(8,128)S(1)}) custom-call(bf16[336,128]{1,0:T(8,128)(2,1)S(1)} %bitcast.17), custom_call_target="tpu_custom_call" | custom-call | flops 600000000 | bytes 16777216 | tf_op jit(solution)/shard_map/own/pallas_call | solution.py:297
  14.9 0.0 collective-permute-done.1
  14.9 0.0 collective-permute-done
  14.9 0.0 collective-permute-done.7
  14.9 0.0 collective-permute-done.6
  14.9 0.0 collective-permute-done.5
  14.9 0.0 copy-done
  14.9 6.2 %mate.1 = f32[3,24,8,128]{3,2,1,0:T(8,128)} custom-call(bf16[176,128]{1,0:T(8,128)(2,1)S(1)} %bitcast.13, bf16[176,128]{1,0:T(8,128)(2,1)S(1)} %bitcast.12, bf16[176,128]{1,0:T(8,128)(2,1)S(1)} %bitcast.11, bf16[160,128]{1,0:T(8,128)(2,1)S(1)} %bitcast.16, bf16[160,128]{1,0:T(8,128)(2,1)S(1)} %bitcast.15, bf16[160,128]{1,0:T(8,128)(2,1)S(1)} %bitcast.14, ...), custom_call_target="tpu_custom_call" | custom-call | tf_op jit(solution)/shard_map/mate/pallas_call | solution.py:324
  (1 shorter events, 0.0 us)
Async XLA Ops:
  0.0 14.9 %copy-start = (f32[1,3,24,8,128]{4,3,2,1,0:T(8,128)S(1)}, f32[1,3,24,8,128]{4,3,2,1,0:T(8,128)}, u32[]{:S(2)}) copy-start(f32[1,3,24,8,128]{4,3,2,1,0:T(8,128)} %vel_hbm.1) | copy-start | bytes 884740
  1.2 9.6 %collective-permute-start.2 = (bf16[22,8,128]{2,1,0:T(8,128)(2,1)S(1)}, bf16[22,8,128]{2,1,0:T(8,128)(2,1)S(1)}, u32[]{:S(2)}, u32[]{:S(2)}) collective-permute-start(bf16[22,8,128]{2,1,0:T(8,128)(2,1)S(1)} %get-tuple-element.16), channel_id=1, source_target_pairs={{0,4},{4,0},{8,12},{12,8},{1,5},{5,1},{9,13},{13,9},{2,6},{6,2},{1... | collective-permute-start | bytes 135176 | tf_op jit(solution)/shard_map/ppermute | solution.py:418
  2.0 5.3 %collective-permute-start.3 = (bf16[13,8,128]{2,1,0:T(8,128)(2,1)S(1)}, bf16[13,8,128]{2,1,0:T(8,128)(2,1)S(1)}, u32[]{:S(2)}, u32[]{:S(2)}) collective-permute-start(bf16[13,8,128]{2,1,0:T(8,128)(2,1)S(1)} %get-tuple-element.18.sent1), channel_id=1, source_target_pairs={{0,1},{2,3},{1,0},{3,2},{4,5},{6,7},{5,4},{7,6},{8,9},{10,11},{9,8... | collective-permute-start | bytes 79880 | tf_op jit(solution)/shard_map/ppermute | solution.py:448
  3.3 4.6 %collective-permute-start.4 = (bf16[13,8,128]{2,1,0:T(8,128)(2,1)S(1)}, bf16[13,8,128]{2,1,0:T(8,128)(2,1)S(1)}, u32[]{:S(2)}, u32[]{:S(2)}) collective-permute-start(bf16[13,8,128]{2,1,0:T(8,128)(2,1)S(1)} %get-tuple-element.19.sent2), channel_id=1, source_target_pairs={{1,2},{2,1},{5,6},{6,5},{9,10},{10,9},{13,14},{14,13},{17,18},{18,... | collective-permute-start | bytes 79880 | tf_op jit(solution)/shard_map/ppermute | solution.py:447
  5.2 9.7 %collective-permute-start.1 = (bf16[22,8,128]{2,1,0:T(8,128)(2,1)S(1)}, bf16[22,8,128]{2,1,0:T(8,128)(2,1)S(1)}, u32[]{:S(2)}, u32[]{:S(2)}) collective-permute-start(bf16[22,8,128]{2,1,0:T(8,128)(2,1)S(1)} %get-tuple-element.16), channel_id=1, source_target_pairs={{0,8},{4,12},{8,0},{12,4},{1,9},{5,13},{9,1},{13,5},{2,10},{6,14},... | collective-permute-start | bytes 135176 | tf_op jit(solution)/shard_map/ppermute | solution.py:418
  6.5 8.4 %collective-permute-start = (bf16[22,8,128]{2,1,0:T(8,128)(2,1)S(1)}, bf16[22,8,128]{2,1,0:T(8,128)(2,1)S(1)}, u32[]{:S(2)}, u32[]{:S(2)}) collective-permute-start(bf16[22,8,128]{2,1,0:T(8,128)(2,1)S(1)} %get-tuple-element.16), channel_id=1, source_target_pairs={{0,12},{4,8},{8,4},{12,0},{1,13},{5,9},{9,5},{13,1},{2,14},{6,10},... | collective-permute-start | bytes 135176 | tf_op jit(solution)/shard_map/ppermute | solution.py:418
  7.9 7.0 %collective-permute-start.7 = (bf16[20,8,128]{2,1,0:T(8,128)(2,1)S(1)}, bf16[20,8,128]{2,1,0:T(8,128)(2,1)S(1)}, u32[]{:S(2)}, u32[]{:S(2)}) collective-permute-start(bf16[20,8,128]{2,1,0:T(8,128)(2,1)S(1)} %get-tuple-element.20), channel_id=1, source_target_pairs={{0,12},{4,8},{8,4},{12,0},{1,13},{5,9},{9,5},{13,1},{2,14},{6,10},... | collective-permute-start | bytes 122888 | tf_op jit(solution)/shard_map/ppermute | solution.py:418
  10.6 4.4 %collective-permute-start.6 = (bf16[20,8,128]{2,1,0:T(8,128)(2,1)S(1)}, bf16[20,8,128]{2,1,0:T(8,128)(2,1)S(1)}, u32[]{:S(2)}, u32[]{:S(2)}) collective-permute-start(bf16[20,8,128]{2,1,0:T(8,128)(2,1)S(1)} %get-tuple-element.20), channel_id=1, source_target_pairs={{0,8},{4,12},{8,0},{12,4},{1,9},{5,13},{9,1},{13,5},{2,10},{6,14},... | collective-permute-start | bytes 122888 | tf_op jit(solution)/shard_map/ppermute | solution.py:418
  10.8 4.1 %collective-permute-start.5 = (bf16[20,8,128]{2,1,0:T(8,128)(2,1)S(1)}, bf16[20,8,128]{2,1,0:T(8,128)(2,1)S(1)}, u32[]{:S(2)}, u32[]{:S(2)}) collective-permute-start(bf16[20,8,128]{2,1,0:T(8,128)(2,1)S(1)} %get-tuple-element.20), channel_id=1, source_target_pairs={{0,4},{4,0},{8,12},{12,8},{1,5},{5,1},{9,13},{13,9},{2,6},{6,2},{1... | collective-permute-start | bytes 122888 | tf_op jit(solution)/shard_map/ppermute | solution.py:418

commit v10 on v9

--- a/solution.py
+++ b/solution.py
@@ -130,18 +130,13 @@
     return [w0, w1, w1 + t[6], lo + hi, lo + hi, w6 + t[1], w6, w7]
 
 
-def own_kernel(planes, own, desc, mean, slope, grads, box3, box9, grad, xs, tb, ys):
+def own_kernel(planes, own, box3, box9, grad, step, desc, mean, slope, grads, xs, tb, ys):
     nx, nd, nf = planes + 18, planes + 16, planes + 8
     low, high = faces()
-    i, j = lanes()
-    for h in (0, 128):
-        box3[h:h + 128] = ones_where(jnp.abs(i - j) <= 1)
-        box9[h:h + 128] = ones_where(jnp.abs(i - j) <= 4)
-        grad[h:h + 128] = jnp.where(i == j + 1, 1.0, jnp.where(i == j - 1, -1.0, 0.0)).astype(bf16)
     x = own[...]
     xs[0] = x.astype(f32)
-    xs[3] = dot(x, ones_where(i == j + 1))
-    xs[4] = dot(x, ones_where(i == j - 1))
+    xs[3] = dot(x, step[0])
+    xs[4] = dot(x, step[1])
 
     def prep(p, _):
         at = pl.ds(pl.multiple_of(p * 8, 8), 8)
@@ -184,23 +179,32 @@
     lax.fori_loop(0, 12 // UNROLL, channels, 0)
 
 
-def mate_kernel(planes, count, *refs):
-    inner, outer = refs[:count][::-1], refs[count:2 * count]
-    meta, adesc, mean, slope, grads, vel, out, box3, box9, smooth, xs, raw, tb, desc, ys, frc = refs[2 * count:]
-    nx, nd, nf = planes + 18, planes + 16, planes + 8
-    low, high = faces()
-    which, dc = meta[0:1, :], meta[16:17, :]
-    dr = jnp.max(meta[8:16, :])
+def tables_kernel(meta, box3, box9, grad, step, smooth, take):
     i, j = lanes()
     weights = jnp.zeros((128, 128), f32)
     for d in range(4):
         weights = jnp.where(jnp.abs(i - j) == d, TAPS[3 + d], weights)
     whi, wlo = split(weights)
     for h in (0, 128):
+        grad[h:h + 128] = jnp.where(i == j + 1, 1.0, jnp.where(i == j - 1, -1.0, 0.0)).astype(bf16)
         box3[h:h + 128] = ones_where(jnp.abs(i - j) <= 1)
         box9[h:h + 128] = ones_where(jnp.abs(i - j) <= 4)
         smooth[h:h + 128] = whi
     smooth[256:384] = wlo
+    step[0] = ones_where(i == j + 1)
+    step[1] = ones_where(i == j - 1)
+    dc = meta[16:17, :]
+    for n, d in ((0, 0), (1, 1), (2, -1)):
+        take[n] = ones_where((i == j + d + dc) & (j + d >= 0) & (j + d < 128))
+
+
+def mate_kernel(planes, count, *refs):
+    inner, outer = refs[:count][::-1], refs[count:2 * count]
+    meta, box3, box9, smooth, take, adesc, mean, slope, grads, vel, out, xs, raw, tb, desc, ys, frc, result, sems = refs[2 * count:]
+    nx, nd, nf = planes + 18, planes + 16, planes + 8
+    low, high = faces()
+    which = meta[0:1, :]
+    dr = jnp.max(meta[8:16, :])
     row = lax.broadcasted_iota(jnp.int32, (8, 128), 0)
 
     x, y = inner[0][...], outer[0][...]
@@ -208,9 +212,8 @@
         x = jnp.where(which == n + 1, inner[n][...], x)
         y = jnp.where(which == n + 1, outer[n][...], y)
     x = jnp.concatenate([y[0:80], x, y[80:160]], axis=0)
-    for n, d in ((0, 0), (1, 1), (2, -1)):
-        take = ones_where((i == j + d + dc) & (j + d >= 0) & (j + d < 128))
-        raw[n, pl.ds(8, nx * 8), :] = dot(x, take)
+    for n in range(3):
+        raw[n, pl.ds(8, nx * 8), :] = dot(x, take[n])
 
     def prep(p, _):
         at = pl.multiple_of(p * 8, 8)
@@ -278,20 +281,25 @@
                 parts.append(v)
     both = halves(parts)
     res = dot(both, smooth[0:256]) + dot(both[:, 0:128], smooth[256:384])
+    copies = []
     for c in range(3):
         for g in range(planes // 8):
             for r in range(8):
                 n = ((c * planes + g * 8) + r) * 8
                 ys[0, pl.ds(g * 8 * PITCH + r, 8, stride=PITCH), :] = res[n:n + 8]
         for o in range(planes):
-            out[c, o] = vel[c, o] + (8.0 * VOLUME / 24.0) * ys[0, pl.ds(o * PITCH, 8), :]
+            result[c, o] = vel[0, c, o] + (8.0 * VOLUME / 24.0) * ys[0, pl.ds(o * PITCH, 8), :]
+        copies.append(pltpu.make_async_copy(result.at[c], out.at[c], sems.at[c]))
+        copies[c].start()
+    for copy in copies:
+        copy.wait()
 
 
 VM = pl.BlockSpec(memory_space=pltpu.VMEM)
 HBM = pl.BlockSpec(memory_space=pltpu.HBM)
 
 
-def own_part(planes, own):
+def own_part(planes, own, tables):
     nx, nd, nf = planes + 18, planes + 16, planes + 8
     shape = jax.ShapeDtypeStruct
     return pl.pallas_call(
@@ -302,12 +310,9 @@
             shape((12, nf * 8, 128), f32),
             shape((3, 12, nf * 8, 128), f32),
         ),
-        in_specs=[VM],
+        in_specs=[VM] * 5,
         out_specs=(VM,) * 4,
         scratch_shapes=[
-            pltpu.VMEM((256, 128), bf16),
-            pltpu.VMEM((256, 128), bf16),
-            pltpu.VMEM((256, 128), bf16),
             pltpu.VMEM((5, nx * 8, 128), f32),
             pltpu.VMEM((13, (nd + 1) * PITCH + SPARE, 128), f32),
             pltpu.VMEM((2 * UNROLL, nf * PITCH + SPARE, 128), f32),
@@ -315,34 +320,33 @@
         compiler_params=pltpu.CompilerParams(vmem_limit_bytes=16 * 2**20),
         cost_estimate=pl.CostEstimate(flops=6 * 10**8, bytes_accessed=16 * 2**20, transcendentals=10**6),
         name="own",
-    )(own.reshape(-1, 128))
-
-
-def mate_part(planes, inner, outer, meta, owned, vel):
+    )(own.reshape(-1, 128), *tables[:4])
+
+
+def mate_part(planes, inner, outer, meta, tables, owned, vel):
     nx, nd, nf = planes + 18, planes + 16, planes + 8
     count = len(inner)
     return pl.pallas_call(
         functools.partial(mate_kernel, planes, count),
-        out_shape=jax.ShapeDtypeStruct(vel.shape, f32),
-        in_specs=[VM] * (2 * count + 6),
-        out_specs=VM,
+        out_shape=jax.ShapeDtypeStruct(vel.shape[1:], f32),
+        in_specs=[VM] * (2 * count + 10),
+        out_specs=HBM,
         scratch_shapes=[
-            pltpu.VMEM((256, 128), bf16),
-            pltpu.VMEM((256, 128), bf16),
-            pltpu.VMEM((384, 128), bf16),
             pltpu.VMEM((5, nx * 8, 128), f32),
             pltpu.VMEM((3, nx * 8 + 16, 128), f32),
             pltpu.VMEM((13, (nd + 1) * PITCH + SPARE, 128), f32),
             pltpu.VMEM((12, nd * PITCH + SPARE, 128), f32),
             pltpu.VMEM((3 * UNROLL, nf * PITCH + SPARE, 128), f32),
             pltpu.VMEM((3, nf * 8, 128), f32),
+            pltpu.VMEM(vel.shape[1:], f32),
+            pltpu.SemaphoreType.DMA((3,)),
         ],
         compiler_params=pltpu.CompilerParams(vmem_limit_bytes=16 * 2**20),
         name="mate",
-    )(*[m.reshape(-1, 128) for m in inner[::-1] + outer], meta, *owned, vel)
-
-
-def advect_kernel(planes, image_hbm, vel_hbm, partner_hbm, offsets_hbm, warp, inner, first, second, meta, image, vel, down, up, partner, offsets, sems):
+    )(*[m.reshape(-1, 128) for m in inner[::-1] + outer], meta, tables[0], tables[1], *tables[4:], *owned, vel)
+
+
+def advect_kernel(planes, image_hbm, vel_hbm, partner_hbm, offsets_hbm, warp, inner, first, second, meta, vel, image, down, up, partner, offsets, sems):
     copies = [
         pltpu.make_async_copy(vel_hbm, vel, sems.at[0]),
         pltpu.make_async_copy(image_hbm, image, sems.at[1]),
@@ -424,14 +428,13 @@
     planes = intensity.shape[1]
     slabs, brains = lax.axis_size("slab"), lax.axis_size("brain")
     edge = jax.ShapeDtypeStruct((EDGE, 8, 128), bf16)
-    warp, inner, first, second, meta = pl.pallas_call(
+    warp, inner, first, second, meta, vel = pl.pallas_call(
         functools.partial(advect_kernel, planes),
-        out_shape=(jax.ShapeDtypeStruct((planes, 8, 128), f32), jax.ShapeDtypeStruct((planes - 2, 8, 128), bf16), edge, edge, jax.ShapeDtypeStruct((24, 128), jnp.int32)),
+        out_shape=(jax.ShapeDtypeStruct((planes, 8, 128), f32), jax.ShapeDtypeStruct((planes - 2, 8, 128), bf16), edge, edge, jax.ShapeDtypeStruct((24, 128), jnp.int32), jax.ShapeDtypeStruct(velocity.shape, f32)),
         in_specs=[HBM] * 4,
-        out_specs=(VM,) * 5,
+        out_specs=(VM,) * 6,
         scratch_shapes=[
             pltpu.VMEM(intensity.shape, bf16),
-            pltpu.VMEM(velocity.shape, f32),
             pltpu.VMEM(edge.shape, bf16),
             pltpu.VMEM(edge.shape, bf16),
             pltpu.SMEM(partner.shape, jnp.int32),
@@ -447,6 +450,16 @@
     from_odd = lax.ppermute(second, "slab", both_ways(odd_pairs))
     from_even = lax.ppermute(first, "slab", both_ways(even_pairs))
     inners = from_brains(inner, partner)
+    matrix = lambda *shape: jax.ShapeDtypeStruct(shape, bf16)
+    tables = pl.pallas_call(
+        tables_kernel,
+        out_shape=(matrix(256, 128),) * 3 + (matrix(2, 128, 128), matrix(384, 128), matrix(3, 128, 128)),
+        in_specs=[VM],
+        out_specs=(VM,) * 6,
+        compiler_params=pltpu.CompilerParams(vmem_limit_bytes=8 * 2**20),
+        cost_estimate=pl.CostEstimate(flops=10**7, bytes_accessed=2**19, transcendentals=0),
+        name="tables",
+    )(meta)
     own, outer = pl.pallas_call(
         functools.partial(widen_kernel, planes),
         out_shape=(jax.ShapeDtypeStruct((planes + 18, 8, 128), bf16), jax.ShapeDtypeStruct((20, 8, 128), bf16)),
@@ -456,7 +469,7 @@
         name="widen",
     )(warp, first, second, from_even, from_odd)
     outers = from_brains(outer, partner)
-    return mate_part(planes, inners, outers, meta, own_part(planes, own), velocity[0])[None]
+    return mate_part(planes, inners, outers, meta, tables, own_part(planes, own, tables), vel)[None]
 
 
 def solution(mesh):

time: 21.3 us -> 21.3 us (level)
  transfers between devices with their start and end apart: 8 -> 8, of which waited for: 1 -> 1; matrix products, arithmetic and copies ran while one was open for 0% -> 0% of each run, Pallas kernels for 18% -> 19%
where the time goes in v10:
time: 21.3 us; the launch traced here: 21 us
  Pallas kernels  11.3 us (53%)
  starting transfers between devices  9.13 us (43%)
  waiting for transfers between devices  0.53 us (2%)
    pallas_call x1, Pallas kernels, mate_part(): pl.pallas_call(functools.partial(mate_kernel, planes, count), out_shape=j...  6.17 us
    ppermute x6, starting transfers between devices, from_brains(): lax.ppermute(x, 'brain', [(n, n ^ k) for n in range(4)])  5.91 us
    pallas_call x1, Pallas kernels, own_part(): pl.pallas_call(functools.partial(own_kernel, planes), out_shape=(shape((1...  3.84 us
    ppermute x1, starting transfers between devices, shards(): from_odd = lax.ppermute(second, 'slab', both_ways(odd_pairs))  1.91 us
    ppermute x1, starting transfers between devices, shards(): from_even = lax.ppermute(first, 'slab', both_ways(even_pairs))  1.31 us
    pallas_call x1, Pallas kernels, shards(): pl.pallas_call(functools.partial(advect_kernel, planes), out_shape=(jax.S...  1.16 us
    ppermute x1, waiting for transfers between devices, shards(): from_odd = lax.ppermute(second, 'slab', both_ways(odd_pairs))  0.52 us
  transfers between devices with their start and end apart: 8, of which 1 were waited for; matrix products, arithmetic and copies ran while one was open for 0% of the time, Pallas kernels for 19%

profile of v10, /device:TPU:17, one launch (start us, length us, event | category | flops | bytes accessed | tf_op | source)
XLA Modules:
  0.0 21.0 jit_solution(9775809365410019255)
XLA Ops:
  0.0 1.2 %advect.1 = (f32[24,8,128]{2,1,0:T(8,128)S(1)}, bf16[22,8,128]{2,1,0:T(8,128)(2,1)S(1)}, bf16[13,8,128]{2,1,0:T(8,128)(2,1)S(1)}, bf16[13,8,128]{2,1,0:T(8,128)(...) custom-call(bf16[1,24,8,128]{3,2,1,0:T(8,128)(2,1)} %image_hbm.1, f32[1,3,24,8,128]{4,3,2,1,0:T(8,128)} %vel_hbm.1, ...), custom_call_target="tpu_custom_call" | custom-call | tf_op jit(solution)/shard_map/advect/pallas_call | solution.py:431
  1.2 0.7 %collective-permute-start.2 = (bf16[22,8,128]{2,1,0:T(8,128)(2,1)S(1)}, bf16[22,8,128]{2,1,0:T(8,128)(2,1)S(1)}, u32[]{:S(2)}, u32[]{:S(2)}) collective-permute-start(bf16[22,8,128]{2,1,0:T(8,128)(2,1)S(1)} %get-tuple-element.23), channel_id=1, source_target_pairs={{0,4},{4,0},{8,12},{12,8},{1,5},{5,1},{9,13},{13,9},{2,6},{6,2},{1... | collective-permute-start | bytes 135176 | tf_op jit(solution)/shard_map/ppermute | solution.py:422
  1.9 1.3 %collective-permute-start.3 = (bf16[13,8,128]{2,1,0:T(8,128)(2,1)S(1)}, bf16[13,8,128]{2,1,0:T(8,128)(2,1)S(1)}, u32[]{:S(2)}, u32[]{:S(2)}) collective-permute-start(bf16[13,8,128]{2,1,0:T(8,128)(2,1)S(1)} %get-tuple-element.25.sent1), channel_id=1, source_target_pairs={{0,1},{2,3},{1,0},{3,2},{4,5},{6,7},{5,4},{7,6},{8,9},{10,11},{9,8... | collective-permute-start | bytes 79880 | tf_op jit(solution)/shard_map/ppermute | solution.py:451
  3.2 1.9 %collective-permute-start.4 = (bf16[13,8,128]{2,1,0:T(8,128)(2,1)S(1)}, bf16[13,8,128]{2,1,0:T(8,128)(2,1)S(1)}, u32[]{:S(2)}, u32[]{:S(2)}) collective-permute-start(bf16[13,8,128]{2,1,0:T(8,128)(2,1)S(1)} %get-tuple-element.26.sent2), channel_id=1, source_target_pairs={{1,2},{2,1},{5,6},{6,5},{9,10},{10,9},{13,14},{14,13},{17,18},{18,... | collective-permute-start | bytes 79880 | tf_op jit(solution)/shard_map/ppermute | solution.py:450
  5.1 1.3 %collective-permute-start.1 = (bf16[22,8,128]{2,1,0:T(8,128)(2,1)S(1)}, bf16[22,8,128]{2,1,0:T(8,128)(2,1)S(1)}, u32[]{:S(2)}, u32[]{:S(2)}) collective-permute-start(bf16[22,8,128]{2,1,0:T(8,128)(2,1)S(1)} %get-tuple-element.23), channel_id=1, source_target_pairs={{0,8},{4,12},{8,0},{12,4},{1,9},{5,13},{9,1},{13,5},{2,10},{6,14},... | collective-permute-start | bytes 135176 | tf_op jit(solution)/shard_map/ppermute | solution.py:422
  6.4 0.8 %collective-permute-start = (bf16[22,8,128]{2,1,0:T(8,128)(2,1)S(1)}, bf16[22,8,128]{2,1,0:T(8,128)(2,1)S(1)}, u32[]{:S(2)}, u32[]{:S(2)}) collective-permute-start(bf16[22,8,128]{2,1,0:T(8,128)(2,1)S(1)} %get-tuple-element.23), channel_id=1, source_target_pairs={{0,12},{4,8},{8,4},{12,0},{1,13},{5,9},{9,5},{13,1},{2,14},{6,10},... | collective-permute-start | bytes 135176 | tf_op jit(solution)/shard_map/ppermute | solution.py:422
  7.2 0.1 tables.1
  7.3 0.0 collective-permute-done.3.got1
  7.3 0.5 %collective-permute-done.4.got2 = bf16[13,8,128]{2,1,0:T(8,128)(2,1)S(1)} collective-permute-done((bf16[13,8,128]{2,1,0:T(8,128)(2,1)S(1)}, bf16[13,8,128]{2,1,0:T(8,128)(2,1)S(1)}, u32[]{:S(2)}, u32[]{:S(2)}) %collective-permute-start.4) | collective-permute-done | bytes 26656 | tf_op jit(solution)/shard_map/ppermute | solution.py:450
  7.8 2.7 %collective-permute-start.7 = (bf16[20,8,128]{2,1,0:T(8,128)(2,1)S(1)}, bf16[20,8,128]{2,1,0:T(8,128)(2,1)S(1)}, u32[]{:S(2)}, u32[]{:S(2)}) collective-permute-start(bf16[20,8,128]{2,1,0:T(8,128)(2,1)S(1)} %get-tuple-element.27), channel_id=1, source_target_pairs={{0,12},{4,8},{8,4},{12,0},{1,13},{5,9},{9,5},{13,1},{2,14},{6,10},... | collective-permute-start | bytes 122888 | tf_op jit(solution)/shard_map/ppermute | solution.py:422
  10.5 0.3 %collective-permute-start.6 = (bf16[20,8,128]{2,1,0:T(8,128)(2,1)S(1)}, bf16[20,8,128]{2,1,0:T(8,128)(2,1)S(1)}, u32[]{:S(2)}, u32[]{:S(2)}) collective-permute-start(bf16[20,8,128]{2,1,0:T(8,128)(2,1)S(1)} %get-tuple-element.27), channel_id=1, source_target_pairs={{0,8},{4,12},{8,0},{12,4},{1,9},{5,13},{9,1},{13,5},{2,10},{6,14},... | collective-permute-start | bytes 122888 | tf_op jit(solution)/shard_map/ppermute | solution.py:422
  10.7 0.0 collective-permute-done.2
  10.8 0.2 %collective-permute-start.5 = (bf16[20,8,128]{2,1,0:T(8,128)(2,1)S(1)}, bf16[20,8,128]{2,1,0:T(8,128)(2,1)S(1)}, u32[]{:S(2)}, u32[]{:S(2)}) collective-permute-start(bf16[20,8,128]{2,1,0:T(8,128)(2,1)S(1)} %get-tuple-element.27), channel_id=1, source_target_pairs={{0,4},{4,0},{8,12},{12,8},{1,5},{5,1},{9,13},{13,9},{2,6},{6,2},{1... | collective-permute-start | bytes 122888 | tf_op jit(solution)/shard_map/ppermute | solution.py:422
  11.0 3.8 %own.1 = (f32[12,376,128]{2,1,0:T(8,128)S(1)}, f32[12,256,128]{2,1,0:T(8,128)S(1)}, f32[12,256,128]{2,1,0:T(8,128)S(1)}, f32[3,12,256,128]{3,2,1,0:T(8,128)S(1)}) custom-call(bf16[336,128]{1,0:T(8,128)(2,1)S(1)} %bitcast.15, bf16[256,128]{1,0:T(8,128)(2,1)S(1)} %get-tuple-element.29.box3.refs_7_, bf16[256,128]{1,0:T(8,128)(2,1)S(1)} %get-tuple-element.30.box9.refs_8_, ...), custom_call_target="tpu_custom_call" | custom-call | flops 600000000 | bytes 16777216 | tf_op jit(solution)/shard_map/own/pallas_call | solution.py:305
  14.8 0.0 collective-permute-done.1
  14.8 0.0 collective-permute-done
  14.8 0.0 collective-permute-done.7
  14.8 0.0 collective-permute-done.6
  14.9 0.0 collective-permute-done.5
  14.9 6.2 %mate.1 = f32[3,24,8,128]{3,2,1,0:T(8,128)} custom-call(bf16[176,128]{1,0:T(8,128)(2,1)S(1)} %bitcast.11, bf16[176,128]{1,0:T(8,128)(2,1)S(1)} %bitcast.10, bf16[176,128]{1,0:T(8,128)(2,1)S(1)} %bitcast.9, bf16[160,128]{1,0:T(8,128)(2,1)S(1)} %bitcast.14, bf16[160,128]{1,0:T(8,128)(2,1)S(1)} %bitcast.13, bf16[160,128]{1,0:T(8,128)(2,1)S(1)} %bitcast.12, ...), custom_call_target="tpu_custom_call" | custom-call | tf_op jit(solution)/shard_map/mate/pallas_call | solution.py:329
  (1 shorter events, 0.0 us)
Async XLA Ops:
  1.2 9.6 %collective-permute-start.2 = (bf16[22,8,128]{2,1,0:T(8,128)(2,1)S(1)}, bf16[22,8,128]{2,1,0:T(8,128)(2,1)S(1)}, u32[]{:S(2)}, u32[]{:S(2)}) collective-permute-start(bf16[22,8,128]{2,1,0:T(8,128)(2,1)S(1)} %get-tuple-element.23), channel_id=1, source_target_pairs={{0,4},{4,0},{8,12},{12,8},{1,5},{5,1},{9,13},{13,9},{2,6},{6,2},{1... | collective-permute-start | bytes 135176 | tf_op jit(solution)/shard_map/ppermute | solution.py:422
  1.9 5.4 %collective-permute-start.3 = (bf16[13,8,128]{2,1,0:T(8,128)(2,1)S(1)}, bf16[13,8,128]{2,1,0:T(8,128)(2,1)S(1)}, u32[]{:S(2)}, u32[]{:S(2)}) collective-permute-start(bf16[13,8,128]{2,1,0:T(8,128)(2,1)S(1)} %get-tuple-element.25.sent1), channel_id=1, source_target_pairs={{0,1},{2,3},{1,0},{3,2},{4,5},{6,7},{5,4},{7,6},{8,9},{10,11},{9,8... | collective-permute-start | bytes 79880 | tf_op jit(solution)/shard_map/ppermute | solution.py:451
  3.2 4.6 %collective-permute-start.4 = (bf16[13,8,128]{2,1,0:T(8,128)(2,1)S(1)}, bf16[13,8,128]{2,1,0:T(8,128)(2,1)S(1)}, u32[]{:S(2)}, u32[]{:S(2)}) collective-permute-start(bf16[13,8,128]{2,1,0:T(8,128)(2,1)S(1)} %get-tuple-element.26.sent2), channel_id=1, source_target_pairs={{1,2},{2,1},{5,6},{6,5},{9,10},{10,9},{13,14},{14,13},{17,18},{18,... | collective-permute-start | bytes 79880 | tf_op jit(solution)/shard_map/ppermute | solution.py:450
  5.1 9.7 %collective-permute-start.1 = (bf16[22,8,128]{2,1,0:T(8,128)(2,1)S(1)}, bf16[22,8,128]{2,1,0:T(8,128)(2,1)S(1)}, u32[]{:S(2)}, u32[]{:S(2)}) collective-permute-start(bf16[22,8,128]{2,1,0:T(8,128)(2,1)S(1)} %get-tuple-element.23), channel_id=1, source_target_pairs={{0,8},{4,12},{8,0},{12,4},{1,9},{5,13},{9,1},{13,5},{2,10},{6,14},... | collective-permute-start | bytes 135176 | tf_op jit(solution)/shard_map/ppermute | solution.py:422
  6.4 8.4 %collective-permute-start = (bf16[22,8,128]{2,1,0:T(8,128)(2,1)S(1)}, bf16[22,8,128]{2,1,0:T(8,128)(2,1)S(1)}, u32[]{:S(2)}, u32[]{:S(2)}) collective-permute-start(bf16[22,8,128]{2,1,0:T(8,128)(2,1)S(1)} %get-tuple-element.23), channel_id=1, source_target_pairs={{0,12},{4,8},{8,4},{12,0},{1,13},{5,9},{9,5},{13,1},{2,14},{6,10},... | collective-permute-start | bytes 135176 | tf_op jit(solution)/shard_map/ppermute | solution.py:422
  7.8 7.0 %collective-permute-start.7 = (bf16[20,8,128]{2,1,0:T(8,128)(2,1)S(1)}, bf16[20,8,128]{2,1,0:T(8,128)(2,1)S(1)}, u32[]{:S(2)}, u32[]{:S(2)}) collective-permute-start(bf16[20,8,128]{2,1,0:T(8,128)(2,1)S(1)} %get-tuple-element.27), channel_id=1, source_target_pairs={{0,12},{4,8},{8,4},{12,0},{1,13},{5,9},{9,5},{13,1},{2,14},{6,10},... | collective-permute-start | bytes 122888 | tf_op jit(solution)/shard_map/ppermute | solution.py:422
  10.5 4.4 %collective-permute-start.6 = (bf16[20,8,128]{2,1,0:T(8,128)(2,1)S(1)}, bf16[20,8,128]{2,1,0:T(8,128)(2,1)S(1)}, u32[]{:S(2)}, u32[]{:S(2)}) collective-permute-start(bf16[20,8,128]{2,1,0:T(8,128)(2,1)S(1)} %get-tuple-element.27), channel_id=1, source_target_pairs={{0,8},{4,12},{8,0},{12,4},{1,9},{5,13},{9,1},{13,5},{2,10},{6,14},... | collective-permute-start | bytes 122888 | tf_op jit(solution)/shard_map/ppermute | solution.py:422
  10.8 4.1 %collective-permute-start.5 = (bf16[20,8,128]{2,1,0:T(8,128)(2,1)S(1)}, bf16[20,8,128]{2,1,0:T(8,128)(2,1)S(1)}, u32[]{:S(2)}, u32[]{:S(2)}) collective-permute-start(bf16[20,8,128]{2,1,0:T(8,128)(2,1)S(1)} %get-tuple-element.27), channel_id=1, source_target_pairs={{0,4},{4,0},{8,12},{12,8},{1,5},{5,1},{9,13},{13,9},{2,6},{6,2},{1... | collective-permute-start | bytes 122888 | tf_op jit(solution)/shard_map/ppermute | solution.py:422

commit v11 on v10

--- a/solution.py
+++ b/solution.py
@@ -14,7 +14,8 @@
 UNROLL = 2
 PITCH = 9
 SPARE = 16
-FLOOR = 1e-5 * VOLUME * VOLUME
+FLOOR = 1e-5 * VOLUME
+ROOT = 1.0 / 27.0
 
 
 def split(v):
@@ -169,11 +170,12 @@
                 at = pl.ds(g * 64 + r * 8, 8)
                 mo, so = [sums[(g * 16 + q * 8 + r) * 8:(g * 16 + q * 8 + r) * 8 + 8] for q in range(2)]
                 gc = across[(g * 8 + r) * 8:(g * 8 + r) * 8 + 8]
-                inv = lax.rsqrt(VOLUME * so - mo * mo + FLOOR)
+                mo = mo * ROOT
+                inv = lax.rsqrt(so - mo * mo + FLOOR)
                 gz = desc[k, pl.ds((g * 8 + 5) * PITCH + r, 8, stride=PITCH), :] - desc[k, pl.ds((g * 8 + 3) * PITCH + r, 8, stride=PITCH), :]
                 gr = a[1] if r == 0 else -a[6] if r == 7 else a[r + 1] - a[r - 1]
                 mean[k, at, :] = mo
-                slope[k, at, :] = (inv * inv) * (VOLUME * a[r] - mo)
+                slope[k, at, :] = (inv * inv) * (a[r] - mo * ROOT)
                 for c, gg in enumerate((gz, gr, gc)):
                     grads[c, k, at, :] = gg * inv
     lax.fori_loop(0, 12 // UNROLL, channels, 0)
@@ -200,7 +202,7 @@
 
 def mate_kernel(planes, count, *refs):
     inner, outer = refs[:count][::-1], refs[count:2 * count]
-    meta, box3, box9, smooth, take, adesc, mean, slope, grads, vel, out, xs, raw, tb, desc, ys, frc, result, sems = refs[2 * count:]
+    meta, box3, box9, smooth, take, adesc, mean, slope, grads, vel, out, xs, raw, tb, desc, ys, frc = refs[2 * count:]
     nx, nd, nf = planes + 18, planes + 16, planes + 8
     low, high = faces()
     which = meta[0:1, :]
@@ -245,9 +247,10 @@
                 for h, k in enumerate(ks):
                     mm, sm, sc = [sums[h][(g * 24 + q * 8 + r) * 8:(g * 24 + q * 8 + r) * 8 + 8] for q in range(3)]
                     b = desc[k, pl.ds((g * 8 + 4) * PITCH + r, 8, stride=PITCH), :]
-                    inv = lax.rsqrt(VOLUME * sm - mm * mm + FLOOR)
-                    cov = VOLUME * sc - mean[k, at, :] * mm
-                    coef = (VOLUME * b - mm - cov * slope[k, at, :]) * inv
+                    mm = mm * ROOT
+                    inv = lax.rsqrt(sm - mm * mm + FLOOR)
+                    cov = sc - mean[k, at, :] * mm
+                    coef = (b - mm * ROOT - cov * slope[k, at, :]) * inv
                     acc = [acc[c] + coef * grads[c, k, at, :] for c in range(3)]
                 for c in range(3):
                     frc[c, at, :] = acc[c]
@@ -281,18 +284,13 @@
                 parts.append(v)
     both = halves(parts)
     res = dot(both, smooth[0:256]) + dot(both[:, 0:128], smooth[256:384])
-    copies = []
     for c in range(3):
         for g in range(planes // 8):
             for r in range(8):
                 n = ((c * planes + g * 8) + r) * 8
                 ys[0, pl.ds(g * 8 * PITCH + r, 8, stride=PITCH), :] = res[n:n + 8]
         for o in range(planes):
-            result[c, o] = vel[0, c, o] + (8.0 * VOLUME / 24.0) * ys[0, pl.ds(o * PITCH, 8), :]
-        copies.append(pltpu.make_async_copy(result.at[c], out.at[c], sems.at[c]))
-        copies[c].start()
-    for copy in copies:
-        copy.wait()
+            out[c, o] = vel[0, c, o] + (8.0 * VOLUME / 24.0) * ys[0, pl.ds(o * PITCH, 8), :]
 
 
 VM = pl.BlockSpec(memory_space=pltpu.VMEM)
@@ -330,7 +328,7 @@
         functools.partial(mate_kernel, planes, count),
         out_shape=jax.ShapeDtypeStruct(vel.shape[1:], f32),
         in_specs=[VM] * (2 * count + 10),
-        out_specs=HBM,
+        out_specs=VM,
         scratch_shapes=[
             pltpu.VMEM((5, nx * 8, 128), f32),
             pltpu.VMEM((3, nx * 8 + 16, 128), f32),
@@ -338,8 +336,6 @@
             pltpu.VMEM((12, nd * PITCH + SPARE, 128), f32),
             pltpu.VMEM((3 * UNROLL, nf * PITCH + SPARE, 128), f32),
             pltpu.VMEM((3, nf * 8, 128), f32),
-            pltpu.VMEM(vel.shape[1:], f32),
-            pltpu.SemaphoreType.DMA((3,)),
         ],
         compiler_params=pltpu.CompilerParams(vmem_limit_bytes=16 * 2**20),
         name="mate",

time: 21.3 us -> 21.4 us (level)
  no operation moved by 1% of the time
where the time goes in v11:
time: 21.4 us; the launch traced here: 21.1 us
  Pallas kernels  11.3 us (53%)
  starting transfers between devices  9.13 us (43%)
  waiting for transfers between devices  0.53 us (2%)
    pallas_call x1, Pallas kernels, mate_part(): pl.pallas_call(functools.partial(mate_kernel, planes, count), out_shape=j...  6.16 us
    ppermute x6, starting transfers between devices, from_brains(): lax.ppermute(x, 'brain', [(n, n ^ k) for n in range(4)])  5.91 us
    pallas_call x1, Pallas kernels, own_part(): pl.pallas_call(functools.partial(own_kernel, planes), out_shape=(shape((1...  3.88 us
    ppermute x1, starting transfers between devices, shards(): from_odd = lax.ppermute(second, 'slab', both_ways(odd_pairs))  1.91 us
    ppermute x1, starting transfers between devices, shards(): from_even = lax.ppermute(first, 'slab', both_ways(even_pairs))  1.31 us
    pallas_call x1, Pallas kernels, shards(): pl.pallas_call(functools.partial(advect_kernel, planes), out_shape=(jax.S...  1.16 us
    ppermute x1, waiting for transfers between devices, shards(): from_odd = lax.ppermute(second, 'slab', both_ways(odd_pairs))  0.52 us
  transfers between devices with their start and end apart: 8, of which 1 were waited for; matrix products, arithmetic and copies ran while one was open for 0% of the time, Pallas kernels for 19%

profile of v11, /device:TPU:17, one launch (start us, length us, event | category | flops | bytes accessed | tf_op | source)
XLA Modules:
  0.0 21.1 jit_solution(15307786926523015279)
XLA Ops:
  0.0 1.2 %advect.1 = (f32[24,8,128]{2,1,0:T(8,128)S(1)}, bf16[22,8,128]{2,1,0:T(8,128)(2,1)S(1)}, bf16[13,8,128]{2,1,0:T(8,128)(2,1)S(1)}, bf16[13,8,128]{2,1,0:T(8,128)(...) custom-call(bf16[1,24,8,128]{3,2,1,0:T(8,128)(2,1)} %image_hbm.1, f32[1,3,24,8,128]{4,3,2,1,0:T(8,128)} %vel_hbm.1, ...), custom_call_target="tpu_custom_call" | custom-call | tf_op jit(solution)/shard_map/advect/pallas_call | solution.py:427
  1.2 0.7 %collective-permute-start.2 = (bf16[22,8,128]{2,1,0:T(8,128)(2,1)S(1)}, bf16[22,8,128]{2,1,0:T(8,128)(2,1)S(1)}, u32[]{:S(2)}, u32[]{:S(2)}) collective-permute-start(bf16[22,8,128]{2,1,0:T(8,128)(2,1)S(1)} %get-tuple-element.23), channel_id=1, source_target_pairs={{0,4},{4,0},{8,12},{12,8},{1,5},{5,1},{9,13},{13,9},{2,6},{6,2},{1... | collective-permute-start | bytes 135176 | tf_op jit(solution)/shard_map/ppermute | solution.py:418
  1.9 1.3 %collective-permute-start.3 = (bf16[13,8,128]{2,1,0:T(8,128)(2,1)S(1)}, bf16[13,8,128]{2,1,0:T(8,128)(2,1)S(1)}, u32[]{:S(2)}, u32[]{:S(2)}) collective-permute-start(bf16[13,8,128]{2,1,0:T(8,128)(2,1)S(1)} %get-tuple-element.25.sent1), channel_id=1, source_target_pairs={{0,1},{2,3},{1,0},{3,2},{4,5},{6,7},{5,4},{7,6},{8,9},{10,11},{9,8... | collective-permute-start | bytes 79880 | tf_op jit(solution)/shard_map/ppermute | solution.py:447
  3.2 1.9 %collective-permute-start.4 = (bf16[13,8,128]{2,1,0:T(8,128)(2,1)S(1)}, bf16[13,8,128]{2,1,0:T(8,128)(2,1)S(1)}, u32[]{:S(2)}, u32[]{:S(2)}) collective-permute-start(bf16[13,8,128]{2,1,0:T(8,128)(2,1)S(1)} %get-tuple-element.26.sent2), channel_id=1, source_target_pairs={{1,2},{2,1},{5,6},{6,5},{9,10},{10,9},{13,14},{14,13},{17,18},{18,... | collective-permute-start | bytes 79880 | tf_op jit(solution)/shard_map/ppermute | solution.py:446
  5.1 1.3 %collective-permute-start.1 = (bf16[22,8,128]{2,1,0:T(8,128)(2,1)S(1)}, bf16[22,8,128]{2,1,0:T(8,128)(2,1)S(1)}, u32[]{:S(2)}, u32[]{:S(2)}) collective-permute-start(bf16[22,8,128]{2,1,0:T(8,128)(2,1)S(1)} %get-tuple-element.23), channel_id=1, source_target_pairs={{0,8},{4,12},{8,0},{12,4},{1,9},{5,13},{9,1},{13,5},{2,10},{6,14},... | collective-permute-start | bytes 135176 | tf_op jit(solution)/shard_map/ppermute | solution.py:418
  6.4 0.8 %collective-permute-start = (bf16[22,8,128]{2,1,0:T(8,128)(2,1)S(1)}, bf16[22,8,128]{2,1,0:T(8,128)(2,1)S(1)}, u32[]{:S(2)}, u32[]{:S(2)}) collective-permute-start(bf16[22,8,128]{2,1,0:T(8,128)(2,1)S(1)} %get-tuple-element.23), channel_id=1, source_target_pairs={{0,12},{4,8},{8,4},{12,0},{1,13},{5,9},{9,5},{13,1},{2,14},{6,10},... | collective-permute-start | bytes 135176 | tf_op jit(solution)/shard_map/ppermute | solution.py:418
  7.2 0.1 tables.1
  7.3 0.0 collective-permute-done.3.got1
  7.3 0.5 %collective-permute-done.4.got2 = bf16[13,8,128]{2,1,0:T(8,128)(2,1)S(1)} collective-permute-done((bf16[13,8,128]{2,1,0:T(8,128)(2,1)S(1)}, bf16[13,8,128]{2,1,0:T(8,128)(2,1)S(1)}, u32[]{:S(2)}, u32[]{:S(2)}) %collective-permute-start.4) | collective-permute-done | bytes 26656 | tf_op jit(solution)/shard_map/ppermute | solution.py:446
  7.8 2.7 %collective-permute-start.7 = (bf16[20,8,128]{2,1,0:T(8,128)(2,1)S(1)}, bf16[20,8,128]{2,1,0:T(8,128)(2,1)S(1)}, u32[]{:S(2)}, u32[]{:S(2)}) collective-permute-start(bf16[20,8,128]{2,1,0:T(8,128)(2,1)S(1)} %get-tuple-element.27), channel_id=1, source_target_pairs={{0,12},{4,8},{8,4},{12,0},{1,13},{5,9},{9,5},{13,1},{2,14},{6,10},... | collective-permute-start | bytes 122888 | tf_op jit(solution)/shard_map/ppermute | solution.py:418
  10.5 0.3 %collective-permute-start.6 = (bf16[20,8,128]{2,1,0:T(8,128)(2,1)S(1)}, bf16[20,8,128]{2,1,0:T(8,128)(2,1)S(1)}, u32[]{:S(2)}, u32[]{:S(2)}) collective-permute-start(bf16[20,8,128]{2,1,0:T(8,128)(2,1)S(1)} %get-tuple-element.27), channel_id=1, source_target_pairs={{0,8},{4,12},{8,0},{12,4},{1,9},{5,13},{9,1},{13,5},{2,10},{6,14},... | collective-permute-start | bytes 122888 | tf_op jit(solution)/shard_map/ppermute | solution.py:418
  10.7 0.0 collective-permute-done.2
  10.8 0.2 %collective-permute-start.5 = (bf16[20,8,128]{2,1,0:T(8,128)(2,1)S(1)}, bf16[20,8,128]{2,1,0:T(8,128)(2,1)S(1)}, u32[]{:S(2)}, u32[]{:S(2)}) collective-permute-start(bf16[20,8,128]{2,1,0:T(8,128)(2,1)S(1)} %get-tuple-element.27), channel_id=1, source_target_pairs={{0,4},{4,0},{8,12},{12,8},{1,5},{5,1},{9,13},{13,9},{2,6},{6,2},{1... | collective-permute-start | bytes 122888 | tf_op jit(solution)/shard_map/ppermute | solution.py:418
  11.0 3.9 %own.1 = (f32[12,376,128]{2,1,0:T(8,128)S(1)}, f32[12,256,128]{2,1,0:T(8,128)S(1)}, f32[12,256,128]{2,1,0:T(8,128)S(1)}, f32[3,12,256,128]{3,2,1,0:T(8,128)S(1)}) custom-call(bf16[336,128]{1,0:T(8,128)(2,1)S(1)} %bitcast.15, bf16[256,128]{1,0:T(8,128)(2,1)S(1)} %get-tuple-element.29.box3.refs_7_, bf16[256,128]{1,0:T(8,128)(2,1)S(1)} %get-tuple-element.30.box9.refs_8_, ...), custom_call_target="tpu_custom_call" | custom-call | flops 600000000 | bytes 16777216 | tf_op jit(solution)/shard_map/own/pallas_call | solution.py:303
  14.9 0.0 collective-permute-done.1
  14.9 0.0 collective-permute-done
  14.9 0.0 collective-permute-done.7
  14.9 0.0 collective-permute-done.6
  14.9 0.0 collective-permute-done.5
  14.9 6.2 %mate.1 = f32[3,24,8,128]{3,2,1,0:T(8,128)} custom-call(bf16[176,128]{1,0:T(8,128)(2,1)S(1)} %bitcast.11, bf16[176,128]{1,0:T(8,128)(2,1)S(1)} %bitcast.10, bf16[176,128]{1,0:T(8,128)(2,1)S(1)} %bitcast.9, bf16[160,128]{1,0:T(8,128)(2,1)S(1)} %bitcast.14, bf16[160,128]{1,0:T(8,128)(2,1)S(1)} %bitcast.13, bf16[160,128]{1,0:T(8,128)(2,1)S(1)} %bitcast.12, ...), custom_call_target="tpu_custom_call" | custom-call | tf_op jit(solution)/shard_map/mate/pallas_call | solution.py:327
  (1 shorter events, 0.0 us)
Async XLA Ops:
  1.2 9.6 %collective-permute-start.2 = (bf16[22,8,128]{2,1,0:T(8,128)(2,1)S(1)}, bf16[22,8,128]{2,1,0:T(8,128)(2,1)S(1)}, u32[]{:S(2)}, u32[]{:S(2)}) collective-permute-start(bf16[22,8,128]{2,1,0:T(8,128)(2,1)S(1)} %get-tuple-element.23), channel_id=1, source_target_pairs={{0,4},{4,0},{8,12},{12,8},{1,5},{5,1},{9,13},{13,9},{2,6},{6,2},{1... | collective-permute-start | bytes 135176 | tf_op jit(solution)/shard_map/ppermute | solution.py:418
  1.9 5.4 %collective-permute-start.3 = (bf16[13,8,128]{2,1,0:T(8,128)(2,1)S(1)}, bf16[13,8,128]{2,1,0:T(8,128)(2,1)S(1)}, u32[]{:S(2)}, u32[]{:S(2)}) collective-permute-start(bf16[13,8,128]{2,1,0:T(8,128)(2,1)S(1)} %get-tuple-element.25.sent1), channel_id=1, source_target_pairs={{0,1},{2,3},{1,0},{3,2},{4,5},{6,7},{5,4},{7,6},{8,9},{10,11},{9,8... | collective-permute-start | bytes 79880 | tf_op jit(solution)/shard_map/ppermute | solution.py:447
  3.2 4.6 %collective-permute-start.4 = (bf16[13,8,128]{2,1,0:T(8,128)(2,1)S(1)}, bf16[13,8,128]{2,1,0:T(8,128)(2,1)S(1)}, u32[]{:S(2)}, u32[]{:S(2)}) collective-permute-start(bf16[13,8,128]{2,1,0:T(8,128)(2,1)S(1)} %get-tuple-element.26.sent2), channel_id=1, source_target_pairs={{1,2},{2,1},{5,6},{6,5},{9,10},{10,9},{13,14},{14,13},{17,18},{18,... | collective-permute-start | bytes 79880 | tf_op jit(solution)/shard_map/ppermute | solution.py:446
  5.1 9.7 %collective-permute-start.1 = (bf16[22,8,128]{2,1,0:T(8,128)(2,1)S(1)}, bf16[22,8,128]{2,1,0:T(8,128)(2,1)S(1)}, u32[]{:S(2)}, u32[]{:S(2)}) collective-permute-start(bf16[22,8,128]{2,1,0:T(8,128)(2,1)S(1)} %get-tuple-element.23), channel_id=1, source_target_pairs={{0,8},{4,12},{8,0},{12,4},{1,9},{5,13},{9,1},{13,5},{2,10},{6,14},... | collective-permute-start | bytes 135176 | tf_op jit(solution)/shard_map/ppermute | solution.py:418
  6.4 8.5 %collective-permute-start = (bf16[22,8,128]{2,1,0:T(8,128)(2,1)S(1)}, bf16[22,8,128]{2,1,0:T(8,128)(2,1)S(1)}, u32[]{:S(2)}, u32[]{:S(2)}) collective-permute-start(bf16[22,8,128]{2,1,0:T(8,128)(2,1)S(1)} %get-tuple-element.23), channel_id=1, source_target_pairs={{0,12},{4,8},{8,4},{12,0},{1,13},{5,9},{9,5},{13,1},{2,14},{6,10},... | collective-permute-start | bytes 135176 | tf_op jit(solution)/shard_map/ppermute | solution.py:418
  7.8 7.0 %collective-permute-start.7 = (bf16[20,8,128]{2,1,0:T(8,128)(2,1)S(1)}, bf16[20,8,128]{2,1,0:T(8,128)(2,1)S(1)}, u32[]{:S(2)}, u32[]{:S(2)}) collective-permute-start(bf16[20,8,128]{2,1,0:T(8,128)(2,1)S(1)} %get-tuple-element.27), channel_id=1, source_target_pairs={{0,12},{4,8},{8,4},{12,0},{1,13},{5,9},{9,5},{13,1},{2,14},{6,10},... | collective-permute-start | bytes 122888 | tf_op jit(solution)/shard_map/ppermute | solution.py:418
  10.5 4.4 %collective-permute-start.6 = (bf16[20,8,128]{2,1,0:T(8,128)(2,1)S(1)}, bf16[20,8,128]{2,1,0:T(8,128)(2,1)S(1)}, u32[]{:S(2)}, u32[]{:S(2)}) collective-permute-start(bf16[20,8,128]{2,1,0:T(8,128)(2,1)S(1)} %get-tuple-element.27), channel_id=1, source_target_pairs={{0,8},{4,12},{8,0},{12,4},{1,9},{5,13},{9,1},{13,5},{2,10},{6,14},... | collective-permute-start | bytes 122888 | tf_op jit(solution)/shard_map/ppermute | solution.py:418
  10.8 4.2 %collective-permute-start.5 = (bf16[20,8,128]{2,1,0:T(8,128)(2,1)S(1)}, bf16[20,8,128]{2,1,0:T(8,128)(2,1)S(1)}, u32[]{:S(2)}, u32[]{:S(2)}) collective-permute-start(bf16[20,8,128]{2,1,0:T(8,128)(2,1)S(1)} %get-tuple-element.27), channel_id=1, source_target_pairs={{0,4},{4,0},{8,12},{12,8},{1,5},{5,1},{9,13},{13,9},{2,6},{6,2},{1... | collective-permute-start | bytes 122888 | tf_op jit(solution)/shard_map/ppermute | solution.py:418

commit v12 on v10

--- a/solution.py
+++ b/solution.py
@@ -200,7 +200,7 @@
 
 def mate_kernel(planes, count, *refs):
     inner, outer = refs[:count][::-1], refs[count:2 * count]
-    meta, box3, box9, smooth, take, adesc, mean, slope, grads, vel, out, xs, raw, tb, desc, ys, frc, result, sems = refs[2 * count:]
+    meta, box3, box9, smooth, take, adesc, mean, slope, grads, vel, out, xs, raw, tb, desc, ys, frc = refs[2 * count:]
     nx, nd, nf = planes + 18, planes + 16, planes + 8
     low, high = faces()
     which = meta[0:1, :]
@@ -281,18 +281,13 @@
                 parts.append(v)
     both = halves(parts)
     res = dot(both, smooth[0:256]) + dot(both[:, 0:128], smooth[256:384])
-    copies = []
     for c in range(3):
         for g in range(planes // 8):
             for r in range(8):
                 n = ((c * planes + g * 8) + r) * 8
                 ys[0, pl.ds(g * 8 * PITCH + r, 8, stride=PITCH), :] = res[n:n + 8]
         for o in range(planes):
-            result[c, o] = vel[0, c, o] + (8.0 * VOLUME / 24.0) * ys[0, pl.ds(o * PITCH, 8), :]
-        copies.append(pltpu.make_async_copy(result.at[c], out.at[c], sems.at[c]))
-        copies[c].start()
-    for copy in copies:
-        copy.wait()
+            out[c, o] = vel[0, c, o] + (8.0 * VOLUME / 24.0) * ys[0, pl.ds(o * PITCH, 8), :]
 
 
 VM = pl.BlockSpec(memory_space=pltpu.VMEM)
@@ -330,7 +325,7 @@
         functools.partial(mate_kernel, planes, count),
         out_shape=jax.ShapeDtypeStruct(vel.shape[1:], f32),
         in_specs=[VM] * (2 * count + 10),
-        out_specs=HBM,
+        out_specs=VM,
         scratch_shapes=[
             pltpu.VMEM((5, nx * 8, 128), f32),
             pltpu.VMEM((3, nx * 8 + 16, 128), f32),
@@ -338,8 +333,6 @@
             pltpu.VMEM((12, nd * PITCH + SPARE, 128), f32),
             pltpu.VMEM((3 * UNROLL, nf * PITCH + SPARE, 128), f32),
             pltpu.VMEM((3, nf * 8, 128), f32),
-            pltpu.VMEM(vel.shape[1:], f32),
-            pltpu.SemaphoreType.DMA((3,)),
         ],
         compiler_params=pltpu.CompilerParams(vmem_limit_bytes=16 * 2**20),
         name="mate",

time: 21.3 us -> 21.3 us (level)
  no operation moved by 1% of the time
where the time goes in v12:
time: 21.3 us; the launch traced here: 21 us
  Pallas kernels  11.3 us (53%)
  starting transfers between devices  9.13 us (43%)
  waiting for transfers between devices  0.53 us (2%)
    pallas_call x1, Pallas kernels, mate_part(): pl.pallas_call(functools.partial(mate_kernel, planes, count), out_shape=j...  6.18 us
    ppermute x6, starting transfers between devices, from_brains(): lax.ppermute(x, 'brain', [(n, n ^ k) for n in range(4)])  5.91 us
    pallas_call x1, Pallas kernels, own_part(): pl.pallas_call(functools.partial(own_kernel, planes), out_shape=(shape((1...  3.84 us
    ppermute x1, starting transfers between devices, shards(): from_odd = lax.ppermute(second, 'slab', both_ways(odd_pairs))  1.91 us
    ppermute x1, starting transfers between devices, shards(): from_even = lax.ppermute(first, 'slab', both_ways(even_pairs))  1.31 us
    pallas_call x1, Pallas kernels, shards(): pl.pallas_call(functools.partial(advect_kernel, planes), out_shape=(jax.S...  1.16 us
    ppermute x1, waiting for transfers between devices, shards(): from_odd = lax.ppermute(second, 'slab', both_ways(odd_pairs))  0.52 us
  transfers between devices with their start and end apart: 8, of which 1 were waited for; matrix products, arithmetic and copies ran while one was open for 0% of the time, Pallas kernels for 19%

profile of v12, /device:TPU:17, one launch (start us, length us, event | category | flops | bytes accessed | tf_op | source)
XLA Modules:
  0.0 21.0 jit_solution(14297520411866067756)
XLA Ops:
  0.0 1.2 %advect.1 = (f32[24,8,128]{2,1,0:T(8,128)S(1)}, bf16[22,8,128]{2,1,0:T(8,128)(2,1)S(1)}, bf16[13,8,128]{2,1,0:T(8,128)(2,1)S(1)}, bf16[13,8,128]{2,1,0:T(8,128)(...) custom-call(bf16[1,24,8,128]{3,2,1,0:T(8,128)(2,1)} %image_hbm.1, f32[1,3,24,8,128]{4,3,2,1,0:T(8,128)} %vel_hbm.1, ...), custom_call_target="tpu_custom_call" | custom-call | tf_op jit(solution)/shard_map/advect/pallas_call | solution.py:424
  1.2 0.7 %collective-permute-start.2 = (bf16[22,8,128]{2,1,0:T(8,128)(2,1)S(1)}, bf16[22,8,128]{2,1,0:T(8,128)(2,1)S(1)}, u32[]{:S(2)}, u32[]{:S(2)}) collective-permute-start(bf16[22,8,128]{2,1,0:T(8,128)(2,1)S(1)} %get-tuple-element.23), channel_id=1, source_target_pairs={{0,4},{4,0},{8,12},{12,8},{1,5},{5,1},{9,13},{13,9},{2,6},{6,2},{1... | collective-permute-start | bytes 135176 | tf_op jit(solution)/shard_map/ppermute | solution.py:415
  1.9 1.3 %collective-permute-start.3 = (bf16[13,8,128]{2,1,0:T(8,128)(2,1)S(1)}, bf16[13,8,128]{2,1,0:T(8,128)(2,1)S(1)}, u32[]{:S(2)}, u32[]{:S(2)}) collective-permute-start(bf16[13,8,128]{2,1,0:T(8,128)(2,1)S(1)} %get-tuple-element.25.sent1), channel_id=1, source_target_pairs={{0,1},{2,3},{1,0},{3,2},{4,5},{6,7},{5,4},{7,6},{8,9},{10,11},{9,8... | collective-permute-start | bytes 79880 | tf_op jit(solution)/shard_map/ppermute | solution.py:444
  3.2 1.9 %collective-permute-start.4 = (bf16[13,8,128]{2,1,0:T(8,128)(2,1)S(1)}, bf16[13,8,128]{2,1,0:T(8,128)(2,1)S(1)}, u32[]{:S(2)}, u32[]{:S(2)}) collective-permute-start(bf16[13,8,128]{2,1,0:T(8,128)(2,1)S(1)} %get-tuple-element.26.sent2), channel_id=1, source_target_pairs={{1,2},{2,1},{5,6},{6,5},{9,10},{10,9},{13,14},{14,13},{17,18},{18,... | collective-permute-start | bytes 79880 | tf_op jit(solution)/shard_map/ppermute | solution.py:443
  5.1 1.3 %collective-permute-start.1 = (bf16[22,8,128]{2,1,0:T(8,128)(2,1)S(1)}, bf16[22,8,128]{2,1,0:T(8,128)(2,1)S(1)}, u32[]{:S(2)}, u32[]{:S(2)}) collective-permute-start(bf16[22,8,128]{2,1,0:T(8,128)(2,1)S(1)} %get-tuple-element.23), channel_id=1, source_target_pairs={{0,8},{4,12},{8,0},{12,4},{1,9},{5,13},{9,1},{13,5},{2,10},{6,14},... | collective-permute-start | bytes 135176 | tf_op jit(solution)/shard_map/ppermute | solution.py:415
  6.4 0.8 %collective-permute-start = (bf16[22,8,128]{2,1,0:T(8,128)(2,1)S(1)}, bf16[22,8,128]{2,1,0:T(8,128)(2,1)S(1)}, u32[]{:S(2)}, u32[]{:S(2)}) collective-permute-start(bf16[22,8,128]{2,1,0:T(8,128)(2,1)S(1)} %get-tuple-element.23), channel_id=1, source_target_pairs={{0,12},{4,8},{8,4},{12,0},{1,13},{5,9},{9,5},{13,1},{2,14},{6,10},... | collective-permute-start | bytes 135176 | tf_op jit(solution)/shard_map/ppermute | solution.py:415
  7.2 0.1 tables.1
  7.3 0.0 collective-permute-done.3.got1
  7.3 0.5 %collective-permute-done.4.got2 = bf16[13,8,128]{2,1,0:T(8,128)(2,1)S(1)} collective-permute-done((bf16[13,8,128]{2,1,0:T(8,128)(2,1)S(1)}, bf16[13,8,128]{2,1,0:T(8,128)(2,1)S(1)}, u32[]{:S(2)}, u32[]{:S(2)}) %collective-permute-start.4) | collective-permute-done | bytes 26656 | tf_op jit(solution)/shard_map/ppermute | solution.py:443
  7.8 2.7 %collective-permute-start.7 = (bf16[20,8,128]{2,1,0:T(8,128)(2,1)S(1)}, bf16[20,8,128]{2,1,0:T(8,128)(2,1)S(1)}, u32[]{:S(2)}, u32[]{:S(2)}) collective-permute-start(bf16[20,8,128]{2,1,0:T(8,128)(2,1)S(1)} %get-tuple-element.27), channel_id=1, source_target_pairs={{0,12},{4,8},{8,4},{12,0},{1,13},{5,9},{9,5},{13,1},{2,14},{6,10},... | collective-permute-start | bytes 122888 | tf_op jit(solution)/shard_map/ppermute | solution.py:415
  10.5 0.3 %collective-permute-start.6 = (bf16[20,8,128]{2,1,0:T(8,128)(2,1)S(1)}, bf16[20,8,128]{2,1,0:T(8,128)(2,1)S(1)}, u32[]{:S(2)}, u32[]{:S(2)}) collective-permute-start(bf16[20,8,128]{2,1,0:T(8,128)(2,1)S(1)} %get-tuple-element.27), channel_id=1, source_target_pairs={{0,8},{4,12},{8,0},{12,4},{1,9},{5,13},{9,1},{13,5},{2,10},{6,14},... | collective-permute-start | bytes 122888 | tf_op jit(solution)/shard_map/ppermute | solution.py:415
  10.7 0.0 collective-permute-done.2
  10.8 0.2 %collective-permute-start.5 = (bf16[20,8,128]{2,1,0:T(8,128)(2,1)S(1)}, bf16[20,8,128]{2,1,0:T(8,128)(2,1)S(1)}, u32[]{:S(2)}, u32[]{:S(2)}) collective-permute-start(bf16[20,8,128]{2,1,0:T(8,128)(2,1)S(1)} %get-tuple-element.27), channel_id=1, source_target_pairs={{0,4},{4,0},{8,12},{12,8},{1,5},{5,1},{9,13},{13,9},{2,6},{6,2},{1... | collective-permute-start | bytes 122888 | tf_op jit(solution)/shard_map/ppermute | solution.py:415
  11.0 3.8 %own.1 = (f32[12,376,128]{2,1,0:T(8,128)S(1)}, f32[12,256,128]{2,1,0:T(8,128)S(1)}, f32[12,256,128]{2,1,0:T(8,128)S(1)}, f32[3,12,256,128]{3,2,1,0:T(8,128)S(1)}) custom-call(bf16[336,128]{1,0:T(8,128)(2,1)S(1)} %bitcast.15, bf16[256,128]{1,0:T(8,128)(2,1)S(1)} %get-tuple-element.29.box3.refs_7_, bf16[256,128]{1,0:T(8,128)(2,1)S(1)} %get-tuple-element.30.box9.refs_8_, ...), custom_call_target="tpu_custom_call" | custom-call | flops 600000000 | bytes 16777216 | tf_op jit(solution)/shard_map/own/pallas_call | solution.py:300
  14.8 0.0 collective-permute-done.1
  14.8 0.0 collective-permute-done
  14.8 0.0 collective-permute-done.7
  14.8 0.0 collective-permute-done.6
  14.9 0.0 collective-permute-done.5
  14.9 6.2 %mate.1 = f32[3,24,8,128]{3,2,1,0:T(8,128)} custom-call(bf16[176,128]{1,0:T(8,128)(2,1)S(1)} %bitcast.11, bf16[176,128]{1,0:T(8,128)(2,1)S(1)} %bitcast.10, bf16[176,128]{1,0:T(8,128)(2,1)S(1)} %bitcast.9, bf16[160,128]{1,0:T(8,128)(2,1)S(1)} %bitcast.14, bf16[160,128]{1,0:T(8,128)(2,1)S(1)} %bitcast.13, bf16[160,128]{1,0:T(8,128)(2,1)S(1)} %bitcast.12, ...), custom_call_target="tpu_custom_call" | custom-call | tf_op jit(solution)/shard_map/mate/pallas_call | solution.py:324
  (1 shorter events, 0.0 us)
Async XLA Ops:
  1.2 9.6 %collective-permute-start.2 = (bf16[22,8,128]{2,1,0:T(8,128)(2,1)S(1)}, bf16[22,8,128]{2,1,0:T(8,128)(2,1)S(1)}, u32[]{:S(2)}, u32[]{:S(2)}) collective-permute-start(bf16[22,8,128]{2,1,0:T(8,128)(2,1)S(1)} %get-tuple-element.23), channel_id=1, source_target_pairs={{0,4},{4,0},{8,12},{12,8},{1,5},{5,1},{9,13},{13,9},{2,6},{6,2},{1... | collective-permute-start | bytes 135176 | tf_op jit(solution)/shard_map/ppermute | solution.py:415
  1.9 5.4 %collective-permute-start.3 = (bf16[13,8,128]{2,1,0:T(8,128)(2,1)S(1)}, bf16[13,8,128]{2,1,0:T(8,128)(2,1)S(1)}, u32[]{:S(2)}, u32[]{:S(2)}) collective-permute-start(bf16[13,8,128]{2,1,0:T(8,128)(2,1)S(1)} %get-tuple-element.25.sent1), channel_id=1, source_target_pairs={{0,1},{2,3},{1,0},{3,2},{4,5},{6,7},{5,4},{7,6},{8,9},{10,11},{9,8... | collective-permute-start | bytes 79880 | tf_op jit(solution)/shard_map/ppermute | solution.py:444
  3.2 4.6 %collective-permute-start.4 = (bf16[13,8,128]{2,1,0:T(8,128)(2,1)S(1)}, bf16[13,8,128]{2,1,0:T(8,128)(2,1)S(1)}, u32[]{:S(2)}, u32[]{:S(2)}) collective-permute-start(bf16[13,8,128]{2,1,0:T(8,128)(2,1)S(1)} %get-tuple-element.26.sent2), channel_id=1, source_target_pairs={{1,2},{2,1},{5,6},{6,5},{9,10},{10,9},{13,14},{14,13},{17,18},{18,... | collective-permute-start | bytes 79880 | tf_op jit(solution)/shard_map/ppermute | solution.py:443
  5.1 9.7 %collective-permute-start.1 = (bf16[22,8,128]{2,1,0:T(8,128)(2,1)S(1)}, bf16[22,8,128]{2,1,0:T(8,128)(2,1)S(1)}, u32[]{:S(2)}, u32[]{:S(2)}) collective-permute-start(bf16[22,8,128]{2,1,0:T(8,128)(2,1)S(1)} %get-tuple-element.23), channel_id=1, source_target_pairs={{0,8},{4,12},{8,0},{12,4},{1,9},{5,13},{9,1},{13,5},{2,10},{6,14},... | collective-permute-start | bytes 135176 | tf_op jit(solution)/shard_map/ppermute | solution.py:415
  6.4 8.4 %collective-permute-start = (bf16[22,8,128]{2,1,0:T(8,128)(2,1)S(1)}, bf16[22,8,128]{2,1,0:T(8,128)(2,1)S(1)}, u32[]{:S(2)}, u32[]{:S(2)}) collective-permute-start(bf16[22,8,128]{2,1,0:T(8,128)(2,1)S(1)} %get-tuple-element.23), channel_id=1, source_target_pairs={{0,12},{4,8},{8,4},{12,0},{1,13},{5,9},{9,5},{13,1},{2,14},{6,10},... | collective-permute-start | bytes 135176 | tf_op jit(solution)/shard_map/ppermute | solution.py:415
  7.8 7.0 %collective-permute-start.7 = (bf16[20,8,128]{2,1,0:T(8,128)(2,1)S(1)}, bf16[20,8,128]{2,1,0:T(8,128)(2,1)S(1)}, u32[]{:S(2)}, u32[]{:S(2)}) collective-permute-start(bf16[20,8,128]{2,1,0:T(8,128)(2,1)S(1)} %get-tuple-element.27), channel_id=1, source_target_pairs={{0,12},{4,8},{8,4},{12,0},{1,13},{5,9},{9,5},{13,1},{2,14},{6,10},... | collective-permute-start | bytes 122888 | tf_op jit(solution)/shard_map/ppermute | solution.py:415
  10.5 4.4 %collective-permute-start.6 = (bf16[20,8,128]{2,1,0:T(8,128)(2,1)S(1)}, bf16[20,8,128]{2,1,0:T(8,128)(2,1)S(1)}, u32[]{:S(2)}, u32[]{:S(2)}) collective-permute-start(bf16[20,8,128]{2,1,0:T(8,128)(2,1)S(1)} %get-tuple-element.27), channel_id=1, source_target_pairs={{0,8},{4,12},{8,0},{12,4},{1,9},{5,13},{9,1},{13,5},{2,10},{6,14},... | collective-permute-start | bytes 122888 | tf_op jit(solution)/shard_map/ppermute | solution.py:415
  10.8 4.1 %collective-permute-start.5 = (bf16[20,8,128]{2,1,0:T(8,128)(2,1)S(1)}, bf16[20,8,128]{2,1,0:T(8,128)(2,1)S(1)}, u32[]{:S(2)}, u32[]{:S(2)}) collective-permute-start(bf16[20,8,128]{2,1,0:T(8,128)(2,1)S(1)} %get-tuple-element.27), channel_id=1, source_target_pairs={{0,4},{4,0},{8,12},{12,8},{1,5},{5,1},{9,13},{13,9},{2,6},{6,2},{1... | collective-permute-start | bytes 122888 | tf_op jit(solution)/shard_map/ppermute | solution.py:415
